TPU v7x, 128 devices: a whole 4x4x4 slice. The times are simulated.
128 devices in a mesh: horiz: 32 (over z, x, core), depth: 4 (over y).
Axes of the slice: x: 4, y: 4, z: 4, core: 2. Of those that a mesh axis runs over, the one named last changes fastest.
Arguments:
- adjoint_seed: bfloat16 [16, 48, 32768], P(None, 'depth', 'horiz'), may hold values from -6 to 6
- transport: bfloat16 [48, 256, 5, 128, 128], P('depth', 'horiz'), may hold values from -0.25 to 0.25
- neighbours: int32 [256, 5], P('horiz'), may hold values from 0 to 255, as said below
- inv_mix: float32 [48, 48, 32768], P(None, None, ('horiz', 'depth')), may hold values from -0.875 to 0.875
- rates: float32 [48, 32768], P('depth', 'horiz'), may hold values from 0.2 to 2
- coupling: float32 [16, 16], replicated, may hold values from -1.5 to 1.5
- sensitivity: bfloat16 [16, 48, 32768], P(None, 'depth', 'horiz')
- depth_count: int32 [32768], P('horiz'), may hold values from 0 to 48, as said below
Outputs:
- first: bfloat16 [16, 48, 32768], P(None, 'depth', 'horiz')
- second: bfloat16 [16, 48, 32768], P(None, 'depth', 'horiz')
- gradient: float32 [16], replicated
Inputs may be any that keep to these rules, and one draw needn't show every extreme that they name: neighbours[b, 0] = b; every entry lies within 8 blocks of its row's block b, counted cyclically over 256 blocks. `depth_count`: 0 marks a land column.
All inputs are finite; a program needn't handle non-finite values.
Results may differ from a plain program's by a relative error of at most 0.011.
Values may be sent and summed in bfloat16 or wider, within the bound.
No kernel may reach another device: no remote copies, remote signals or barrier semaphores. Data moves between devices by JAX's collectives and lax.ppermute only.
A program may use at most 128 MiB of HBM per device.

v0:
```python
import math

import jax
import jax.numpy as jnp
from jax import lax
from jax.sharding import PartitionSpec as P


def padded(cells, sides, width):
    for axis, dim in sides:
        count = lax.axis_size(axis)
        head = lax.slice_in_dim(cells, 0, width, axis=dim)
        tail = lax.slice_in_dim(cells, cells.shape[dim] - width, cells.shape[dim], axis=dim)
        cells = jnp.concatenate(
            [
                lax.ppermute(tail, axis, [(i, (i + 1) % count) for i in range(count)]),
                cells,
                lax.ppermute(head, axis, [((i + 1) % count, i) for i in range(count)]),
            ],
            axis=dim,
        )
    return cells


def per_device(
    adjoint_seed, transport, neighbours, inv_mix, rates, coupling, sensitivity, depth_count
):
    tracers, lev_dev, cols = adjoint_seed.shape
    blocks, slots = neighbours.shape
    width = transport.shape[3]
    total_blocks = blocks * lax.axis_size("horiz")
    levels = lev_dev * lax.axis_size("depth")
    row_ids = lax.axis_index("horiz") * blocks + jnp.arange(blocks, dtype=jnp.int32)
    offset = (neighbours - row_ids[:, None] + blocks) % total_blocks - blocks
    source_rows = (jnp.arange(blocks, dtype=jnp.int32)[:, None] + blocks + offset).reshape(-1)
    level_ids = (
        lax.broadcasted_iota(jnp.int32, (lev_dev, cols), 0) + lax.axis_index("depth") * lev_dev
    )
    wet = (level_ids < depth_count[None, :]).astype(jnp.float32)
    sens = sensitivity.astype(jnp.float32)
    state = adjoint_seed
    results = []
    partials = []
    for step in range(2):
        full = lax.all_to_all(state, "depth", split_axis=2, concat_axis=1, tiled=True)
        mixed_cols = jnp.einsum(
            "pqc,tpc->tqc", inv_mix, full.astype(jnp.float32), precision=lax.Precision.HIGHEST
        ).astype(jnp.bfloat16)
        mixed = lax.all_to_all(mixed_cols, "depth", split_axis=1, concat_axis=2, tiled=True)
        mixed_f = mixed.astype(jnp.float32)
        grouped = mixed.reshape(tracers, lev_dev, blocks, width)
        nearby = padded(grouped, (("horiz", 2),), blocks)
        picked = jnp.take(nearby, source_rows, axis=2).reshape(
            tracers, lev_dev, blocks, slots, width
        )
        moved = jnp.einsum(
            "lrkij,tlrkj->tlri", transport, picked, preferred_element_type=jnp.float32
        )
        moved = moved.reshape(tracers, lev_dev, cols)
        source_term = rates[None, :, :] * jnp.einsum(
            "ut,ulc->tlc", coupling, mixed_f, precision=lax.Precision.HIGHEST
        )
        new_state = (wet[None] * (moved + source_term - state.astype(jnp.float32))).astype(
            jnp.bfloat16
        )
        local_terms = jnp.sum(wet[None] * mixed_f * sens, axis=(1, 2))
        partials.append(lax.psum(local_terms, ("horiz", "depth")))
        results.append(new_state)
        state = new_state
    grad_total = partials[0] + partials[1]
    gradient = grad_total / math.sqrt(levels * total_blocks * width)
    return (results[0], results[1], gradient)


def solution(mesh):
    return jax.shard_map(
        per_device,
        mesh=mesh,
        in_specs=(
            P(None, "depth", "horiz"),
            P("depth", "horiz", None, None, None),
            P("horiz", None),
            P(None, None, ("horiz", "depth")),
            P("depth", "horiz"),
            P(),
            P(None, "depth", "horiz"),
            P("horiz"),
        ),
        out_specs=(P(None, "depth", "horiz"), P(None, "depth", "horiz"), P()),
        check_vma=False,
    )
```

profile of v0, /device:TPU:1, one launch (start us, length us, event | category | flops | bytes accessed | tf_op | source)
XLA Modules:
  0.0 209.3 jit_solution(15735979041424803006)
XLA Ops:
  0.6 5.7 %copy.89 = bf16[16,12,1024]{0,1,2:T(8,128)(2,1)} copy(bf16[16,12,1024]{2,0,1:T(8,128)(2,1)} %param.10) | data formatting | bytes 786432 | tf_op args[0]
  6.3 5.9 %reshape.103 = bf16[4,2,24576]{2,1,0:T(2,128)(2,1)} reshape(bf16[1024,12,16]{2,1,0:T(8,128)(2,1)} %bitcast.82) | data formatting | bytes 786432
  12.2 5.0 %all-to-all-start = ((bf16[4,2,24576]{2,1,0:T(2,128)(2,1)}), bf16[4,2,24576]{2,1,0:T(2,128)(2,1)S(1)}, u32[]{:S(2)}, u32[]{:S(2)}) async-start(bf16[4,2,24576]{2,1,0:T(2,128)(2,1)} %reshape.103), calls=%async_computation | async-start | bytes 786432 | tf_op jit(solution)/shard_map/all_to_all | solution.py:45
  17.4 5.2 %copy.93 = f32[48,48,256]{1,0,2:T(8,128)} copy(f32[48,48,256]{2,1,0:T(8,128)S(1)} %copy-done.5) | data formatting | bytes 4718592 | tf_op args[3]
  22.6 1.5 all-to-all-done
  24.1 4.9 %reshape.104 = bf16[1024,12,16]{2,1,0:T(8,128)(2,1)} reshape(bf16[4,2,24576]{2,1,0:T(2,128)(2,1)S(1)} %all-to-all-done) | data formatting | bytes 786432
  29.0 4.9 %copy.121 = bf16[16,12,4,256]{3,2,0,1:T(4,128)(2,1)S(1)} copy(bf16[16,12,4,256]{0,1,3,2:T(8,128)(2,1)} %bitcast.80) | data formatting | bytes 786432 | tf_op jit(solution)/shard_map/all_to_all | solution.py:45
  34.0 1.2 copy.92
  35.2 5.1 %fusion.4 = bf16[16,48,256]{1,0,2:T(8,128)(2,1)S(1)} fusion(bf16[16,48,256]{1,0,2:T(8,128)(2,1)S(1)} %copy.92, f32[48,48,256]{1,0,2:T(8,128)} %copy.93), kind=kOutput, calls=%fused_computation.10 | convolution fusion | flops 113442816 | bytes 3145728 | tf_op jit(solution)/shard_map/pqc,tpc->tqc/dot_general | solution.py:46
  40.3 2.0 copy.94
  42.3 3.5 %all-to-all-start.1 = ((bf16[16,48,256]{2,0,1:T(8,128)(2,1)}), bf16[16,48,256]{2,0,1:T(8,128)(2,1)S(1)}, u32[]{:S(2)}, u32[]{:S(2)}) async-start(bf16[16,48,256]{2,0,1:T(8,128)(2,1)} %copy.94), calls=%async_computation.1 | async-start | bytes 786432 | tf_op jit(solution)/shard_map/all_to_all | solution.py:49
  45.8 6.2 %all-to-all-done.1 = bf16[16,48,256]{2,0,1:T(8,128)(2,1)S(1)} async-done(((bf16[16,48,256]{2,0,1:T(8,128)(2,1)}), bf16[16,48,256]{2,0,1:T(8,128)(2,1)S(1)}, u32[]{:S(2)}, u32[]{:S(2)}) %all-to-all-start.1) | async-done | bytes 393248 | tf_op jit(solution)/shard_map/all_to_all | solution.py:49
  52.5 3.4 %collective-permute-start.1 = (bf16[16,12,8,128]{3,0,2,1:T(8,128)(2,1)S(1)}, bf16[16,12,8,128]{3,0,2,1:T(8,128)(2,1)S(1)}, u32[]{:S(2)}, u32[]{:S(2)}) collective-permute-start(bf16[16,12,8,128]{3,0,2,1:T(8,128)(2,1)S(1)} %copy.96), channel_id=1, source_target_pairs={{4,0},{8,4},{12,8},{16,12},{20,16},{24,20},{28,24},{32,28},{36,32}... | collective-permute-start | bytes 1179656 | tf_op jit(solution)/shard_map/ppermute | solution.py:18
  55.9 1.4 collective-permute-start
  58.8 3.7 %collective-permute-done.1 = bf16[16,12,8,128]{3,0,2,1:T(8,128)(2,1)S(1)} collective-permute-done((bf16[16,12,8,128]{3,0,2,1:T(8,128)(2,1)S(1)}, bf16[16,12,8,128]{3,0,2,1:T(8,128)(2,1)S(1)}, u32[]{:S(2)}, u32[]{:S(2)}) %collective-permute-start.1) | collective-permute-done | bytes 393248 | tf_op jit(solution)/shard_map/ppermute | solution.py:18
  63.7 1.6 broadcast_select_fusion.1
  65.2 8.7 %fusion.6 = f32[12,8,2,8,128]{4,3,2,1,0:T(8,128)S(1)} fusion(bf16[12,8,5,128,128]{4,3,2,1,0:T(8,128)(2,1)} %param.11, bf16[16,12,8,5,128]{4,0,1,3,2:T(8,128)(2,1)} %bitcast.85), kind=kOutput, calls=%fused_computation.12 | convolution fusion | flops 251658240 | bytes 18481152 | tf_op jit(solution)/shard_map/lrkij,tlrkj->tlri/dot_general | solution.py:56
  74.7 4.7 %copy.103 = bf16[16,12,1024]{0,1,2:T(8,128)(2,1)} copy(bf16[16,12,1024]{2,0,1:T(8,128)(2,1)S(1)} %fusion.20) | data formatting | bytes 786432 | tf_op jit(solution)/shard_map/convert_element_type | solution.py:63
  79.4 5.1 %reshape.105 = bf16[4,2,24576]{2,1,0:T(2,128)(2,1)S(1)} reshape(bf16[1024,12,16]{2,1,0:T(8,128)(2,1)} %bitcast.83) | data formatting | bytes 786432
  84.5 8.6 %all_to_all.72 = bf16[4,2,24576]{2,1,0:T(2,128)(2,1)S(1)} all-to-all(bf16[4,2,24576]{2,1,0:T(2,128)(2,1)S(1)} %reshape.105), channel_id=1, replica_groups=mesh['horiz'=32,'depth'=4] {'depth'}, dimensions={0} | all-to-all | bytes 786432 | tf_op jit(solution)/shard_map/all_to_all | solution.py:45
  93.1 4.9 %reshape.106 = bf16[1024,12,16]{2,1,0:T(8,128)(2,1)} reshape(bf16[4,2,24576]{2,1,0:T(2,128)(2,1)S(1)} %all_to_all.72) | data formatting | bytes 786432
  98.0 4.9 %copy.123 = bf16[16,12,4,256]{3,2,0,1:T(4,128)(2,1)S(1)} copy(bf16[16,12,4,256]{0,1,3,2:T(8,128)(2,1)} %bitcast.81) | data formatting | bytes 786432 | tf_op jit(solution)/shard_map/all_to_all | solution.py:45
  103.0 1.2 copy.106
  104.2 5.1 %fusion.5 = bf16[16,48,256]{1,0,2:T(8,128)(2,1)S(1)} fusion(bf16[16,48,256]{1,0,2:T(8,128)(2,1)S(1)} %copy.106, f32[48,48,256]{1,0,2:T(8,128)} %copy.93), kind=kOutput, calls=%fused_computation.11 | convolution fusion | flops 113442816 | bytes 3145728 | tf_op jit(solution)/shard_map/pqc,tpc->tqc/dot_general | solution.py:46
  109.3 1.2 copy.108
  110.5 8.8 %all_to_all.73 = bf16[16,48,256]{2,0,1:T(8,128)(2,1)S(1)} all-to-all(bf16[16,48,256]{2,0,1:T(8,128)(2,1)S(1)} %copy.108), channel_id=1, replica_groups=mesh['horiz'=32,'depth'=4] {'depth'}, dimensions={1} | all-to-all | bytes 786432 | tf_op jit(solution)/shard_map/all_to_all | solution.py:49
  119.9 9.4 %collective-permute-start.3 = (bf16[16,12,8,128]{3,0,2,1:T(8,128)(2,1)S(1)}, bf16[16,12,8,128]{3,0,2,1:T(8,128)(2,1)S(1)}, u32[]{:S(2)}, u32[]{:S(2)}) collective-permute-start(bf16[16,12,8,128]{3,0,2,1:T(8,128)(2,1)S(1)} %copy.110), channel_id=1, source_target_pairs={{4,0},{8,4},{12,8},{16,12},{20,16},{24,20},{28,24},{32,28},{36,32}... | collective-permute-start | bytes 1179656 | tf_op jit(solution)/shard_map/ppermute | solution.py:18
  129.8 65.1 %psum.16 = f32[16]{0:T(128)S(1)} all-reduce(f32[16]{0:T(128)S(1)} %add.73), channel_id=1, replica_groups=mesh['horiz'=32,'depth'=4] {'horiz','depth'}, use_global_device_ids=true, to_apply=%region_1.3 | all-reduce | flops 16 | bytes 128 | tf_op jit(solution)/shard_map/psum | solution.py:67
  195.4 1.1 pad_maximum_fusion.1
  197.5 1.6 broadcast_select_fusion
  199.1 8.7 %fusion.9 = f32[12,8,2,8,128]{4,3,2,1,0:T(8,128)S(1)} fusion(bf16[12,8,5,128,128]{4,3,2,1,0:T(8,128)(2,1)} %param.11, bf16[16,12,8,5,128]{4,0,1,3,2:T(8,128)(2,1)} %bitcast.84), kind=kOutput, calls=%fused_computation.13 | convolution fusion | flops 251658240 | bytes 18481152 | tf_op jit(solution)/shard_map/lrkij,tlrkj->tlri/dot_general | solution.py:56
  207.8 1.4 fusion.21
  (57 shorter events, 7.0 us)
Async XLA Ops:
  0.6 73.3 %copy-start = (f32[16,16]{1,0:T(8,128)S(1)}, f32[16,16]{1,0:T(8,128)}, u32[]{:S(2)}) copy-start(f32[16,16]{1,0:T(8,128)} %param.15) | copy-start | bytes 3076
  6.3 10.9 %copy-start.13 = (s32[8,5]{1,0:T(8,128)S(1)}, s32[8,5]{1,0:T(8,128)}, u32[]{:S(2)}) copy-start(s32[8,5]{1,0:T(8,128)} %param.12) | copy-start | bytes 484
  6.3 11.1 %copy-start.5 = (f32[48,48,256]{2,1,0:T(8,128)S(1)}, f32[48,48,256]{2,1,0:T(8,128)}, u32[]{:S(2)}) copy-start(f32[48,48,256]{2,1,0:T(8,128)} %param.13) | copy-start | bytes 7077892
  12.2 11.9 %all-to-all-start = ((bf16[4,2,24576]{2,1,0:T(2,128)(2,1)}), bf16[4,2,24576]{2,1,0:T(2,128)(2,1)S(1)}, u32[]{:S(2)}, u32[]{:S(2)}) async-start(bf16[4,2,24576]{2,1,0:T(2,128)(2,1)} %reshape.103), calls=%async_computation | async-start | bytes 786432 | tf_op jit(solution)/shard_map/all_to_all | solution.py:45
  40.3 17.0 %copy-start.12 = (s32[1024]{0:T(1024)S(1)}, s32[1024]{0:T(1024)}, u32[]{:S(2)}) copy-start(s32[1024]{0:T(1024)} %param.17) | copy-start | bytes 12292
  42.3 9.7 %all-to-all-start.1 = ((bf16[16,48,256]{2,0,1:T(8,128)(2,1)}), bf16[16,48,256]{2,0,1:T(8,128)(2,1)S(1)}, u32[]{:S(2)}, u32[]{:S(2)}) async-start(bf16[16,48,256]{2,0,1:T(8,128)(2,1)} %copy.94), calls=%async_computation.1 | async-start | bytes 786432 | tf_op jit(solution)/shard_map/all_to_all | solution.py:49
  52.5 9.9 %collective-permute-start.1 = (bf16[16,12,8,128]{3,0,2,1:T(8,128)(2,1)S(1)}, bf16[16,12,8,128]{3,0,2,1:T(8,128)(2,1)S(1)}, u32[]{:S(2)}, u32[]{:S(2)}) collective-permute-start(bf16[16,12,8,128]{3,0,2,1:T(8,128)(2,1)S(1)} %copy.96), channel_id=1, source_target_pairs={{4,0},{8,4},{12,8},{16,12},{20,16},{24,20},{28,24},{32,28},{36,32}... | collective-permute-start | bytes 1179656 | tf_op jit(solution)/shard_map/ppermute | solution.py:18
  55.9 6.6 %collective-permute-start = (bf16[16,12,8,128]{3,0,2,1:T(8,128)(2,1)S(1)}, bf16[16,12,8,128]{3,0,2,1:T(8,128)(2,1)S(1)}, u32[]{:S(2)}, u32[]{:S(2)}) collective-permute-start(bf16[16,12,8,128]{3,0,2,1:T(8,128)(2,1)S(1)} %copy.96), channel_id=1, source_target_pairs={{0,4},{4,8},{8,12},{12,16},{16,20},{20,24},{24,28},{28,32},{32,36}... | collective-permute-start | bytes 1179656 | tf_op jit(solution)/shard_map/ppermute | solution.py:16
  65.2 8.8 %copy-start.2 = (bf16[4,12,2,8,256]{4,3,0,2,1:T(8,128)(2,1)S(1)}, bf16[4,12,2,8,256]{4,3,0,2,1:T(8,128)(2,1)}, u32[]{:S(2)}) copy-start(bf16[4,12,2,8,256]{4,3,0,2,1:T(8,128)(2,1)} %copy.126) | copy-start | bytes 1179652
  65.2 8.8 %copy-start.6 = (bf16[16,12,1024]{2,0,1:T(8,128)(2,1)S(1)}, bf16[16,12,1024]{2,0,1:T(8,128)(2,1)}, u32[]{:S(2)}) copy-start(bf16[16,12,1024]{2,0,1:T(8,128)(2,1)} %param.10) | copy-start | bytes 1179652
  65.2 8.8 %copy-start.7 = (f32[12,1024]{1,0:T(8,128)S(1)}, f32[12,1024]{1,0:T(8,128)}, u32[]{:S(2)}) copy-start(f32[12,1024]{1,0:T(8,128)} %compare_convert_fusion) | copy-start | bytes 147460
  65.2 8.8 %copy-start.10 = (f32[12,1024]{1,0:T(8,128)S(1)}, f32[12,1024]{1,0:T(8,128)}, u32[]{:S(2)}) copy-start(f32[12,1024]{1,0:T(8,128)} %param.14) | copy-start | bytes 147460
  74.7 133.1 %copy-start.1 = (bf16[16,12,1024]{2,0,1:T(8,128)(2,1)}, bf16[16,12,1024]{2,0,1:T(8,128)(2,1)S(1)}, u32[]{:S(2)}) copy-start(bf16[16,12,1024]{2,0,1:T(8,128)(2,1)S(1)} %fusion.20) | copy-start | bytes 1179652
  110.5 18.8 %copy-start.9 = (bf16[16,12,1024]{2,0,1:T(8,128)(2,1)S(1)}, bf16[16,12,1024]{2,0,1:T(8,128)(2,1)}, u32[]{:S(2)}) copy-start(bf16[16,12,1024]{2,0,1:T(8,128)(2,1)} %param.16) | copy-start | bytes 1179652
  119.9 75.4 %collective-permute-start.3 = (bf16[16,12,8,128]{3,0,2,1:T(8,128)(2,1)S(1)}, bf16[16,12,8,128]{3,0,2,1:T(8,128)(2,1)S(1)}, u32[]{:S(2)}, u32[]{:S(2)}) collective-permute-start(bf16[16,12,8,128]{3,0,2,1:T(8,128)(2,1)S(1)} %copy.110), channel_id=1, source_target_pairs={{4,0},{8,4},{12,8},{16,12},{20,16},{24,20},{28,24},{32,28},{36,32}... | collective-permute-start | bytes 1179656 | tf_op jit(solution)/shard_map/ppermute | solution.py:18
  129.3 66.1 %collective-permute-start.2 = (bf16[16,12,8,128]{3,0,2,1:T(8,128)(2,1)S(1)}, bf16[16,12,8,128]{3,0,2,1:T(8,128)(2,1)}, u32[]{:S(2)}, u32[]{:S(2)}) collective-permute-start(bf16[16,12,8,128]{3,0,2,1:T(8,128)(2,1)S(1)} %copy.110), channel_id=1, source_target_pairs={{0,4},{4,8},{8,12},{12,16},{16,20},{20,24},{24,28},{28,32},{32,36}... | collective-permute-start | bytes 1179656 | tf_op jit(solution)/shard_map/ppermute | solution.py:16
  129.3 66.0 %copy-start.3 = (bf16[4,12,2,8,256]{4,3,0,2,1:T(8,128)(2,1)}, bf16[4,12,2,8,256]{4,3,0,2,1:T(8,128)(2,1)S(1)}, u32[]{:S(2)}) copy-start(bf16[4,12,2,8,256]{4,3,0,2,1:T(8,128)(2,1)S(1)} %copy.128) | copy-start | bytes 1179652
  199.1 8.7 %copy-start.4 = (bf16[4,12,2,8,256]{4,3,0,2,1:T(8,128)(2,1)S(1)}, bf16[4,12,2,8,256]{4,3,0,2,1:T(8,128)(2,1)}, u32[]{:S(2)}) copy-start(bf16[4,12,2,8,256]{4,3,0,2,1:T(8,128)(2,1)} %copy-done.3) | copy-start | bytes 1179652
  199.1 8.7 %copy-start.8 = (f32[12,1024]{1,0:T(8,128)S(1)}, f32[12,1024]{1,0:T(8,128)}, u32[]{:S(2)}) copy-start(f32[12,1024]{1,0:T(8,128)} %compare_convert_fusion) | copy-start | bytes 147460
  199.1 8.7 %copy-start.11 = (f32[12,1024]{1,0:T(8,128)S(1)}, f32[12,1024]{1,0:T(8,128)}, u32[]{:S(2)}) copy-start(f32[12,1024]{1,0:T(8,128)} %param.14) | copy-start | bytes 147460
where the time goes:
time: 210 us; the launch traced here: 209 us
  blocking collectives  82.4 us (39%)
  local copies, waits for them, and re-layouts  56.2 us (27%)
  matrix products  29.6 us (14%)
  starting transfers between devices  22.6 us (11%)
  waiting for transfers between devices  11.3 us (5%)
  other arithmetic  6.09 us (3%)
    psum x1, blocking collectives, per_device(): partials.append(lax.psum(local_terms, ('horiz', 'depth')))  65.1 us
    unnamed x34, local copies, waits for them, and re-layouts  31.8 us
    dot_general x2, matrix products, per_device(): jnp.einsum('lrkij,tlrkj->tlri', transport, picked, preferred_element_type...  17.4 us
    ppermute x2, starting transfers between devices, padded(): lax.ppermute(head, axis, [((i + 1) % count, i) for i in range(count)])  12.7 us
    all_to_all x6, local copies, waits for them, and re-layouts, per_device(): lax.all_to_all(state, 'depth', split_axis=2, concat_axis=1, tiled=True)  12.3 us
    dot_general x2, matrix products, per_device(): jnp.einsum('pqc,tpc->tqc', inv_mix, full.astype(jnp.float32), precision=l...  10.1 us
    all_to_all x1, blocking collectives, per_device(): lax.all_to_all(mixed_cols, 'depth', split_axis=1, concat_axis=2, tiled=True)  8.76 us
    all_to_all x1, blocking collectives, per_device(): lax.all_to_all(state, 'depth', split_axis=2, concat_axis=1, tiled=True)  8.62 us
  transfers between devices with their start and end apart: 6, of which 3 were waited for; matrix products, arithmetic and copies ran while one was open for 4% of the time, Pallas kernels for 0%

commit v1 on v0

v1 whole, which is shorter than its diff:
```python
import functools
import math

import jax
import jax.numpy as jnp
from jax import lax
from jax.experimental import pallas as pl
from jax.experimental.pallas import tpu as pltpu
from jax.sharding import PartitionSpec as P

VMEM = pl.BlockSpec(memory_space=pltpu.VMEM)
SMEM = pl.BlockSpec(memory_space=pltpu.SMEM)
HBM = pl.BlockSpec(memory_space=pltpu.HBM)
MIB = 1024 * 1024
GROUP = 4


def split_kernel(place, state, sens, *refs):
    parts, sem = refs[:-1], refs[-1]
    depth, levels, width = len(parts), state.shape[0], parts[0].shape[2]
    copies = []
    for s in range(depth):
        start = pl.multiple_of(lax.rem(place[0] + s, depth) * width, width)
        for i, whole in enumerate((state, sens)):
            copies.append(
                pltpu.make_async_copy(
                    whole.at[:, :, pl.ds(start, width)],
                    parts[s].at[pl.ds(i * levels, levels)],
                    sem.at[2 * s + i],
                )
            )
    for copy in copies:
        copy.start()
    for copy in copies:
        copy.wait()


def list_entries(place, neighbours, entries, total_blocks):
    blocks, slots = neighbours.shape
    half = entries.shape[1] // 2
    odd = place[1]
    counts = (jnp.int32(0), jnp.int32(0))
    for b in range(blocks):
        row = place[2] * blocks + b
        for k in range(slots):
            ahead = lax.rem(neighbours[b, k] - row + blocks + total_blocks, total_blocks)
            source = b + jnp.clip(ahead, 0, 2 * blocks)
            beside = lax.div(source, blocks)
            far = (beside == 2 * odd).astype(jnp.int32)
            at = jnp.where(far == 1, half + counts[1], counts[0])
            entries[0, at] = b * slots + k
            entries[1, at] = b
            entries[2, at] = jnp.where(far == 1, source - 2 * odd * blocks, source)
            counts = (counts[0] + 1 - far, counts[1] + far)
    for begin, number, none in ((0, counts[0], 3 * blocks), (half, counts[1], blocks)):
        for g in range(GROUP - 1):
            entries[0, begin + number + g] = 0
            entries[1, begin + number + g] = 0
            entries[2, begin + number + g] = none
    entries[0, 2 * half - 1] = lax.div(counts[0] + GROUP - 1, GROUP)
    entries[1, 2 * half - 1] = lax.div(counts[1] + GROUP - 1, GROUP)
    entries[2, half - 1] = counts[0]
    entries[2, 2 * half - 1] = counts[1]


def prepare_kernel(total_blocks, place, neighbours, inverse, held, entries, sem):
    copy = pltpu.make_async_copy(inverse, held, sem.at[0])
    copy.start()
    list_entries(place, neighbours, entries, total_blocks)
    copy.wait()


def mix_kernel(levels, place, *refs):
    depth = (len(refs) - 6) // 3
    slabs, sens = refs[:depth], refs[depth : 2 * depth]
    inverse, count, before = refs[2 * depth : 2 * depth + 3]
    parts, (terms, mixed, weighted) = refs[2 * depth + 3 : -3], refs[-3:]
    tracers, cols = slabs[0].shape[1:]
    offset = sens[0].shape[0] - levels
    for s in range(depth):
        weighted[lax.rem(place[0] + depth - s, depth)] = sens[s][offset:]
    terms[...] = before[...]
    for target in range(depth):
        at = lax.rem(target - place[0] + depth, depth)
        for lane in range(0, cols, 128):
            lanes = slice(lane, lane + 128)
            here = pl.ds(pl.multiple_of(place[0] * cols + lane, 128), 128)
            totals = tuple(jnp.zeros((tracers, 128), jnp.float32) for _ in range(levels))
            for s in range(depth):
                base = lax.rem(place[0] + depth - s, depth) * levels

                def add(p, totals, s=s, base=base):
                    value = slabs[s][p, :, lanes].astype(jnp.float32)
                    rows = inverse[base + p, target * levels : (target + 1) * levels, lanes]
                    return tuple(t + rows[q : q + 1] * value for q, t in enumerate(totals))

                totals = lax.fori_loop(0, levels, add, totals, unroll=4)
            wet_levels = count[:, here] - target * levels
            term = jnp.zeros((tracers, 128), jnp.float32)
            for q in range(levels):
                value = totals[q].astype(jnp.bfloat16)
                mixed[at, q, :, lanes] = value
                product = value.astype(jnp.float32) * weighted[target, q, :, lanes].astype(jnp.float32)
                term = term + jnp.where(wet_levels > q, product, 0.0)
            terms[...] += term
    high = terms[...].astype(jnp.bfloat16)
    low = (terms[...] - high.astype(jnp.float32)).astype(jnp.bfloat16)
    for s in range(depth):
        parts[s][:levels] = mixed[s]
        parts[s][levels] = jnp.concatenate([high, low], axis=1)


def gather_kernel(place, *refs):
    slabs, mixed, terms = refs[:-2], refs[-2], refs[-1]
    depth, levels = len(slabs), mixed.shape[1]
    per = slabs[0].shape[2] // 128
    total = jnp.zeros(terms.shape, jnp.float32)
    for s in range(depth):
        origin = lax.rem(place[0] + depth - s, depth)
        for i in range(per):
            mixed[origin * per + i] = slabs[s][:levels, :, i * 128 : (i + 1) * 128]
        behind = slabs[s][levels].astype(jnp.float32)
        total = total + (behind[:, :128] + behind[:, 128:])
    terms[...] = total


def add_entries(entries, start, steps, weights, near, total, ready=None):
    levels = near.shape[1]
    zero = jnp.zeros(near.shape[2:], jnp.bfloat16)
    tracers = zero.shape[0]

    def step(i, _):
        if ready is not None:
            for g in range(GROUP):
                ready(start + i * GROUP + g)
        found = []
        for g in range(GROUP):
            at = start + i * GROUP + g
            entry, block, source = entries[0, at], entries[1, at], entries[2, at]
            for l in range(0, levels, 2):
                lhs = jnp.concatenate([weights[entry, l], weights[entry, l + 1]], axis=1)
                rhs = jnp.concatenate(
                    [
                        jnp.concatenate([near[source, l], zero], axis=1),
                        jnp.concatenate([zero, near[source, l + 1]], axis=1),
                    ],
                    axis=0,
                )
                if g % 2:
                    lhs, rhs = rhs, lhs
                moved = lax.dot_general(
                    lhs, rhs, (((1,), (1,)), ((), ())), preferred_element_type=jnp.float32
                )
                found.append((g, block, l, moved))
        for g, block, l, moved in found:
            moved = moved if g % 2 else moved.T
            total[block, l] += moved[:tracers]
            total[block, l + 1] += moved[tracers:]
        return 0

    lax.fori_loop(0, steps, step, 0)


def near_kernel(load, place, entries, weights, own, mate, state, rates, coupling, *refs):
    if load:
        held, total, near, rates_in, extra, state_in, sem = refs
    else:
        total, near, rates_in, extra = refs
        held, state_in = weights, state
    blocks, levels, tracers, _ = own.shape
    odd = place[1]
    half = entries.shape[1] // 2
    more = [pltpu.make_async_copy(rates, rates_in, extra.at[0])]
    if load:
        more.append(pltpu.make_async_copy(state, state_in, extra.at[1]))
    for copy in more:
        copy.start()

    ready = None
    if load:
        slots = weights.shape[2]

        def fetch(at):
            entry = entries[0, at]
            return pltpu.make_async_copy(
                weights.at[:, lax.div(entry, slots), lax.rem(entry, slots)],
                held.at[entry],
                sem.at[entry],
            )

        def begin(at, _):
            fetch(at).start()
            return 0

        def finish(at, _):
            fetch(at).wait()
            return 0

        lax.fori_loop(0, entries[2, half - 1], begin, 0)
        lax.fori_loop(half, half + entries[2, 2 * half - 1], begin, 0)

        def ready(at):
            @pl.when(at < entries[2, half - 1])
            def _():
                fetch(at).wait()

    near[pl.ds(blocks, blocks)] = own[...]
    near[pl.ds((1 - odd) * 2 * blocks, blocks)] = mate[...]
    near[3 * blocks] = jnp.zeros(near.shape[1:], near.dtype)
    total[...] = jnp.zeros(total.shape, total.dtype)
    add_entries(entries, 0, entries[0, 2 * half - 1], held, near, total, ready)
    for copy in more:
        copy.wait()
    for b in range(blocks):
        lanes = slice(b * 128, (b + 1) * 128)
        values = jnp.concatenate([own[b, l] for l in range(levels)], axis=1)
        both = jnp.dot(coupling[...], values, preferred_element_type=jnp.float32)
        both = both[:tracers] + both[tracers:]
        for l in range(levels):
            source = rates_in[l : l + 1, lanes] * both[:, l * 128 : (l + 1) * 128]
            total[b, l] += source - state_in[l, :, lanes].astype(jnp.float32)
    if load:
        lax.fori_loop(half, half + entries[2, 2 * half - 1], finish, 0)


def far_kernel(place, entries, weights, far, before, count, new, *refs):
    parts, near, total = refs[:-2], refs[-2], refs[-1]
    blocks, levels, tracers, _ = far.shape
    half = entries.shape[1] // 2
    near[pl.ds(0, blocks)] = far[...]
    near[blocks] = jnp.zeros(near.shape[1:], near.dtype)
    total[...] = before[...]
    add_entries(entries, half, entries[1, 2 * half - 1], weights, near, total)
    for b in range(blocks):
        lanes = slice(b * 128, (b + 1) * 128)
        wet_levels = count[:, lanes] - place[0] * levels
        for l in range(levels):
            value = jnp.where(wet_levels > l, total[b, l], 0.0)
            new[l, :, lanes] = value.astype(jnp.bfloat16)
    depth = len(parts)
    for s in range(depth):
        width = parts[s].shape[2]
        start = lax.rem(place[0] + s, depth) * width
        parts[s][...] = new[:, :, pl.ds(pl.multiple_of(start, width), width)]


def ring(count, shift):
    return [(j, (j + shift) % count) for j in range(count)]


def exchange(parts, axis):
    count = len(parts)
    return [parts[0]] + [
        lax.ppermute(parts[s], axis, ring(count, s)) for s in range(1, count)
    ]


def params(mib):
    return pltpu.CompilerParams(vmem_limit_bytes=mib * MIB)


def cost(flops, size):
    return pl.CostEstimate(flops=flops, bytes_accessed=size, transcendentals=0)


def per_device(
    adjoint_seed, transport, neighbours, inv_mix, rates, coupling, sensitivity, depth_count
):
    tracers, levels, cols = adjoint_seed.shape
    blocks, slots = neighbours.shape
    horiz, depth = lax.axis_size("horiz"), lax.axis_size("depth")
    total_blocks = blocks * horiz
    h = lax.axis_index("horiz")
    place = jnp.stack([lax.axis_index("depth"), h % 2, h]).astype(jnp.int32)
    state = jnp.transpose(adjoint_seed, (1, 0, 2))
    sens = jnp.transpose(sensitivity, (1, 0, 2))
    count = depth_count.reshape(1, cols)
    mixing = coupling.T
    high = lax.reduce_precision(mixing, 8, 7)
    pair = jnp.concatenate([high, mixing - high], axis=0).astype(jnp.bfloat16)

    width = cols // depth
    block_shape = (blocks, levels, tracers, 128)
    terms_shape = jax.ShapeDtypeStruct((tracers, 128), jnp.float32)
    swap = [(i, i ^ 1) for i in range(horiz)]
    cross = []
    for i in range(1, horiz, 2):
        cross += [(i, (i + 1) % horiz), ((i + 1) % horiz, i)]

    def keep(value):
        return pltpu.with_memory_space_constraint(value, pltpu.VMEM)

    def leave(value):
        return pltpu.with_memory_space_constraint(value, pltpu.HBM)

    parts = pl.pallas_call(
        split_kernel,
        out_shape=[jax.ShapeDtypeStruct((2 * levels, tracers, width), jnp.bfloat16)] * depth,
        in_specs=[SMEM, HBM, HBM],
        out_specs=[VMEM] * depth,
        scratch_shapes=[pltpu.SemaphoreType.DMA((2 * depth,))],
        compiler_params=params(4),
        name="split",
    )(place, leave(state), leave(sens))
    slabs = exchange(parts, "depth")
    sens_slabs = slabs
    inverse, entries = pl.pallas_call(
        functools.partial(prepare_kernel, total_blocks),
        out_shape=[
            pltpu.VMEM(inv_mix.shape, jnp.float32),
            jax.ShapeDtypeStruct((3, 128), jnp.int32),
        ],
        in_specs=[SMEM, SMEM, HBM],
        out_specs=[VMEM, SMEM],
        scratch_shapes=[pltpu.SemaphoreType.DMA((1,))],
        compiler_params=params(4),
        name="prepare",
    )(place, neighbours, leave(inv_mix))
    results = []
    terms = jnp.zeros((tracers, 128), jnp.float32)
    held = None
    for step in range(2):
        last = step == 1
        *parts, terms = pl.pallas_call(
            functools.partial(mix_kernel, levels),
            out_shape=[jax.ShapeDtypeStruct((levels + 1, tracers, width), jnp.bfloat16)] * depth
            + [terms_shape],
            in_specs=[SMEM] + [VMEM] * (2 * depth + 3),
            out_specs=[VMEM] * (depth + 1),
            scratch_shapes=[pltpu.VMEM((depth, levels, tracers, width), jnp.bfloat16)] * 2,
            compiler_params=params(4),
            name="mix",
        )(place, *slabs, *sens_slabs, keep(inverse), count, terms)
        slabs = exchange(parts, "depth")
        own, total_terms = pl.pallas_call(
            gather_kernel,
            out_shape=[jax.ShapeDtypeStruct(block_shape, jnp.bfloat16), terms_shape],
            in_specs=[SMEM] + [VMEM] * depth,
            out_specs=[VMEM] * 2,
            compiler_params=params(4),
            name="gather",
        )(place, *slabs)
        mate = lax.ppermute(own, "horiz", swap)
        far = lax.ppermute(own, "horiz", cross)
        total_shape = jax.ShapeDtypeStruct(block_shape, jnp.float32)
        scratch = [
            pltpu.VMEM((3 * blocks + 1,) + block_shape[1:], jnp.bfloat16),
            pltpu.VMEM((levels, cols), jnp.float32),
            pltpu.SemaphoreType.DMA((2,)),
        ]
        if not last:
            held, total = pl.pallas_call(
                functools.partial(near_kernel, True),
                out_shape=[
                    pltpu.VMEM((blocks * slots, levels, 128, 128), jnp.bfloat16),
                    total_shape,
                ],
                in_specs=[SMEM, SMEM, HBM, VMEM, VMEM, HBM, HBM, VMEM],
                out_specs=[VMEM, VMEM],
                scratch_shapes=scratch
                + [
                    pltpu.VMEM((levels, tracers, cols), jnp.bfloat16),
                    pltpu.SemaphoreType.DMA((blocks * slots,)),
                ],
                compiler_params=params(4),
                cost_estimate=cost(0, 16 * MIB),
                name="near_load",
            )(place, entries, leave(transport), own, mate, leave(state), leave(rates), pair)
        else:
            total = pl.pallas_call(
                functools.partial(near_kernel, False),
                out_shape=total_shape,
                in_specs=[SMEM, SMEM, VMEM, VMEM, VMEM, VMEM, HBM, VMEM],
                out_specs=VMEM,
                scratch_shapes=scratch,
                compiler_params=params(4),
                cost_estimate=cost(0, 16 * MIB),
                name="near",
            )(place, entries, keep(held), own, mate, state, leave(rates), pair)
        whole = jax.ShapeDtypeStruct((levels, tracers, cols), jnp.bfloat16)
        slab = jax.ShapeDtypeStruct((levels, tracers, width), jnp.bfloat16)
        state, *parts = pl.pallas_call(
            far_kernel,
            out_shape=[whole] + ([] if last else [slab] * depth),
            in_specs=[SMEM] * 2 + [VMEM] * 4,
            out_specs=[VMEM] * (1 if last else depth + 1),
            scratch_shapes=[
                pltpu.VMEM((blocks + 1,) + block_shape[1:], jnp.bfloat16),
                pltpu.VMEM(block_shape, jnp.float32),
            ],
            compiler_params=params(4),
            name="far",
        )(place, entries, keep(held), far, total, count)
        results.append(jnp.transpose(state, (1, 0, 2)))
        if not last:
            slabs = exchange(parts, "depth")
    terms = total_terms
    for flip in (1, 3, 7, 9, 25):
        if flip == 7:
            terms, _ = lax.optimization_barrier((terms, total))
        terms = terms + lax.ppermute(terms, "horiz", [(i, i ^ flip) for i in range(horiz)])
    gradient = jnp.sum(terms, axis=1) / math.sqrt(levels * depth * total_blocks * 128)
    return (results[0], results[1], gradient)


def solution(mesh):
    return jax.shard_map(
        per_device,
        mesh=mesh,
        in_specs=(
            P(None, "depth", "horiz"),
            P("depth", "horiz", None, None, None),
            P("horiz", None),
            P(None, None, ("horiz", "depth")),
            P("depth", "horiz"),
            P(),
            P(None, "depth", "horiz"),
            P("horiz"),
        ),
        out_specs=(P(None, "depth", "horiz"), P(None, "depth", "horiz"), P()),
        check_vma=False,
    )
```

time: 210 us -> 101 us (0.48)
  blocking collectives: 82.4 us -> 0 us
  local copies, waits for them, and re-layouts: 56.2 us -> 3.75 us
  Pallas kernels: 0 us -> 34.4 us
  matrix products: 29.6 us -> 0 us
  waiting for transfers between devices: 11.3 us -> 30.1 us
  starting transfers between devices: 22.6 us -> 31 us
  other arithmetic: 6.09 us -> 1.43 us
    psum x1 -> x0, blocking collectives: 65.1 us -> none  [per_device(): partials.append(lax.psum(local_terms, ('horiz', 'depth')))]
    pallas_call x0 -> x10, Pallas kernels: none -> 34.4 us  [the longest x2 8.78 us: per_device(): pl.pallas_call(functools.partial(mix_kernel, levels), out_shape=[jax.Shap...]
    dot_general x6 -> x0, matrix products: 29.6 us -> none  [the longest x2 17.4 us: per_device(): jnp.einsum('lrkij,tlrkj->tlri', transport, picked, preferred_element_type...]
    unnamed x34 -> x13, local copies, waits for them, and re-layouts: 31.8 us -> 3.75 us
    ppermute x4 -> x21, waiting for transfers between devices: 3.7 us -> 30.1 us  [the longest x5 15.1 us: per_device(): lax.ppermute(terms, 'horiz', [(i, i ^ flip) for i in range(horiz)])]
    all_to_all x2 -> x0, blocking collectives: 17.4 us -> none  [the longest x1 8.76 us: per_device(): lax.all_to_all(mixed_cols, 'depth', split_axis=1, concat_axis=2, tiled=True)]
    ppermute x4 -> x21, starting transfers between devices: 14.1 us -> 31 us  [the longest x12 17.1 us: exchange(): lax.ppermute(parts[s], axis, ring(count, s))]
    all_to_all x10 -> x0, local copies, waits for them, and re-layouts: 13.7 us -> none  [the longest x6 12.3 us: per_device(): lax.all_to_all(state, 'depth', split_axis=2, concat_axis=1, tiled=True)]
  transfers between devices with their start and end apart: 6 -> 21, of which waited for: 3 -> 15; matrix products, arithmetic and copies ran while one was open for 4% -> 2% of each run, Pallas kernels for 0% -> 19%
where the time goes in v1:
time: 101 us
  Pallas kernels  34.4 us (34%)
  starting transfers between devices  31 us (31%)
  waiting for transfers between devices  30.1 us (30%)
  local copies, waits for them, and re-layouts  3.75 us (4%)
  other arithmetic  1.43 us (1%)
    ppermute x12, starting transfers between devices, exchange(): lax.ppermute(parts[s], axis, ring(count, s))  17.1 us
    ppermute x5, waiting for transfers between devices, per_device(): lax.ppermute(terms, 'horiz', [(i, i ^ flip) for i in range(horiz)])  15.1 us
    ppermute x12, waiting for transfers between devices, exchange(): lax.ppermute(parts[s], axis, ring(count, s))  14.9 us
    ppermute x2, starting transfers between devices, per_device(): mate = lax.ppermute(own, 'horiz', swap)  10.7 us
    pallas_call x2, Pallas kernels, per_device(): pl.pallas_call(functools.partial(mix_kernel, levels), out_shape=[jax.Shap...  8.78 us
    pallas_call x1, Pallas kernels, per_device(): pl.pallas_call(functools.partial(near_kernel, True), out_shape=[pltpu.VME...  8.44 us
    pallas_call x1, Pallas kernels, per_device(): pl.pallas_call(functools.partial(near_kernel, False), out_shape=total_sha...  5.99 us
    pallas_call x2, Pallas kernels, per_device(): pl.pallas_call(far_kernel, out_shape=[whole] + ([] if last else [slab] *...  4.65 us
  transfers between devices with their start and end apart: 21, of which 15 were waited for; matrix products, arithmetic and copies ran while one was open for 2% of the time, Pallas kernels for 19%

profile of v1, /device:TPU:1, one launch (start us, length us, event | category | flops | bytes accessed | tf_op | source)
XLA Modules:
  0.0 101.5 jit_solution(10255573811658238011)
XLA Ops:
  0.7 1.8 %split.1 = (bf16[24,16,256]{2,1,0:T(8,128)(2,1)S(1)}, bf16[24,16,256]{2,1,0:T(8,128)(2,1)S(1)}, bf16[24,16,256]{2,1,0:T(8,128)(2,1)S(1)}, bf16[24,16,256]{2,1,0:T(8,128)(2,1)S(1)}) custom-call(s32[3]{0:T(128)S(1)} %pad_add_fusion.place, bf16[12,16,1024]{2,1,0:T(8,128)(2,1)} %bitcast.16, bf16[12,16,1024]{2,1,0:T(8,128)(2,1)} %bitcast.18), custom_call_target="tpu_custom_call" | custom-call | tf_op jit(solution)/shard_map/split/pallas_call | solution.py:296
  2.6 2.2 %collective-permute-start = (bf16[24,16,256]{2,1,0:T(8,128)(2,1)S(1)}, bf16[24,16,256]{2,1,0:T(8,128)(2,1)S(1)}, u32[]{:S(2)}, u32[]{:S(2)}) collective-permute-start(bf16[24,16,256]{2,1,0:T(8,128)(2,1)S(1)} %get-tuple-element.31), channel_id=1, source_target_pairs={{0,1},{1,2},{2,3},{3,0},{4,5},{5,6},{6,7},{7,4},{8,9},{9,10},{10,1... | collective-permute-start | bytes 589832 | tf_op jit(solution)/shard_map/ppermute | solution.py:254
  4.8 2.6 %collective-permute-start.1 = (bf16[24,16,256]{2,1,0:T(8,128)(2,1)S(1)}, bf16[24,16,256]{2,1,0:T(8,128)(2,1)S(1)}, u32[]{:S(2)}, u32[]{:S(2)}) collective-permute-start(bf16[24,16,256]{2,1,0:T(8,128)(2,1)S(1)} %get-tuple-element.32), channel_id=1, source_target_pairs={{0,2},{1,3},{2,0},{3,1},{4,6},{5,7},{6,4},{7,5},{8,10},{9,11},{10,... | collective-permute-start | bytes 589832 | tf_op jit(solution)/shard_map/ppermute | solution.py:254
  7.4 1.1 %collective-permute-start.2 = (bf16[24,16,256]{2,1,0:T(8,128)(2,1)S(1)}, bf16[24,16,256]{2,1,0:T(8,128)(2,1)S(1)}, u32[]{:S(2)}, u32[]{:S(2)}) collective-permute-start(bf16[24,16,256]{2,1,0:T(8,128)(2,1)S(1)} %get-tuple-element.33), channel_id=1, source_target_pairs={{0,3},{1,0},{2,1},{3,2},{4,7},{5,4},{6,5},{7,6},{8,11},{9,8},{10,9... | collective-permute-start | bytes 589832 | tf_op jit(solution)/shard_map/ppermute | solution.py:254
  9.2 2.9 %prepare.1 = (f32[48,48,256]{2,1,0:T(8,128)S(1)}, s32[3,128]{1,0:T(4,128)S(1)}) custom-call(s32[3]{0:T(128)S(1)} %pad_add_fusion.place, s32[8,5]{1,0:T(8,128)S(1)} %copy-done.5, f32[48,48,256]{2,1,0:T(8,128)} %inverse.1), custom_call_target="tpu_custom_call" | custom-call | tf_op jit(solution)/shard_map/prepare/pallas_call | solution.py:307
  12.1 3.9 %collective-permute-done.1.refs_2_.refs_6_ = bf16[24,16,256]{2,1,0:T(8,128)(2,1)S(1)} collective-permute-done((bf16[24,16,256]{2,1,0:T(8,128)(2,1)S(1)}, bf16[24,16,256]{2,1,0:T(8,128)(2,1)S(1)}, u32[]{:S(2)}, u32[]{:S(2)}) %collective-permute-start.1) | collective-permute-done | bytes 196640 | tf_op jit(solution)/shard_map/ppermute | solution.py:254
  16.6 4.1 %mix.2 = (bf16[13,16,256]{2,1,0:T(8,128)(2,1)S(1)}, bf16[13,16,256]{2,1,0:T(8,128)(2,1)S(1)}, bf16[13,16,256]{2,1,0:T(8,128)(2,1)S(1)}, bf16[13,16,256]{2,1,0:T(8,128)(2,1)S(1)}, f32[16,128]{1,0:T(8,128)S(1)}) custom-call(s32[3]{0:T(128)S(1)} %pad_add_fusion.place, bf16[24,16,256]{2,1,0:T(8,128)(2,1)S(1)} %get-tuple-element.30.refs_0_.refs_4_, ...), custom_call_target="tpu_custom_call" | custom-call | tf_op jit(solution)/shard_map/mix/pallas_call | solution.py:324
  20.7 1.3 %collective-permute-start.3 = (bf16[13,16,256]{2,1,0:T(8,128)(2,1)S(1)}, bf16[13,16,256]{2,1,0:T(8,128)(2,1)S(1)}, u32[]{:S(2)}, u32[]{:S(2)}) collective-permute-start(bf16[13,16,256]{2,1,0:T(8,128)(2,1)S(1)} %get-tuple-element.36), channel_id=1, source_target_pairs={{0,1},{1,2},{2,3},{3,0},{4,5},{5,6},{6,7},{7,4},{8,9},{9,10},{10,1... | collective-permute-start | bytes 319496 | tf_op jit(solution)/shard_map/ppermute | solution.py:254
  22.0 2.7 %collective-permute-start.4 = (bf16[13,16,256]{2,1,0:T(8,128)(2,1)S(1)}, bf16[13,16,256]{2,1,0:T(8,128)(2,1)S(1)}, u32[]{:S(2)}, u32[]{:S(2)}) collective-permute-start(bf16[13,16,256]{2,1,0:T(8,128)(2,1)S(1)} %get-tuple-element.37), channel_id=1, source_target_pairs={{0,2},{1,3},{2,0},{3,1},{4,6},{5,7},{6,4},{7,5},{8,10},{9,11},{10,... | collective-permute-start | bytes 319496 | tf_op jit(solution)/shard_map/ppermute | solution.py:254
  25.6 3.4 %collective-permute-done.4.refs_2_ = bf16[13,16,256]{2,1,0:T(8,128)(2,1)S(1)} collective-permute-done((bf16[13,16,256]{2,1,0:T(8,128)(2,1)S(1)}, bf16[13,16,256]{2,1,0:T(8,128)(2,1)S(1)}, u32[]{:S(2)}, u32[]{:S(2)}) %collective-permute-start.4) | collective-permute-done | bytes 106528 | tf_op jit(solution)/shard_map/ppermute | solution.py:254
  29.6 1.2 %gather.2 = (bf16[8,12,16,128]{3,2,1,0:T(8,128)(2,1)S(1)}, f32[16,128]{1,0:T(8,128)}) custom-call(s32[3]{0:T(128)S(1)} %pad_add_fusion.place, bf16[13,16,256]{2,1,0:T(8,128)(2,1)S(1)} %get-tuple-element.35.refs_0_, bf16[13,16,256]{2,1,0:T(8,128)(2,1)S(1)} %collective-permute-done.3.refs_1_, bf16[13,16,256]{2,1,0:T(8,128)(2,1)S(1)} %collective-permute-done.4.refs_2_, ...), custom_call_target="tpu_custom_call" | custom-call | tf_op jit(solution)/shard_map/gather/pallas_call | solution.py:335
  30.8 1.7 %collective-permute-start.6 = (bf16[8,12,16,128]{3,2,1,0:T(8,128)(2,1)S(1)}, bf16[8,12,16,128]{3,2,1,0:T(8,128)(2,1)}, u32[]{:S(2)}, u32[]{:S(2)}) collective-permute-start(bf16[8,12,16,128]{3,2,1,0:T(8,128)(2,1)S(1)} %get-tuple-element.39.own), channel_id=1, source_target_pairs={{0,4},{4,0},{8,12},{12,8},{16,20},{20,16},{24,28},{28,24},{32,36},... | collective-permute-start | bytes 1179656 | tf_op jit(solution)/shard_map/ppermute | solution.py:343
  32.5 1.1 %collective-permute-start.7 = (bf16[8,12,16,128]{3,2,1,0:T(8,128)(2,1)S(1)}, bf16[8,12,16,128]{3,2,1,0:T(8,128)(2,1)}, u32[]{:S(2)}, u32[]{:S(2)}) collective-permute-start(bf16[8,12,16,128]{3,2,1,0:T(8,128)(2,1)S(1)} %get-tuple-element.39.own), channel_id=1, source_target_pairs={{4,8},{8,4},{12,16},{16,12},{20,24},{24,20},{28,32},{32,28},{36,40... | collective-permute-start | bytes 1179656 | tf_op jit(solution)/shard_map/ppermute | solution.py:344
  33.5 1.4 %copy.11 = f32[16,16]{0,1:T(8,128)} copy(f32[16,16]{1,0:T(8,128)} %param.13) | data formatting | bytes 2048 | tf_op args[5]
  35.6 8.4 %near_load.1 = (bf16[40,12,128,128]{3,2,1,0:T(8,128)(2,1)S(1)}, f32[8,12,16,128]{3,2,1,0:T(8,128)S(1)}) custom-call(s32[3]{0:T(128)S(1)} %pad_add_fusion.place, s32[3,128]{1,0:T(4,128)S(1)} %get-tuple-element.29.entries, bf16[12,8,5,128,128]{4,3,2,1,0:T(8,128)(2,1)} %weights.1, bf16[8,12,16,128]{3,2,1,0:T(8,128)(2,1)S(1)} %get-tuple-element.39.own, ...), custom_call_target="tpu_custom_call" | custom-call | bytes 16777216 | tf_op jit(solution)/shard_map/near_load/pallas_call | solution.py:352
  44.1 2.6 %far.2 = (bf16[12,16,1024]{2,1,0:T(8,128)(2,1)}, bf16[12,16,256]{2,1,0:T(8,128)(2,1)S(1)}, bf16[12,16,256]{2,1,0:T(8,128)(2,1)S(1)}, bf16[12,16,256]{2,1,0:T(8,128)(2,1)S(1)}, bf16[12,16,256]{2,1,0:T(8,128)(2,1)S(1)}) custom-call(s32[3]{0:T(128)S(1)} %pad_add_fusion.place, s32[3,128]{1,0:T(4,128)S(1)} %get-tuple-element.29.entries, ...), custom_call_target="tpu_custom_call" | custom-call | tf_op jit(solution)/shard_map/far/pallas_call | solution.py:382
  47.4 2.7 %collective-permute-start.9 = (bf16[12,16,256]{2,1,0:T(8,128)(2,1)S(1)}, bf16[12,16,256]{2,1,0:T(8,128)(2,1)S(1)}, u32[]{:S(2)}, u32[]{:S(2)}) collective-permute-start(bf16[12,16,256]{2,1,0:T(8,128)(2,1)S(1)} %get-tuple-element.45), channel_id=1, source_target_pairs={{0,2},{1,3},{2,0},{3,1},{4,6},{5,7},{6,4},{7,5},{8,10},{9,11},{10,... | collective-permute-start | bytes 294920 | tf_op jit(solution)/shard_map/ppermute | solution.py:254
  50.1 1.2 %collective-permute-done.8.refs_1_ = bf16[12,16,256]{2,1,0:T(8,128)(2,1)S(1)} collective-permute-done((bf16[12,16,256]{2,1,0:T(8,128)(2,1)S(1)}, bf16[12,16,256]{2,1,0:T(8,128)(2,1)S(1)}, u32[]{:S(2)}, u32[]{:S(2)}) %collective-permute-start.8) | collective-permute-done | bytes 98336 | tf_op jit(solution)/shard_map/ppermute | solution.py:254
  51.3 1.8 %collective-permute-done.9.refs_2_ = bf16[12,16,256]{2,1,0:T(8,128)(2,1)S(1)} collective-permute-done((bf16[12,16,256]{2,1,0:T(8,128)(2,1)S(1)}, bf16[12,16,256]{2,1,0:T(8,128)(2,1)S(1)}, u32[]{:S(2)}, u32[]{:S(2)}) %collective-permute-start.9) | collective-permute-done | bytes 98336 | tf_op jit(solution)/shard_map/ppermute | solution.py:254
  53.6 4.7 %mix.3 = (bf16[13,16,256]{2,1,0:T(8,128)(2,1)S(1)}, bf16[13,16,256]{2,1,0:T(8,128)(2,1)S(1)}, bf16[13,16,256]{2,1,0:T(8,128)(2,1)S(1)}, bf16[13,16,256]{2,1,0:T(8,128)(2,1)S(1)}, f32[16,128]{1,0:T(8,128)}) custom-call(s32[3]{0:T(128)S(1)} %pad_add_fusion.place, bf16[12,16,256]{2,1,0:T(8,128)(2,1)S(1)} %get-tuple-element.43.refs_0_, ...), custom_call_target="tpu_custom_call" | custom-call | tf_op jit(solution)/shard_map/mix/pallas_call | solution.py:324
  58.4 2.8 %collective-permute-start.12 = (bf16[13,16,256]{2,1,0:T(8,128)(2,1)S(1)}, bf16[13,16,256]{2,1,0:T(8,128)(2,1)S(1)}, u32[]{:S(2)}, u32[]{:S(2)}) collective-permute-start(bf16[13,16,256]{2,1,0:T(8,128)(2,1)S(1)} %get-tuple-element.50), channel_id=1, source_target_pairs={{0,2},{1,3},{2,0},{3,1},{4,6},{5,7},{6,4},{7,5},{8,10},{9,11},{10,... | collective-permute-start | bytes 319496 | tf_op jit(solution)/shard_map/ppermute | solution.py:254
  61.8 1.2 %collective-permute-done.11.refs_1_ = bf16[13,16,256]{2,1,0:T(8,128)(2,1)S(1)} collective-permute-done((bf16[13,16,256]{2,1,0:T(8,128)(2,1)S(1)}, bf16[13,16,256]{2,1,0:T(8,128)(2,1)S(1)}, u32[]{:S(2)}, u32[]{:S(2)}) %collective-permute-start.11) | collective-permute-done | bytes 106528 | tf_op jit(solution)/shard_map/ppermute | solution.py:254
  63.0 1.4 %collective-permute-done.12.refs_2_ = bf16[13,16,256]{2,1,0:T(8,128)(2,1)S(1)} collective-permute-done((bf16[13,16,256]{2,1,0:T(8,128)(2,1)S(1)}, bf16[13,16,256]{2,1,0:T(8,128)(2,1)S(1)}, u32[]{:S(2)}, u32[]{:S(2)}) %collective-permute-start.12) | collective-permute-done | bytes 106528 | tf_op jit(solution)/shard_map/ppermute | solution.py:254
  65.4 9.0 %collective-permute-start.15 = (bf16[8,12,16,128]{3,2,1,0:T(8,128)(2,1)S(1)}, bf16[8,12,16,128]{3,2,1,0:T(8,128)(2,1)S(1)}, u32[]{:S(2)}, u32[]{:S(2)}) collective-permute-start(bf16[8,12,16,128]{3,2,1,0:T(8,128)(2,1)S(1)} %get-tuple-element.52.own), channel_id=1, source_target_pairs={{0,4},{4,0},{8,12},{12,8},{16,20},{20,16},{24,28},{28,24},{32,36},... | collective-permute-start | bytes 1179656 | tf_op jit(solution)/shard_map/ppermute | solution.py:343
  74.4 1.4 %collective-permute-start.16 = (f32[16,128]{1,0:T(8,128)S(1)}, f32[16,128]{1,0:T(8,128)S(1)}, u32[]{:S(2)}, u32[]{:S(2)}) collective-permute-start(f32[16,128]{1,0:T(8,128)S(1)} %get-tuple-element.53), channel_id=1, source_target_pairs={{0,4},{4,0},{8,12},{12,8},{16,20},{20,16},{24,28},{28,24},{32,36},... | collective-permute-start | bytes 24584 | tf_op jit(solution)/shard_map/ppermute | solution.py:401
  77.4 4.7 %collective-permute-done.17 = f32[16,128]{1,0:T(8,128)S(1)} collective-permute-done((f32[16,128]{1,0:T(8,128)S(1)}, f32[16,128]{1,0:T(8,128)S(1)}, u32[]{:S(2)}, u32[]{:S(2)}) %collective-permute-start.17) | collective-permute-done | bytes 8224 | tf_op jit(solution)/shard_map/ppermute | solution.py:401
  82.1 1.0 copy-done
  83.1 6.0 %near.1.before = f32[8,12,16,128]{3,2,1,0:T(8,128)S(1)} custom-call(s32[3]{0:T(128)S(1)} %pad_add_fusion.place, s32[3,128]{1,0:T(4,128)S(1)} %get-tuple-element.29.entries, bf16[40,12,128,128]{3,2,1,0:T(8,128)(2,1)S(1)} %get-tuple-element.40.weights, bf16[8,12,16,128]{3,2,1,0:T(8,128)(2,1)S(1)} %get-tuple-element.52.own, ...), custom_call_target="tpu_custom_call" | custom-call | bytes 16777216 | tf_op jit(solution)/shard_map/near/pallas_call | solution.py:370
  89.2 4.3 %collective-permute-done.18 = f32[16,128]{1,0:T(8,128)S(1)} collective-permute-done((f32[16,128]{1,0:T(8,128)S(1)}, f32[16,128]{1,0:T(8,128)S(1)}, u32[]{:S(2)}, u32[]{:S(2)}) %collective-permute-start.18) | collective-permute-done | bytes 8224 | tf_op jit(solution)/shard_map/ppermute | solution.py:401
  93.5 3.1 %collective-permute-done.19 = f32[16,128]{1,0:T(8,128)S(1)} collective-permute-done((f32[16,128]{1,0:T(8,128)S(1)}, f32[16,128]{1,0:T(8,128)S(1)}, u32[]{:S(2)}, u32[]{:S(2)}) %collective-permute-start.19) | collective-permute-done | bytes 8224 | tf_op jit(solution)/shard_map/ppermute | solution.py:401
  96.6 2.1 %far.3 = bf16[12,16,1024]{2,1,0:T(8,128)(2,1)} custom-call(s32[3]{0:T(128)S(1)} %pad_add_fusion.place, s32[3,128]{1,0:T(4,128)S(1)} %get-tuple-element.29.entries, bf16[40,12,128,128]{3,2,1,0:T(8,128)(2,1)S(1)} %get-tuple-element.40.weights, bf16[8,12,16,128]{3,2,1,0:T(8,128)(2,1)S(1)} %collective-permute-done.14.far, f32[8,12,16,128]{3,2,1,0:T(8,128)S(1)} %near.1.before, ...), custom_call_target="tpu_custom_call" | custom-call | tf_op jit(solution)/shard_map/far/pallas_call | solution.py:382
  98.6 2.2 %collective-permute-done.20 = f32[16,128]{1,0:T(8,128)S(1)} collective-permute-done((f32[16,128]{1,0:T(8,128)S(1)}, f32[16,128]{1,0:T(8,128)S(1)}, u32[]{:S(2)}, u32[]{:S(2)}) %collective-permute-start.20) | collective-permute-done | bytes 8224 | tf_op jit(solution)/shard_map/ppermute | solution.py:401
  (43 shorter events, 8.7 us)
Async XLA Ops:
  0.6 43.4 %copy-start.2 = (s32[1024]{0:T(1024)S(1)}, s32[1024]{0:T(1024)}, u32[]{:S(2)}) copy-start(s32[1024]{0:T(1024)} %param.15) | copy-start | bytes 12292
  2.6 9.5 %collective-permute-start = (bf16[24,16,256]{2,1,0:T(8,128)(2,1)S(1)}, bf16[24,16,256]{2,1,0:T(8,128)(2,1)S(1)}, u32[]{:S(2)}, u32[]{:S(2)}) collective-permute-start(bf16[24,16,256]{2,1,0:T(8,128)(2,1)S(1)} %get-tuple-element.31), channel_id=1, source_target_pairs={{0,1},{1,2},{2,3},{3,0},{4,5},{5,6},{6,7},{7,4},{8,9},{9,10},{10,1... | collective-permute-start | bytes 589832 | tf_op jit(solution)/shard_map/ppermute | solution.py:254
  4.8 11.1 %collective-permute-start.1 = (bf16[24,16,256]{2,1,0:T(8,128)(2,1)S(1)}, bf16[24,16,256]{2,1,0:T(8,128)(2,1)S(1)}, u32[]{:S(2)}, u32[]{:S(2)}) collective-permute-start(bf16[24,16,256]{2,1,0:T(8,128)(2,1)S(1)} %get-tuple-element.32), channel_id=1, source_target_pairs={{0,2},{1,3},{2,0},{3,1},{4,6},{5,7},{6,4},{7,5},{8,10},{9,11},{10,... | collective-permute-start | bytes 589832 | tf_op jit(solution)/shard_map/ppermute | solution.py:254
  7.4 8.5 %collective-permute-start.2 = (bf16[24,16,256]{2,1,0:T(8,128)(2,1)S(1)}, bf16[24,16,256]{2,1,0:T(8,128)(2,1)S(1)}, u32[]{:S(2)}, u32[]{:S(2)}) collective-permute-start(bf16[24,16,256]{2,1,0:T(8,128)(2,1)S(1)} %get-tuple-element.33), channel_id=1, source_target_pairs={{0,3},{1,0},{2,1},{3,2},{4,7},{5,4},{6,5},{7,6},{8,11},{9,8},{10,9... | collective-permute-start | bytes 589832 | tf_op jit(solution)/shard_map/ppermute | solution.py:254
  8.5 0.7 copy-start.5
  15.9 0.7 copy-start.1
  20.7 10.1 %copy-start.3 = (f32[16,128]{1,0:T(8,128)}, f32[16,128]{1,0:T(8,128)S(1)}, u32[]{:S(2)}) copy-start(f32[16,128]{1,0:T(8,128)S(1)} %get-tuple-element.47.refs_10_) | copy-start | bytes 24580
  20.7 4.9 %collective-permute-start.3 = (bf16[13,16,256]{2,1,0:T(8,128)(2,1)S(1)}, bf16[13,16,256]{2,1,0:T(8,128)(2,1)S(1)}, u32[]{:S(2)}, u32[]{:S(2)}) collective-permute-start(bf16[13,16,256]{2,1,0:T(8,128)(2,1)S(1)} %get-tuple-element.36), channel_id=1, source_target_pairs={{0,1},{1,2},{2,3},{3,0},{4,5},{5,6},{6,7},{7,4},{8,9},{9,10},{10,1... | collective-permute-start | bytes 319496 | tf_op jit(solution)/shard_map/ppermute | solution.py:254
  22.0 7.0 %collective-permute-start.4 = (bf16[13,16,256]{2,1,0:T(8,128)(2,1)S(1)}, bf16[13,16,256]{2,1,0:T(8,128)(2,1)S(1)}, u32[]{:S(2)}, u32[]{:S(2)}) collective-permute-start(bf16[13,16,256]{2,1,0:T(8,128)(2,1)S(1)} %get-tuple-element.37), channel_id=1, source_target_pairs={{0,2},{1,3},{2,0},{3,1},{4,6},{5,7},{6,4},{7,5},{8,10},{9,11},{10,... | collective-permute-start | bytes 319496 | tf_op jit(solution)/shard_map/ppermute | solution.py:254
  24.7 4.8 %collective-permute-start.5 = (bf16[13,16,256]{2,1,0:T(8,128)(2,1)S(1)}, bf16[13,16,256]{2,1,0:T(8,128)(2,1)S(1)}, u32[]{:S(2)}, u32[]{:S(2)}) collective-permute-start(bf16[13,16,256]{2,1,0:T(8,128)(2,1)S(1)} %get-tuple-element.38), channel_id=1, source_target_pairs={{0,3},{1,0},{2,1},{3,2},{4,7},{5,4},{6,5},{7,6},{8,11},{9,8},{10,9... | collective-permute-start | bytes 319496 | tf_op jit(solution)/shard_map/ppermute | solution.py:254
  30.8 4.8 %collective-permute-start.6 = (bf16[8,12,16,128]{3,2,1,0:T(8,128)(2,1)S(1)}, bf16[8,12,16,128]{3,2,1,0:T(8,128)(2,1)}, u32[]{:S(2)}, u32[]{:S(2)}) collective-permute-start(bf16[8,12,16,128]{3,2,1,0:T(8,128)(2,1)S(1)} %get-tuple-element.39.own), channel_id=1, source_target_pairs={{0,4},{4,0},{8,12},{12,8},{16,20},{20,16},{24,28},{28,24},{32,36},... | collective-permute-start | bytes 1179656 | tf_op jit(solution)/shard_map/ppermute | solution.py:343
  32.5 11.6 %collective-permute-start.7 = (bf16[8,12,16,128]{3,2,1,0:T(8,128)(2,1)S(1)}, bf16[8,12,16,128]{3,2,1,0:T(8,128)(2,1)}, u32[]{:S(2)}, u32[]{:S(2)}) collective-permute-start(bf16[8,12,16,128]{3,2,1,0:T(8,128)(2,1)S(1)} %get-tuple-element.39.own), channel_id=1, source_target_pairs={{4,8},{8,4},{12,16},{16,12},{20,24},{24,20},{28,32},{32,28},{36,40... | collective-permute-start | bytes 1179656 | tf_op jit(solution)/shard_map/ppermute | solution.py:344
  35.6 18.0 %copy-start.4 = (f32[16,128]{1,0:T(8,128)S(1)}, f32[16,128]{1,0:T(8,128)}, u32[]{:S(2)}) copy-start(f32[16,128]{1,0:T(8,128)} %copy-done.3) | copy-start | bytes 24580
  46.6 4.7 %collective-permute-start.8 = (bf16[12,16,256]{2,1,0:T(8,128)(2,1)S(1)}, bf16[12,16,256]{2,1,0:T(8,128)(2,1)S(1)}, u32[]{:S(2)}, u32[]{:S(2)}) collective-permute-start(bf16[12,16,256]{2,1,0:T(8,128)(2,1)S(1)} %get-tuple-element.44), channel_id=1, source_target_pairs={{0,1},{1,2},{2,3},{3,0},{4,5},{5,6},{6,7},{7,4},{8,9},{9,10},{10,1... | collective-permute-start | bytes 294920 | tf_op jit(solution)/shard_map/ppermute | solution.py:254
  47.4 5.8 %collective-permute-start.9 = (bf16[12,16,256]{2,1,0:T(8,128)(2,1)S(1)}, bf16[12,16,256]{2,1,0:T(8,128)(2,1)S(1)}, u32[]{:S(2)}, u32[]{:S(2)}) collective-permute-start(bf16[12,16,256]{2,1,0:T(8,128)(2,1)S(1)} %get-tuple-element.45), channel_id=1, source_target_pairs={{0,2},{1,3},{2,0},{3,1},{4,6},{5,7},{6,4},{7,5},{8,10},{9,11},{10,... | collective-permute-start | bytes 294920 | tf_op jit(solution)/shard_map/ppermute | solution.py:254
  50.1 3.5 %collective-permute-start.10 = (bf16[12,16,256]{2,1,0:T(8,128)(2,1)S(1)}, bf16[12,16,256]{2,1,0:T(8,128)(2,1)S(1)}, u32[]{:S(2)}, u32[]{:S(2)}) collective-permute-start(bf16[12,16,256]{2,1,0:T(8,128)(2,1)S(1)} %get-tuple-element.46), channel_id=1, source_target_pairs={{0,3},{1,0},{2,1},{3,2},{4,7},{5,4},{6,5},{7,6},{8,11},{9,8},{10,9... | collective-permute-start | bytes 294920 | tf_op jit(solution)/shard_map/ppermute | solution.py:254
  58.3 4.8 %collective-permute-start.11 = (bf16[13,16,256]{2,1,0:T(8,128)(2,1)S(1)}, bf16[13,16,256]{2,1,0:T(8,128)(2,1)S(1)}, u32[]{:S(2)}, u32[]{:S(2)}) collective-permute-start(bf16[13,16,256]{2,1,0:T(8,128)(2,1)S(1)} %get-tuple-element.49), channel_id=1, source_target_pairs={{0,1},{1,2},{2,3},{3,0},{4,5},{5,6},{6,7},{7,4},{8,9},{9,10},{10,1... | collective-permute-start | bytes 319496 | tf_op jit(solution)/shard_map/ppermute | solution.py:254
  58.4 6.1 %collective-permute-start.12 = (bf16[13,16,256]{2,1,0:T(8,128)(2,1)S(1)}, bf16[13,16,256]{2,1,0:T(8,128)(2,1)S(1)}, u32[]{:S(2)}, u32[]{:S(2)}) collective-permute-start(bf16[13,16,256]{2,1,0:T(8,128)(2,1)S(1)} %get-tuple-element.50), channel_id=1, source_target_pairs={{0,2},{1,3},{2,0},{3,1},{4,6},{5,7},{6,4},{7,5},{8,10},{9,11},{10,... | collective-permute-start | bytes 319496 | tf_op jit(solution)/shard_map/ppermute | solution.py:254
  61.2 3.6 %collective-permute-start.13 = (bf16[13,16,256]{2,1,0:T(8,128)(2,1)S(1)}, bf16[13,16,256]{2,1,0:T(8,128)(2,1)S(1)}, u32[]{:S(2)}, u32[]{:S(2)}) collective-permute-start(bf16[13,16,256]{2,1,0:T(8,128)(2,1)S(1)} %get-tuple-element.51), channel_id=1, source_target_pairs={{0,3},{1,0},{2,1},{3,2},{4,7},{5,4},{6,5},{7,6},{8,11},{9,8},{10,9... | collective-permute-start | bytes 319496 | tf_op jit(solution)/shard_map/ppermute | solution.py:254
  65.4 16.7 %collective-permute-start.15 = (bf16[8,12,16,128]{3,2,1,0:T(8,128)(2,1)S(1)}, bf16[8,12,16,128]{3,2,1,0:T(8,128)(2,1)S(1)}, u32[]{:S(2)}, u32[]{:S(2)}) collective-permute-start(bf16[8,12,16,128]{3,2,1,0:T(8,128)(2,1)S(1)} %get-tuple-element.52.own), channel_id=1, source_target_pairs={{0,4},{4,0},{8,12},{12,8},{16,20},{20,16},{24,28},{28,24},{32,36},... | collective-permute-start | bytes 1179656 | tf_op jit(solution)/shard_map/ppermute | solution.py:343
  74.4 22.1 %collective-permute-start.14 = (bf16[8,12,16,128]{3,2,1,0:T(8,128)(2,1)S(1)}, bf16[8,12,16,128]{3,2,1,0:T(8,128)(2,1)S(1)}, u32[]{:S(2)}, u32[]{:S(2)}) collective-permute-start(bf16[8,12,16,128]{3,2,1,0:T(8,128)(2,1)S(1)} %get-tuple-element.52.own), channel_id=1, source_target_pairs={{4,8},{8,4},{12,16},{16,12},{20,24},{24,20},{28,32},{32,28},{36,40... | collective-permute-start | bytes 1179656 | tf_op jit(solution)/shard_map/ppermute | solution.py:344
  74.4 2.2 %collective-permute-start.16 = (f32[16,128]{1,0:T(8,128)S(1)}, f32[16,128]{1,0:T(8,128)S(1)}, u32[]{:S(2)}, u32[]{:S(2)}) collective-permute-start(f32[16,128]{1,0:T(8,128)S(1)} %get-tuple-element.53), channel_id=1, source_target_pairs={{0,4},{4,0},{8,12},{12,8},{16,20},{20,16},{24,28},{28,24},{32,36},... | collective-permute-start | bytes 24584 | tf_op jit(solution)/shard_map/ppermute | solution.py:401
  76.7 5.4 %collective-permute-start.17 = (f32[16,128]{1,0:T(8,128)S(1)}, f32[16,128]{1,0:T(8,128)S(1)}, u32[]{:S(2)}, u32[]{:S(2)}) collective-permute-start(f32[16,128]{1,0:T(8,128)S(1)} %add.20), channel_id=1, source_target_pairs={{0,12},{4,8},{8,4},{12,0},{16,28},{20,24},{24,20},{28,16},{32,44},... | collective-permute-start | bytes 24584 | tf_op jit(solution)/shard_map/ppermute | solution.py:401
  82.1 1.0 copy-start
  89.1 4.4 %collective-permute-start.18 = (f32[16,128]{1,0:T(8,128)S(1)}, f32[16,128]{1,0:T(8,128)S(1)}, u32[]{:S(2)}, u32[]{:S(2)}) collective-permute-start(f32[16,128]{1,0:T(8,128)S(1)} %add.21), channel_id=1, source_target_pairs={{0,28},{4,24},{8,20},{12,16},{16,12},{20,8},{24,4},{28,0},{32,60},... | collective-permute-start | bytes 24584 | tf_op jit(solution)/shard_map/ppermute | solution.py:401
  93.5 3.1 %collective-permute-start.19 = (f32[16,128]{1,0:T(8,128)S(1)}, f32[16,128]{1,0:T(8,128)S(1)}, u32[]{:S(2)}, u32[]{:S(2)}) collective-permute-start(f32[16,128]{1,0:T(8,128)S(1)} %add.22), channel_id=1, source_target_pairs={{0,36},{4,32},{8,44},{12,40},{16,52},{20,48},{24,60},{28,56},{32,4... | collective-permute-start | bytes 24584 | tf_op jit(solution)/shard_map/ppermute | solution.py:401
  96.6 4.3 %collective-permute-start.20 = (f32[16,128]{1,0:T(8,128)S(1)}, f32[16,128]{1,0:T(8,128)S(1)}, u32[]{:S(2)}, u32[]{:S(2)}) collective-permute-start(f32[16,128]{1,0:T(8,128)S(1)} %add.23), channel_id=1, source_target_pairs={{0,100},{4,96},{8,108},{12,104},{16,116},{20,112},{24,124},{28,120... | collective-permute-start | bytes 24584 | tf_op jit(solution)/shard_map/ppermute | solution.py:401

commit v2 on v1

v2 whole, which is shorter than its diff:
```python
import functools
import math

import jax
import jax.numpy as jnp
from jax import lax
from jax.experimental import pallas as pl
from jax.experimental.pallas import tpu as pltpu
from jax.sharding import PartitionSpec as P

VMEM = pl.BlockSpec(memory_space=pltpu.VMEM)
SMEM = pl.BlockSpec(memory_space=pltpu.SMEM)
HBM = pl.BlockSpec(memory_space=pltpu.HBM)
MIB = 1024 * 1024
GROUP = 4


def split_kernel(place, state, sens, *refs):
    one, two, three, own, own_sens, later, held, sem = refs
    levels, _, width = own.shape
    depth = state.shape[2] // width
    copies = [
        pltpu.make_async_copy(whole, held.at[i], sem.at[i])
        for i, whole in enumerate((state, sens))
    ]
    for copy in copies:
        copy.start()
    for i, targets in enumerate(
        (
            ((own, 0, 0), (one, 0, 1), (two, 0, 2), (three, 0, 3)),
            ((own_sens, 0, 0), (one, 1, 1), (later, 0, 2), (three, 1, 3)),
        )
    ):
        copies[i].wait()
        for part, at, s in targets:
            start = lax.rem(place[0] + s, depth) * width
            part[at * levels : (at + 1) * levels] = held[
                i, :, :, pl.ds(pl.multiple_of(start, width), width)
            ]


def list_entries(place, neighbours, entries, total_blocks):
    blocks, slots = neighbours.shape
    half = entries.shape[1] // 2
    odd = place[1]
    shift = 2 * blocks * odd
    counts = (jnp.int32(0), jnp.int32(0))
    for b in range(blocks):
        row = place[2] * blocks + (b - blocks)
        for k in range(slots):
            ahead = neighbours[b, k] - row
            ahead = jnp.where(ahead < 0, ahead + total_blocks, ahead)
            ahead = jnp.where(ahead >= total_blocks, ahead - total_blocks, ahead)
            source = b + jnp.clip(ahead, 0, 2 * blocks)
            inside = source - shift
            far = jnp.where((inside >= 0) & (inside < blocks), 1, 0)
            at = jnp.where(far == 1, half + counts[1], counts[0])
            entries[0, at] = b * slots + k
            entries[1, at] = b
            entries[2, at] = jnp.where(far == 1, inside, source)
            counts = (counts[0] + 1 - far, counts[1] + far)
    for begin, number, none in ((0, counts[0], 3 * blocks), (half, counts[1], blocks)):
        for g in range(GROUP - 1):
            entries[0, begin + number + g] = 0
            entries[1, begin + number + g] = 0
            entries[2, begin + number + g] = none
    entries[0, 2 * half - 1] = lax.div(counts[0] + GROUP - 1, GROUP)
    entries[1, 2 * half - 1] = lax.div(counts[1] + GROUP - 1, GROUP)
    entries[2, half - 1] = counts[0]
    entries[2, 2 * half - 1] = counts[1]


def prepare_kernel(inverse, held, sem):
    copy = pltpu.make_async_copy(inverse, held, sem.at[0])
    copy.start()
    copy.wait()


def list_kernel(total_blocks, place, neighbours, pair, count, entries, pair_out, count_out):
    pair_out[...] = pair[...]
    count_out[...] = count[...]
    list_entries(place, neighbours, entries, total_blocks)


def add_products(place, slabs, steps, inverse, totals, target, lanes, levels):
    depth = inverse.shape[0] // levels
    for slab, s in zip(slabs, steps):
        base = lax.rem(place[0] + depth - s, depth) * levels

        def add(p, totals):
            value = slab[p, :, lanes].astype(jnp.float32)
            rows = inverse[base + p, target * levels : (target + 1) * levels, lanes]
            return tuple(t + rows[q : q + 1] * value for q, t in enumerate(totals))

        totals = lax.fori_loop(0, levels, add, totals, unroll=levels)
    return totals


def early_kernel(place, slab, inverse, partial):
    levels, tracers, cols = slab.shape
    for target in range(inverse.shape[0] // levels):
        for lane in range(0, cols, 128):
            lanes = slice(lane, lane + 128)
            totals = tuple(jnp.zeros((tracers, 128), jnp.float32) for _ in range(levels))
            totals = add_products(place, [slab], [0], inverse, totals, target, lanes, levels)
            for q in range(levels):
                partial[target, q, :, lanes] = totals[q]


def weigh(place, pairs, count):
    total = None
    for s, mixed, sens in pairs:
        levels, _, cols = pairs[0][2].shape
        depth = count.shape[1] // cols
        offset = sens.shape[0] - levels
        target = lax.rem(place[0] + depth - s, depth)
        for lane in range(0, cols, 128):
            lanes = slice(lane, lane + 128)
            here = pl.ds(pl.multiple_of(place[0] * cols + lane, 128), 128)
            wet_levels = count[:, here] - target * levels
            for q in range(levels):
                value = sum(part[q, :, lanes].astype(jnp.float32) for part in mixed)
                product = value * sens[offset + q, :, lanes].astype(jnp.float32)
                product = jnp.where(wet_levels > q, product, 0.0)
                total = product if total is None else total + product
    return total


def weigh_kernel(place, *refs):
    own, one, three, own_sens, one_sens, three_sens, count, terms = refs
    pairs = ((0, [own], own_sens), (1, [three], one_sens), (3, [one], three_sens))
    terms[...] = weigh(place, pairs, count)


def mix_kernel(number, place, *refs):
    mixed = refs[-1]
    depth, levels, tracers, cols = mixed.shape
    slabs, inverse, partial = refs[: depth - 1], refs[depth - 1], refs[depth]
    parts = refs[-1 - depth : -1]
    for target in range(depth):
        at = lax.rem(target - place[0] + depth, depth)
        for lane in range(0, cols, 128):
            lanes = slice(lane, lane + 128)
            totals = tuple(partial[target, q, :, lanes] for q in range(levels))
            totals = add_products(
                place, slabs, range(1, depth), inverse, totals, target, lanes, levels
            )
            for q in range(levels):
                mixed[at, q, :, lanes] = totals[q].astype(jnp.bfloat16)
    for s in range(depth):
        parts[s][:levels] = mixed[s]
    if number:
        parts[depth - 1][levels:] = refs[depth + 1][...]


def mix_last_kernel(place, *refs):
    mixed = refs[-1]
    depth, levels = mixed.shape[:2]
    own_sens, one_sens, three_sens, early_mixed, count, before = refs[depth + 1 : depth + 7]
    parts = refs[-1 - depth : -1]
    mix_kernel(0, place, *refs[: depth + 1], *parts, mixed)
    pairs = (
        (0, [mixed.at[0]], own_sens),
        (1, [mixed.at[3]], one_sens),
        (2, [mixed.at[2], early_mixed], refs[2]),
        (3, [mixed.at[1]], three_sens),
    )
    terms = before[...] + weigh(place, pairs, count)
    high = terms.astype(jnp.bfloat16)
    low = (terms - high.astype(jnp.float32)).astype(jnp.bfloat16)
    for s in range(depth):
        parts[s][levels] = jnp.concatenate([high, low], axis=1)


def gather_kernel(depth, scale, place, *refs):
    slabs, mixed = refs[:depth], refs[depth]
    levels = mixed.shape[1]
    per = slabs[0].shape[2] // 128
    for s in range(depth):
        origin = lax.rem(place[0] + depth - s, depth)
        for i in range(per):
            mixed[origin * per + i] = slabs[s][:levels, :, i * 128 : (i + 1) * 128]
    if len(refs) > depth + 1:
        terms, message = refs[depth + 1 :]
        total = jnp.zeros(terms.shape, jnp.float32)
        for s in range(depth):
            behind = slabs[s][levels].astype(jnp.float32)
            total = total + (behind[:, :128] + behind[:, 128:])
        total = jnp.broadcast_to(jnp.sum(total, axis=1, keepdims=True), terms.shape) * scale
        terms[...] = total
        high = total.astype(jnp.bfloat16)
        blocks = mixed.shape[0]
        message[:blocks] = mixed[...]
        message[blocks, 0] = high
        message[blocks, 1] = (total - high.astype(jnp.float32)).astype(jnp.bfloat16)
        for l in range(2, levels):
            message[blocks, l] = jnp.zeros_like(high)


def add_entries(entries, start, steps, weights, near, total, ready=None):
    levels = near.shape[1]
    zero = jnp.zeros(near.shape[2:], jnp.bfloat16)
    tracers = zero.shape[0]

    def step(i, _):
        if ready is not None:
            for g in range(GROUP):
                ready(start + i * GROUP + g)
        found = []
        for g in range(GROUP):
            at = start + i * GROUP + g
            entry, block, source = entries[0, at], entries[1, at], entries[2, at]
            for l in range(0, levels, 2):
                lhs = jnp.concatenate([weights[entry, l], weights[entry, l + 1]], axis=1)
                rhs = jnp.concatenate(
                    [
                        jnp.concatenate([near[source, l], zero], axis=1),
                        jnp.concatenate([zero, near[source, l + 1]], axis=1),
                    ],
                    axis=0,
                )
                if g % 2:
                    lhs, rhs = rhs, lhs
                moved = lax.dot_general(
                    lhs, rhs, (((1,), (1,)), ((), ())), preferred_element_type=jnp.float32
                )
                found.append((g, block, l, moved))
        for g, block, l, moved in found:
            moved = moved if g % 2 else moved.T
            total[block, l] += moved[:tracers]
            total[block, l + 1] += moved[tracers:]
        return 0

    lax.fori_loop(0, steps, step, 0)


def near_kernel(load, place, entries, weights, own, mate, state, rates, coupling, *refs):
    if load:
        held, total, near, rates_in, state_in, extra, sem = refs
    else:
        total, near, rates_in, state_in, extra = refs
        held = weights
    blocks, levels, tracers, _ = own.shape
    odd = place[1]
    half = entries.shape[1] // 2
    more = [
        pltpu.make_async_copy(rates, rates_in, extra.at[0]),
        pltpu.make_async_copy(state, state_in, extra.at[1]),
    ]
    for copy in more:
        copy.start()

    ready = None
    if load:
        slots = weights.shape[2]

        def fetch(at):
            entry, block = entries[0, at], entries[1, at]
            return pltpu.make_async_copy(
                weights.at[:, block, entry - block * slots],
                held.at[entry],
                sem.at[entry],
            )

        def begin(at, _):
            fetch(at).start()
            return 0

        def finish(at, _):
            fetch(at).wait()
            return 0

        lax.fori_loop(0, entries[2, half - 1], begin, 0)
        lax.fori_loop(half, half + entries[2, 2 * half - 1], begin, 0)

        def ready(at):
            @pl.when(at < entries[2, half - 1])
            def _():
                fetch(at).wait()

    near[pl.ds(blocks, blocks)] = own[...]
    near[pl.ds((1 - odd) * 2 * blocks, blocks)] = mate[:blocks]
    near[3 * blocks] = jnp.zeros(near.shape[1:], near.dtype)

    def add_source():
        for copy in more:
            copy.wait()
        for b in range(blocks):
            lanes = slice(b * 128, (b + 1) * 128)
            values = jnp.concatenate([own[b, l] for l in range(levels)], axis=1)
            both = lax.dot_general(
                coupling[...], values, (((0,), (0,)), ((), ())), preferred_element_type=jnp.float32
            )
            both = both[:tracers] + both[tracers:]
            for l in range(levels):
                source = rates_in[l : l + 1, lanes] * both[:, l * 128 : (l + 1) * 128]
                total[b, l] += source - state_in[l, :, lanes].astype(jnp.float32)

    total[...] = jnp.zeros(total.shape, total.dtype)
    if load:
        add_source()
    steps = entries[0, 2 * half - 1]
    if not load:
        steps = lax.div(steps, 2)
    add_entries(entries, 0, steps, held, near, total, ready)
    if not load:
        add_source()
    if load:
        lax.fori_loop(half, half + entries[2, 2 * half - 1], finish, 0)


def rest_kernel(place, entries, weights, own, mate, before, total, near):
    blocks = own.shape[0]
    half = entries.shape[1] // 2
    near[pl.ds(blocks, blocks)] = own[...]
    near[pl.ds((1 - place[1]) * 2 * blocks, blocks)] = mate[:blocks]
    near[3 * blocks] = jnp.zeros(near.shape[1:], near.dtype)
    total[...] = before[...]
    steps = entries[0, 2 * half - 1]
    done = lax.div(steps, 2)
    add_entries(entries, done * GROUP, steps - done, weights, near, total)


def far_kernel(more, place, entries, weights, far, before, count, *refs):
    behind, new, parts, (near, total) = refs[:more], refs[more], refs[more + 1 : -2], refs[-2:]
    blocks, levels, tracers, _ = far.shape
    half = entries.shape[1] // 2
    near[pl.ds(0, blocks)] = far[...]
    near[blocks] = jnp.zeros(near.shape[1:], near.dtype)
    total[...] = before[...]
    add_entries(entries, half, entries[1, 2 * half - 1], weights, near, total)
    for b in range(blocks):
        lanes = slice(b * 128, (b + 1) * 128)
        wet_levels = count[:, lanes] - place[0] * levels
        for l in range(levels):
            value = jnp.where(wet_levels > l, total[b, l], 0.0)
            new[l, :, lanes] = value.astype(jnp.bfloat16)
    depth = len(parts)
    for s in range(depth):
        width = parts[s].shape[2]
        start = lax.rem(place[0] + s, depth) * width
        parts[s][:levels] = new[:, :, pl.ds(pl.multiple_of(start, width), width)]
    for passed_on in behind:
        parts[depth - 1][levels:] = passed_on[levels:]


def ring(count, shift):
    return [(j, (j + shift) % count) for j in range(count)]


def exchange(parts, axis):
    count = len(parts)
    return [parts[0]] + [
        lax.ppermute(parts[s], axis, ring(count, s)) for s in range(1, count)
    ]


def params(mib):
    return pltpu.CompilerParams(vmem_limit_bytes=mib * MIB)


def cost(flops, size):
    return pl.CostEstimate(flops=flops, bytes_accessed=size, transcendentals=0)


def per_device(
    adjoint_seed, transport, neighbours, inv_mix, rates, coupling, sensitivity, depth_count
):
    tracers, levels, cols = adjoint_seed.shape
    blocks, slots = neighbours.shape
    horiz, depth = lax.axis_size("horiz"), lax.axis_size("depth")
    total_blocks = blocks * horiz
    h = lax.axis_index("horiz")
    place = jnp.stack([lax.axis_index("depth"), h % 2, h]).astype(jnp.int32)
    state = jnp.transpose(adjoint_seed, (1, 0, 2))
    sens = jnp.transpose(sensitivity, (1, 0, 2))
    count = depth_count.reshape(1, cols)
    high = lax.reduce_precision(coupling, 8, 7)
    pair = jnp.concatenate([high, coupling - high], axis=1).astype(jnp.bfloat16)
    scale = 1.0 / math.sqrt(levels * depth * total_blocks * 128)

    width = cols // depth
    block_shape = (blocks, levels, tracers, 128)
    terms_shape = jax.ShapeDtypeStruct((tracers, 128), jnp.float32)
    swap = [(i, i ^ 1) for i in range(horiz)]
    cross = []
    for i in range(1, horiz, 2):
        cross += [(i, (i + 1) % horiz), ((i + 1) % horiz, i)]

    def keep(value):
        return pltpu.with_memory_space_constraint(value, pltpu.VMEM)

    def leave(value):
        return pltpu.with_memory_space_constraint(value, pltpu.HBM)

    whole = jax.ShapeDtypeStruct((levels, tracers, cols), jnp.bfloat16)
    slab = jax.ShapeDtypeStruct((levels, tracers, width), jnp.bfloat16)
    longer = jax.ShapeDtypeStruct((levels + 1, tracers, width), jnp.bfloat16)
    total_shape = jax.ShapeDtypeStruct(block_shape, jnp.float32)
    partial_shape = jax.ShapeDtypeStruct((depth, levels, tracers, width), jnp.float32)
    mixed_scratch = pltpu.VMEM((depth, levels, tracers, width), jnp.bfloat16)

    def several(number):
        return jax.ShapeDtypeStruct((number * levels, tracers, width), jnp.bfloat16)

    *messages, own_state, own_sens, later_sens = pl.pallas_call(
        split_kernel,
        out_shape=[several(number) for number in (2, 1, 2, 1, 1, 1)],
        in_specs=[SMEM, HBM, HBM],
        out_specs=[VMEM] * 6,
        scratch_shapes=[
            pltpu.VMEM((2,) + whole.shape, jnp.bfloat16),
            pltpu.SemaphoreType.DMA((2,)),
        ],
        compiler_params=params(8),
        name="split",
    )(place, leave(state), leave(sens))
    slabs = exchange([own_state] + messages, "depth")
    inverse = pl.pallas_call(
        prepare_kernel,
        out_shape=pltpu.VMEM(inv_mix.shape, jnp.float32),
        in_specs=[HBM],
        out_specs=VMEM,
        scratch_shapes=[pltpu.SemaphoreType.DMA((1,))],
        compiler_params=params(4),
        name="prepare",
    )(leave(inv_mix))

    def early(slab):
        return pl.pallas_call(
            early_kernel,
            out_shape=partial_shape,
            in_specs=[SMEM] + [VMEM] * 2,
            out_specs=VMEM,
            compiler_params=params(4),
            cost_estimate=cost(0, 3 * MIB),
            name="early",
        )(place, slab, keep(inverse))

    def gather(slabs, shapes):
        return pl.pallas_call(
            functools.partial(gather_kernel, depth, scale),
            out_shape=shapes,
            in_specs=[SMEM] + [VMEM] * depth,
            out_specs=[VMEM] * len(shapes),
            compiler_params=params(4),
            name="gather",
        )(place, *slabs)

    def move_far(far, total, shapes, *behind):
        return pl.pallas_call(
            functools.partial(far_kernel, len(behind)),
            out_shape=shapes,
            in_specs=[SMEM] * 2 + [VMEM] * (4 + len(behind)),
            out_specs=[VMEM] * len(shapes),
            scratch_shapes=[
                pltpu.VMEM((blocks + 1,) + block_shape[1:], jnp.bfloat16),
                pltpu.VMEM(block_shape, jnp.float32),
            ],
            compiler_params=params(4),
            cost_estimate=cost(0, 8 * MIB),
            name="far",
        )(place, entries, keep(held), keep(far), keep(total), keep(count), *behind)

    near_scratch = pltpu.VMEM((3 * blocks + 1,) + block_shape[1:], jnp.bfloat16)
    scratch = [
        near_scratch,
        pltpu.VMEM((levels, cols), jnp.float32),
        pltpu.VMEM((levels, tracers, cols), jnp.bfloat16),
        pltpu.SemaphoreType.DMA((2,)),
    ]
    block_array = jax.ShapeDtypeStruct(block_shape, jnp.bfloat16)

    partial = early(slabs[0])
    one_sens, three_sens = slabs[1], slabs[3]
    mixed = pl.pallas_call(
        functools.partial(mix_kernel, 1),
        out_shape=[slab] * (depth - 1) + [several(2)],
        in_specs=[SMEM] + [VMEM] * (depth + 2),
        out_specs=[VMEM] * depth,
        scratch_shapes=[mixed_scratch],
        compiler_params=params(4),
        name="mix",
    )(place, *slabs[1:], keep(inverse), keep(partial), later_sens)
    slabs = exchange(mixed, "depth")
    pair, neighbours, _ = lax.optimization_barrier((pair, neighbours, mixed))
    entries, pair, count = pl.pallas_call(
        functools.partial(list_kernel, total_blocks),
        out_shape=[
            jax.ShapeDtypeStruct((3, 128), jnp.int32),
            jax.ShapeDtypeStruct(pair.shape, pair.dtype),
            jax.ShapeDtypeStruct(count.shape, count.dtype),
        ],
        in_specs=[SMEM, SMEM, VMEM, VMEM],
        out_specs=[SMEM, VMEM, VMEM],
        compiler_params=params(4),
        name="list",
    )(place, neighbours, pair, count)
    slabs, entries, pair = lax.optimization_barrier((slabs, entries, pair))
    (own,) = gather(slabs, [block_array])
    mate = lax.ppermute(own, "horiz", swap)
    far = lax.ppermute(own, "horiz", cross)
    held, total = pl.pallas_call(
        functools.partial(near_kernel, True),
        out_shape=[
            pltpu.VMEM((blocks * slots, levels, 128, 128), jnp.bfloat16),
            total_shape,
        ],
        in_specs=[SMEM, SMEM, HBM, VMEM, VMEM, HBM, HBM, VMEM],
        out_specs=[VMEM, VMEM],
        scratch_shapes=scratch + [pltpu.SemaphoreType.DMA((blocks * slots,))],
        compiler_params=params(4),
        cost_estimate=cost(0, 16 * MIB),
        name="near_load",
    )(place, entries, leave(transport), keep(own), keep(mate), leave(state), leave(rates), pair)
    shapes = [whole] + [slab] * (depth - 1) + [several(2)]
    first, *parts = move_far(far, total, shapes, slabs[3])

    slabs = exchange(parts, "depth")
    partial = early(slabs[0])
    terms = pl.pallas_call(
        weigh_kernel,
        out_shape=terms_shape,
        in_specs=[SMEM] + [VMEM] * 7,
        out_specs=VMEM,
        compiler_params=params(4),
        name="weigh",
    )(place, mixed[0], mixed[1], mixed[3], own_sens, one_sens, three_sens, count)
    parts = pl.pallas_call(
        mix_last_kernel,
        out_shape=[longer] * depth,
        in_specs=[SMEM] + [VMEM] * (depth + 7),
        out_specs=[VMEM] * depth,
        scratch_shapes=[mixed_scratch],
        compiler_params=params(4),
        name="mix_last",
    )(
        place, *slabs[1:], keep(inverse), keep(partial),
        own_sens, one_sens, three_sens, mixed[2], keep(count), terms,
    )
    slabs = exchange(parts, "depth")
    message_shape = jax.ShapeDtypeStruct((blocks + 1,) + block_shape[1:], jnp.bfloat16)
    own, terms, message = gather(slabs, [block_array, terms_shape, message_shape])
    mate = lax.ppermute(message, "horiz", swap)
    far = lax.ppermute(own, "horiz", cross)

    def add_pairs(terms, flip):
        return terms + lax.ppermute(terms, "horiz", [(i, i ^ flip) for i in range(horiz)])

    terms = terms + (mate[blocks, 0].astype(jnp.float32) + mate[blocks, 1].astype(jnp.float32))
    terms, own, mate = lax.optimization_barrier((terms, own, mate))
    total = pl.pallas_call(
        functools.partial(near_kernel, False),
        out_shape=total_shape,
        in_specs=[SMEM, SMEM, VMEM, VMEM, VMEM, HBM, HBM, VMEM],
        out_specs=VMEM,
        scratch_shapes=scratch,
        compiler_params=params(4),
        cost_estimate=cost(0, 10 * MIB),
        name="near",
    )(place, entries, keep(held), keep(own), keep(mate), leave(first), leave(rates), pair)
    terms = add_pairs(terms, 7)
    terms, total = lax.optimization_barrier((terms, total))
    total = pl.pallas_call(
        rest_kernel,
        out_shape=total_shape,
        in_specs=[SMEM, SMEM] + [VMEM] * 4,
        out_specs=VMEM,
        scratch_shapes=[near_scratch],
        compiler_params=params(4),
        cost_estimate=cost(0, 10 * MIB),
        name="rest",
    )(place, entries, keep(held), keep(own), keep(mate), keep(total))
    terms = add_pairs(terms, 25)
    terms, total = lax.optimization_barrier((terms, total))
    (second,) = move_far(far, total, [whole])
    terms = add_pairs(terms, 9)
    terms, second = lax.optimization_barrier((terms, second))
    terms = add_pairs(terms, 3)
    gradient = terms[:, 0]
    return (jnp.transpose(first, (1, 0, 2)), jnp.transpose(second, (1, 0, 2)), gradient)


def solution(mesh):
    return jax.shard_map(
        per_device,
        mesh=mesh,
        in_specs=(
            P(None, "depth", "horiz"),
            P("depth", "horiz", None, None, None),
            P("horiz", None),
            P(None, None, ("horiz", "depth")),
            P("depth", "horiz"),
            P(),
            P(None, "depth", "horiz"),
            P("horiz"),
        ),
        out_specs=(P(None, "depth", "horiz"), P(None, "depth", "horiz"), P()),
        check_vma=False,
    )
```

time: 101 us -> 87.6 us (0.87)
  waiting for transfers between devices: 30.1 us -> 16.9 us
  starting transfers between devices: 31 us -> 33.4 us
  local copies, waits for them, and re-layouts: 3.75 us -> 1.37 us
    ppermute x5, starting transfers between devices: 2.18 us -> 14 us  [the longest x1 8.99 us: per_device(): mate = lax.ppermute(message, 'horiz', swap)]
    ppermute x5, waiting for transfers between devices: 15.1 us -> 6.26 us  [the longest x4 4.84 us: add_pairs(): lax.ppermute(terms, 'horiz', [(i, i ^ flip) for i in range(horiz)])]
    ppermute x2 -> x1, starting transfers between devices: 10.7 us -> 3.74 us  [per_device(): mate = lax.ppermute(own, 'horiz', swap)]
    ppermute x12, waiting for transfers between devices: 14.9 us -> 10.5 us  [exchange(): lax.ppermute(parts[s], axis, ring(count, s))]
    pallas_call x8 -> x13, Pallas kernels: 20 us -> 23.9 us  [the longest x2 6.41 us: move_far(): pl.pallas_call(functools.partial(far_kernel, len(behind)), out_shape=shap...]
    pallas_call x1, Pallas kernels: 5.99 us -> 2.8 us  [per_device(): pl.pallas_call(functools.partial(near_kernel, False), out_shape=total_sha...]
    ppermute x12, starting transfers between devices: 17.1 us -> 14.4 us  [exchange(): lax.ppermute(parts[s], axis, ring(count, s))]
    unnamed x13 -> x4, local copies, waits for them, and re-layouts: 3.75 us -> 1.37 us
  transfers between devices with their start and end apart: 21 -> 20, of which waited for: 15 -> 11; matrix products, arithmetic and copies ran while one was open for 2% -> 1% of each run, Pallas kernels for 19% -> 25%
where the time goes in v2:
time: 87.6 us; the launch traced here: 87.3 us
  Pallas kernels  33.4 us (38%)
  starting transfers between devices  33.4 us (38%)
  waiting for transfers between devices  16.9 us (19%)
  other arithmetic  1.5 us (2%)
  local copies, waits for them, and re-layouts  1.37 us (2%)
    ppermute x12, starting transfers between devices, exchange(): lax.ppermute(parts[s], axis, ring(count, s))  14.4 us
    ppermute x12, waiting for transfers between devices, exchange(): lax.ppermute(parts[s], axis, ring(count, s))  10.5 us
    ppermute x1, starting transfers between devices, per_device(): mate = lax.ppermute(message, 'horiz', swap)  8.99 us
    pallas_call x1, Pallas kernels, per_device(): pl.pallas_call(functools.partial(near_kernel, True), out_shape=[pltpu.VME...  6.66 us
    pallas_call x2, Pallas kernels, move_far(): pl.pallas_call(functools.partial(far_kernel, len(behind)), out_shape=shap...  6.41 us
    ppermute x4, starting transfers between devices, add_pairs(): lax.ppermute(terms, 'horiz', [(i, i ^ flip) for i in range(horiz)])  5.04 us
    ppermute x4, waiting for transfers between devices, add_pairs(): lax.ppermute(terms, 'horiz', [(i, i ^ flip) for i in range(horiz)])  4.84 us
    ppermute x1, starting transfers between devices, per_device(): mate = lax.ppermute(own, 'horiz', swap)  3.74 us
  transfers between devices with their start and end apart: 20, of which 11 were waited for; matrix products, arithmetic and copies ran while one was open for 1% of the time, Pallas kernels for 25%

profile of v2, /device:TPU:1, one launch (start us, length us, event | category | flops | bytes accessed | tf_op | source)
XLA Modules:
  0.0 87.3 jit_solution(449476509028810145)
XLA Ops:
  0.7 1.7 %split.1 = (bf16[24,16,256]{2,1,0:T(8,128)(2,1)S(1)}, bf16[12,16,256]{2,1,0:T(8,128)(2,1)S(1)}, bf16[24,16,256]{2,1,0:T(8,128)(2,1)S(1)}, bf16[12,16,256]{2,1,0:...) custom-call(s32[3]{0:T(128)S(1)} %pad_add_fusion.place, ...), custom_call_target="tpu_custom_call" | custom-call | tf_op jit(solution)/shard_map/split/pallas_call | solution.py:406
  2.4 2.2 %collective-permute-start = (bf16[24,16,256]{2,1,0:T(8,128)(2,1)S(1)}, bf16[24,16,256]{2,1,0:T(8,128)(2,1)S(1)}, u32[]{:S(2)}, u32[]{:S(2)}) collective-permute-start(bf16[24,16,256]{2,1,0:T(8,128)(2,1)S(1)} %get-tuple-element.47), channel_id=1, source_target_pairs={{0,1},{1,2},{2,3},{3,0},{4,5},{5,6},{6,7},{7,4},{8,9},{9,10},{10,1... | collective-permute-start | bytes 589832 | tf_op jit(solution)/shard_map/ppermute | solution.py:354
  4.6 1.5 %collective-permute-start.2 = (bf16[24,16,256]{2,1,0:T(8,128)(2,1)S(1)}, bf16[24,16,256]{2,1,0:T(8,128)(2,1)S(1)}, u32[]{:S(2)}, u32[]{:S(2)}) collective-permute-start(bf16[24,16,256]{2,1,0:T(8,128)(2,1)S(1)} %get-tuple-element.49), channel_id=1, source_target_pairs={{0,3},{1,0},{2,1},{3,2},{4,7},{5,4},{6,5},{7,6},{8,11},{9,8},{10,9... | collective-permute-start | bytes 589832 | tf_op jit(solution)/shard_map/ppermute | solution.py:354
  6.2 1.6 %collective-permute-start.1 = (bf16[12,16,256]{2,1,0:T(8,128)(2,1)S(1)}, bf16[12,16,256]{2,1,0:T(8,128)(2,1)S(1)}, u32[]{:S(2)}, u32[]{:S(2)}) collective-permute-start(bf16[12,16,256]{2,1,0:T(8,128)(2,1)S(1)} %get-tuple-element.48), channel_id=1, source_target_pairs={{0,2},{1,3},{2,0},{3,1},{4,6},{5,7},{6,4},{7,5},{8,10},{9,11},{10,... | collective-permute-start | bytes 294920 | tf_op jit(solution)/shard_map/ppermute | solution.py:354
  7.7 1.7 %prepare.1.inverse.refs_3_ = f32[48,48,256]{2,1,0:T(8,128)S(1)} custom-call(f32[48,48,256]{2,1,0:T(8,128)} %inverse.1), custom_call_target="tpu_custom_call" | custom-call | tf_op jit(solution)/shard_map/prepare/pallas_call | solution.py:419
  9.4 1.2 %early.2.refs_4_ = f32[4,12,16,256]{3,2,1,0:T(8,128)S(1)} custom-call(s32[3]{0:T(128)S(1)} %pad_add_fusion.place, bf16[12,16,256]{2,1,0:T(8,128)(2,1)S(1)} %get-tuple-element.50.slab, f32[48,48,256]{2,1,0:T(8,128)S(1)} %prepare.1.inverse.refs_3_), custom_call_target="tpu_custom_call" | custom-call | bytes 3145728 | tf_op jit(solution)/shard_map/early/pallas_call | solution.py:430
  10.6 2.8 %collective-permute-done.1.refs_1_ = bf16[12,16,256]{2,1,0:T(8,128)(2,1)S(1)} collective-permute-done((bf16[12,16,256]{2,1,0:T(8,128)(2,1)S(1)}, bf16[12,16,256]{2,1,0:T(8,128)(2,1)S(1)}, u32[]{:S(2)}, u32[]{:S(2)}) %collective-permute-start.1) | collective-permute-done | bytes 98336 | tf_op jit(solution)/shard_map/ppermute | solution.py:354
  13.4 2.5 %mix.1 = (bf16[12,16,256]{2,1,0:T(8,128)(2,1)S(1)}, bf16[12,16,256]{2,1,0:T(8,128)(2,1)S(1)}, bf16[12,16,256]{2,1,0:T(8,128)(2,1)S(1)}, bf16[24,16,256]{2,1,0:T(8,128)(2,1)S(1)}) custom-call(s32[3]{0:T(128)S(1)} %pad_add_fusion.place, bf16[24,16,256]{2,1,0:T(8,128)(2,1)S(1)} %collective-permute-done.refs_0_.refs_4_.refs_6_, ...), custom_call_target="tpu_custom_call" | custom-call | tf_op jit(solution)/shard_map/mix/pallas_call | solution.py:476
  15.9 1.0 %collective-permute-start.5 = (bf16[24,16,256]{2,1,0:T(8,128)(2,1)S(1)}, bf16[24,16,256]{2,1,0:T(8,128)(2,1)S(1)}, u32[]{:S(2)}, u32[]{:S(2)}) collective-permute-start(bf16[24,16,256]{2,1,0:T(8,128)(2,1)S(1)} %get-tuple-element.55.refs_2_), channel_id=1, source_target_pairs={{0,3},{1,0},{2,1},{3,2},{4,7},{5,4},{6,5},{7,6},{8,11},{9,8},{10,9... | collective-permute-start | bytes 589832 | tf_op jit(solution)/shard_map/ppermute | solution.py:354
  18.2 0.9 collective-permute-start.4
  20.5 1.6 %list.1 = (s32[3,128]{1,0:T(4,128)S(1)}, bf16[16,32]{1,0:T(8,128)(2,1)S(1)}, s32[1,1024]{1,0:T(1,128)S(1)}) custom-call(s32[3]{0:T(128)S(1)} %pad_add_fusion.place, s32[8,5]{1,0:T(8,128)S(1)} %copy-done, bf16[16,32]{1,0:T(8,128)(2,1)S(1)} %pad_maximum_fusion.pair, s32[1,1024]{1,0:T(1,128)S(1)} %bitcast.10), custom_call_target="tpu_custom_call" | custom-call | tf_op jit(solution)/shard_map/list/pallas_call | solution.py:487
  22.1 1.0 %collective-permute-done.3.refs_1_ = bf16[12,16,256]{2,1,0:T(8,128)(2,1)S(1)} collective-permute-done((bf16[12,16,256]{2,1,0:T(8,128)(2,1)S(1)}, bf16[12,16,256]{2,1,0:T(8,128)(2,1)S(1)}, u32[]{:S(2)}, u32[]{:S(2)}) %collective-permute-start.3) | collective-permute-done | bytes 98336 | tf_op jit(solution)/shard_map/ppermute | solution.py:354
  24.2 3.7 %collective-permute-start.6 = (bf16[8,12,16,128]{3,2,1,0:T(8,128)(2,1)S(1)}, bf16[8,12,16,128]{3,2,1,0:T(8,128)(2,1)S(1)}, u32[]{:S(2)}, u32[]{:S(2)}) collective-permute-start(bf16[8,12,16,128]{3,2,1,0:T(8,128)(2,1)S(1)} %gather.2.own), channel_id=1, source_target_pairs={{0,4},{4,0},{8,12},{12,8},{16,20},{20,16},{24,28},{28,24},{32,36},... | collective-permute-start | bytes 1179656 | tf_op jit(solution)/shard_map/ppermute | solution.py:501
  28.0 1.2 %collective-permute-start.7 = (bf16[8,12,16,128]{3,2,1,0:T(8,128)(2,1)S(1)}, bf16[8,12,16,128]{3,2,1,0:T(8,128)(2,1)S(1)}, u32[]{:S(2)}, u32[]{:S(2)}) collective-permute-start(bf16[8,12,16,128]{3,2,1,0:T(8,128)(2,1)S(1)} %gather.2.own), channel_id=1, source_target_pairs={{4,8},{8,4},{12,16},{16,12},{20,24},{24,20},{28,32},{32,28},{36,40... | collective-permute-start | bytes 1179656 | tf_op jit(solution)/shard_map/ppermute | solution.py:502
  29.3 6.7 %near_load.1 = (bf16[40,12,128,128]{3,2,1,0:T(8,128)(2,1)S(1)}, f32[8,12,16,128]{3,2,1,0:T(8,128)S(1)}) custom-call(s32[3]{0:T(128)S(1)} %pad_add_fusion.place, s32[3,128]{1,0:T(4,128)S(1)} %get-tuple-element.60.entries, bf16[12,8,5,128,128]{4,3,2,1,0:T(8,128)(2,1)} %weights.1, bf16[8,12,16,128]{3,2,1,0:T(8,128)(2,1)S(1)} %gather.2.own, ...), custom_call_target="tpu_custom_call" | custom-call | bytes 16777216 | tf_op jit(solution)/shard_map/near_load/pallas_call | solution.py:503
  36.0 3.2 %far.2 = (bf16[12,16,1024]{2,1,0:T(8,128)(2,1)}, bf16[12,16,256]{2,1,0:T(8,128)(2,1)S(1)}, bf16[12,16,256]{2,1,0:T(8,128)(2,1)S(1)}, bf16[12,16,256]{2,1,0:T(8,128)(2,1)S(1)}, bf16[24,16,256]{2,1,0:T(8,128)(2,1)S(1)}) custom-call(s32[3]{0:T(128)S(1)} %pad_add_fusion.place, s32[3,128]{1,0:T(4,128)S(1)} %get-tuple-element.60.entries, ...), custom_call_target="tpu_custom_call" | custom-call | bytes 8388608 | tf_op jit(solution)/shard_map/far/pallas_call | solution.py:451
  39.2 2.2 %collective-permute-start.10 = (bf16[24,16,256]{2,1,0:T(8,128)(2,1)S(1)}, bf16[24,16,256]{2,1,0:T(8,128)(2,1)S(1)}, u32[]{:S(2)}, u32[]{:S(2)}) collective-permute-start(bf16[24,16,256]{2,1,0:T(8,128)(2,1)S(1)} %get-tuple-element.72), channel_id=1, source_target_pairs={{0,3},{1,0},{2,1},{3,2},{4,7},{5,4},{6,5},{7,6},{8,11},{9,8},{10,9... | collective-permute-start | bytes 589832 | tf_op jit(solution)/shard_map/ppermute | solution.py:354
  41.4 1.2 %collective-permute-start.9 = (bf16[12,16,256]{2,1,0:T(8,128)(2,1)S(1)}, bf16[12,16,256]{2,1,0:T(8,128)(2,1)S(1)}, u32[]{:S(2)}, u32[]{:S(2)}) collective-permute-start(bf16[12,16,256]{2,1,0:T(8,128)(2,1)S(1)} %get-tuple-element.71), channel_id=1, source_target_pairs={{0,2},{1,3},{2,0},{3,1},{4,6},{5,7},{6,4},{7,5},{8,10},{9,11},{10,... | collective-permute-start | bytes 294920 | tf_op jit(solution)/shard_map/ppermute | solution.py:354
  43.3 1.2 %early.3.refs_4_ = f32[4,12,16,256]{3,2,1,0:T(8,128)S(1)} custom-call(s32[3]{0:T(128)S(1)} %pad_add_fusion.place, bf16[12,16,256]{2,1,0:T(8,128)(2,1)S(1)} %get-tuple-element.73.slab, f32[48,48,256]{2,1,0:T(8,128)S(1)} %prepare.1.inverse.refs_3_), custom_call_target="tpu_custom_call" | custom-call | bytes 3145728 | tf_op jit(solution)/shard_map/early/pallas_call | solution.py:430
  44.5 2.6 %collective-permute-done.8.refs_0_ = bf16[12,16,256]{2,1,0:T(8,128)(2,1)S(1)} collective-permute-done((bf16[12,16,256]{2,1,0:T(8,128)(2,1)S(1)}, bf16[12,16,256]{2,1,0:T(8,128)(2,1)S(1)}, u32[]{:S(2)}, u32[]{:S(2)}) %collective-permute-start.8) | collective-permute-done | bytes 98336 | tf_op jit(solution)/shard_map/ppermute | solution.py:354
  47.2 2.7 %mix_last.1 = (bf16[13,16,256]{2,1,0:T(8,128)(2,1)S(1)}, bf16[13,16,256]{2,1,0:T(8,128)(2,1)S(1)}, bf16[13,16,256]{2,1,0:T(8,128)(2,1)S(1)}, bf16[13,16,256]{2,1,0:T(8,128)(2,1)S(1)}) custom-call(s32[3]{0:T(128)S(1)} %pad_add_fusion.place, bf16[12,16,256]{2,1,0:T(8,128)(2,1)S(1)} %collective-permute-done.8.refs_0_, ...), custom_call_target="tpu_custom_call" | custom-call | tf_op jit(solution)/shard_map/mix_last/pallas_call | solution.py:529
  50.1 3.1 %collective-permute-start.12 = (bf16[13,16,256]{2,1,0:T(8,128)(2,1)S(1)}, bf16[13,16,256]{2,1,0:T(8,128)(2,1)S(1)}, u32[]{:S(2)}, u32[]{:S(2)}) collective-permute-start(bf16[13,16,256]{2,1,0:T(8,128)(2,1)S(1)} %get-tuple-element.77), channel_id=1, source_target_pairs={{0,2},{1,3},{2,0},{3,1},{4,6},{5,7},{6,4},{7,5},{8,10},{9,11},{10,... | collective-permute-start | bytes 319496 | tf_op jit(solution)/shard_map/ppermute | solution.py:354
  53.2 1.7 %collective-permute-done.11.refs_1_ = bf16[13,16,256]{2,1,0:T(8,128)(2,1)S(1)} collective-permute-done((bf16[13,16,256]{2,1,0:T(8,128)(2,1)S(1)}, bf16[13,16,256]{2,1,0:T(8,128)(2,1)S(1)}, u32[]{:S(2)}, u32[]{:S(2)}) %collective-permute-start.11) | collective-permute-done | bytes 106528 | tf_op jit(solution)/shard_map/ppermute | solution.py:354
  54.9 1.6 %collective-permute-done.12.refs_2_ = bf16[13,16,256]{2,1,0:T(8,128)(2,1)S(1)} collective-permute-done((bf16[13,16,256]{2,1,0:T(8,128)(2,1)S(1)}, bf16[13,16,256]{2,1,0:T(8,128)(2,1)S(1)}, u32[]{:S(2)}, u32[]{:S(2)}) %collective-permute-start.12) | collective-permute-done | bytes 106528 | tf_op jit(solution)/shard_map/ppermute | solution.py:354
  57.4 9.0 %collective-permute-start.14 = (bf16[9,12,16,128]{3,2,1,0:T(8,128)(2,1)S(1)}, bf16[9,12,16,128]{3,2,1,0:T(8,128)(2,1)S(1)}, u32[]{:S(2)}, u32[]{:S(2)}) collective-permute-start(bf16[9,12,16,128]{3,2,1,0:T(8,128)(2,1)S(1)} %get-tuple-element.80), channel_id=1, source_target_pairs={{0,4},{4,0},{8,12},{12,8},{16,20},{20,16},{24,28},{28,24},{32,36},... | collective-permute-start | bytes 1327112 | tf_op jit(solution)/shard_map/ppermute | solution.py:544
  66.4 1.4 %collective-permute-done.14.mate = bf16[9,12,16,128]{3,2,1,0:T(8,128)(2,1)S(1)} collective-permute-done((bf16[9,12,16,128]{3,2,1,0:T(8,128)(2,1)S(1)}, bf16[9,12,16,128]{3,2,1,0:T(8,128)(2,1)S(1)}, u32[]{:S(2)}, u32[]{:S(2)}) %collective-permute-start.14) | collective-permute-done | bytes 442400 | tf_op jit(solution)/shard_map/ppermute | solution.py:544
  67.9 2.8 %near.1.before = f32[8,12,16,128]{3,2,1,0:T(8,128)S(1)} custom-call(s32[3]{0:T(128)S(1)} %pad_add_fusion.place, s32[3,128]{1,0:T(4,128)S(1)} %get-tuple-element.60.entries, bf16[40,12,128,128]{3,2,1,0:T(8,128)(2,1)S(1)} %get-tuple-element.66.weights, bf16[8,12,16,128]{3,2,1,0:T(8,128)(2,1)S(1)} %get-tuple-element.83.own, ...), custom_call_target="tpu_custom_call" | custom-call | bytes 10485760 | tf_op jit(solution)/shard_map/near/pallas_call | solution.py:552
  70.7 1.8 %collective-permute-done.15 = f32[16,128]{1,0:T(8,128)S(1)} collective-permute-done((f32[16,128]{1,0:T(8,128)S(1)}, f32[16,128]{1,0:T(8,128)S(1)}, u32[]{:S(2)}, u32[]{:S(2)}) %collective-permute-start.15) | collective-permute-done | bytes 8224 | tf_op jit(solution)/shard_map/ppermute | solution.py:548
  72.4 5.0 %collective-permute-start.16 = (f32[16,128]{1,0:T(8,128)S(1)}, f32[16,128]{1,0:T(8,128)S(1)}, u32[]{:S(2)}, u32[]{:S(2)}) collective-permute-start(f32[16,128]{1,0:T(8,128)S(1)} %add.29), channel_id=1, source_target_pairs={{0,100},{4,96},{8,108},{12,104},{16,116},{20,112},{24,124},{28,120... | collective-permute-start | bytes 24584 | tf_op jit(solution)/shard_map/ppermute | solution.py:548
  77.4 2.9 %rest.1.before = f32[8,12,16,128]{3,2,1,0:T(8,128)S(1)} custom-call(s32[3]{0:T(128)S(1)} %pad_add_fusion.place, s32[3,128]{1,0:T(4,128)S(1)} %get-tuple-element.60.entries, bf16[40,12,128,128]{3,2,1,0:T(8,128)(2,1)S(1)} %get-tuple-element.66.weights, bf16[8,12,16,128]{3,2,1,0:T(8,128)(2,1)S(1)} %get-tuple-element.83.own, ...), custom_call_target="tpu_custom_call" | custom-call | bytes 10485760 | tf_op jit(solution)/shard_map/rest/pallas_call | solution.py:564
  80.4 3.2 %far.3 = bf16[12,16,1024]{2,1,0:T(8,128)(2,1)} custom-call(s32[3]{0:T(128)S(1)} %pad_add_fusion.place, s32[3,128]{1,0:T(4,128)S(1)} %get-tuple-element.60.entries, bf16[40,12,128,128]{3,2,1,0:T(8,128)(2,1)S(1)} %get-tuple-element.66.weights, bf16[8,12,16,128]{3,2,1,0:T(8,128)(2,1)S(1)} %collective-permute-done.18.far, f32[8,12,16,128]{3,2,1,0:T(8,128)S(1)} %rest.1.before, ...), custom_call_target="tpu_custom_call" | custom-call | bytes 8388608 | tf_op jit(solution)/shard_map/far/pallas_call | solution.py:451
  83.6 3.1 %collective-permute-done.19 = f32[16,128]{1,0:T(8,128)S(1)} collective-permute-done((f32[16,128]{1,0:T(8,128)S(1)}, f32[16,128]{1,0:T(8,128)S(1)}, u32[]{:S(2)}, u32[]{:S(2)}) %collective-permute-start.19) | collective-permute-done | bytes 8224 | tf_op jit(solution)/shard_map/ppermute | solution.py:548
  (35 shorter events, 6.8 us)
Async XLA Ops:
  2.4 10.9 %collective-permute-start = (bf16[24,16,256]{2,1,0:T(8,128)(2,1)S(1)}, bf16[24,16,256]{2,1,0:T(8,128)(2,1)S(1)}, u32[]{:S(2)}, u32[]{:S(2)}) collective-permute-start(bf16[24,16,256]{2,1,0:T(8,128)(2,1)S(1)} %get-tuple-element.47), channel_id=1, source_target_pairs={{0,1},{1,2},{2,3},{3,0},{4,5},{5,6},{6,7},{7,4},{8,9},{9,10},{10,1... | collective-permute-start | bytes 589832 | tf_op jit(solution)/shard_map/ppermute | solution.py:354
  4.6 8.7 %collective-permute-start.2 = (bf16[24,16,256]{2,1,0:T(8,128)(2,1)S(1)}, bf16[24,16,256]{2,1,0:T(8,128)(2,1)S(1)}, u32[]{:S(2)}, u32[]{:S(2)}) collective-permute-start(bf16[24,16,256]{2,1,0:T(8,128)(2,1)S(1)} %get-tuple-element.49), channel_id=1, source_target_pairs={{0,3},{1,0},{2,1},{3,2},{4,7},{5,4},{6,5},{7,6},{8,11},{9,8},{10,9... | collective-permute-start | bytes 589832 | tf_op jit(solution)/shard_map/ppermute | solution.py:354
  6.2 7.2 %collective-permute-start.1 = (bf16[12,16,256]{2,1,0:T(8,128)(2,1)S(1)}, bf16[12,16,256]{2,1,0:T(8,128)(2,1)S(1)}, u32[]{:S(2)}, u32[]{:S(2)}) collective-permute-start(bf16[12,16,256]{2,1,0:T(8,128)(2,1)S(1)} %get-tuple-element.48), channel_id=1, source_target_pairs={{0,2},{1,3},{2,0},{3,1},{4,6},{5,7},{6,4},{7,5},{8,10},{9,11},{10,... | collective-permute-start | bytes 294920 | tf_op jit(solution)/shard_map/ppermute | solution.py:354
  15.9 7.7 %collective-permute-start.5 = (bf16[24,16,256]{2,1,0:T(8,128)(2,1)S(1)}, bf16[24,16,256]{2,1,0:T(8,128)(2,1)S(1)}, u32[]{:S(2)}, u32[]{:S(2)}) collective-permute-start(bf16[24,16,256]{2,1,0:T(8,128)(2,1)S(1)} %get-tuple-element.55.refs_2_), channel_id=1, source_target_pairs={{0,3},{1,0},{2,1},{3,2},{4,7},{5,4},{6,5},{7,6},{8,11},{9,8},{10,9... | collective-permute-start | bytes 589832 | tf_op jit(solution)/shard_map/ppermute | solution.py:354
  17.6 5.5 %collective-permute-start.3 = (bf16[12,16,256]{2,1,0:T(8,128)(2,1)S(1)}, bf16[12,16,256]{2,1,0:T(8,128)(2,1)S(1)}, u32[]{:S(2)}, u32[]{:S(2)}) collective-permute-start(bf16[12,16,256]{2,1,0:T(8,128)(2,1)S(1)} %get-tuple-element.53.refs_1_), channel_id=1, source_target_pairs={{0,1},{1,2},{2,3},{3,0},{4,5},{5,6},{6,7},{7,4},{8,9},{9,10},{10,1... | collective-permute-start | bytes 294920 | tf_op jit(solution)/shard_map/ppermute | solution.py:354
  18.2 5.4 %collective-permute-start.4 = (bf16[12,16,256]{2,1,0:T(8,128)(2,1)S(1)}, bf16[12,16,256]{2,1,0:T(8,128)(2,1)S(1)}, u32[]{:S(2)}, u32[]{:S(2)}) collective-permute-start(bf16[12,16,256]{2,1,0:T(8,128)(2,1)S(1)} %get-tuple-element.54.refs_8_), channel_id=1, source_target_pairs={{0,2},{1,3},{2,0},{3,1},{4,6},{5,7},{6,4},{7,5},{8,10},{9,11},{10,... | collective-permute-start | bytes 294920 | tf_op jit(solution)/shard_map/ppermute | solution.py:354
  19.1 0.7 copy-start
  19.8 0.7 copy-start.1
  24.2 5.1 %collective-permute-start.6 = (bf16[8,12,16,128]{3,2,1,0:T(8,128)(2,1)S(1)}, bf16[8,12,16,128]{3,2,1,0:T(8,128)(2,1)S(1)}, u32[]{:S(2)}, u32[]{:S(2)}) collective-permute-start(bf16[8,12,16,128]{3,2,1,0:T(8,128)(2,1)S(1)} %gather.2.own), channel_id=1, source_target_pairs={{0,4},{4,0},{8,12},{12,8},{16,20},{20,16},{24,28},{28,24},{32,36},... | collective-permute-start | bytes 1179656 | tf_op jit(solution)/shard_map/ppermute | solution.py:501
  28.0 8.0 %collective-permute-start.7 = (bf16[8,12,16,128]{3,2,1,0:T(8,128)(2,1)S(1)}, bf16[8,12,16,128]{3,2,1,0:T(8,128)(2,1)S(1)}, u32[]{:S(2)}, u32[]{:S(2)}) collective-permute-start(bf16[8,12,16,128]{3,2,1,0:T(8,128)(2,1)S(1)} %gather.2.own), channel_id=1, source_target_pairs={{4,8},{8,4},{12,16},{16,12},{20,24},{24,20},{28,32},{32,28},{36,40... | collective-permute-start | bytes 1179656 | tf_op jit(solution)/shard_map/ppermute | solution.py:502
  39.2 7.9 %collective-permute-start.10 = (bf16[24,16,256]{2,1,0:T(8,128)(2,1)S(1)}, bf16[24,16,256]{2,1,0:T(8,128)(2,1)S(1)}, u32[]{:S(2)}, u32[]{:S(2)}) collective-permute-start(bf16[24,16,256]{2,1,0:T(8,128)(2,1)S(1)} %get-tuple-element.72), channel_id=1, source_target_pairs={{0,3},{1,0},{2,1},{3,2},{4,7},{5,4},{6,5},{7,6},{8,11},{9,8},{10,9... | collective-permute-start | bytes 589832 | tf_op jit(solution)/shard_map/ppermute | solution.py:354
  41.4 5.7 %collective-permute-start.8 = (bf16[12,16,256]{2,1,0:T(8,128)(2,1)S(1)}, bf16[12,16,256]{2,1,0:T(8,128)(2,1)S(1)}, u32[]{:S(2)}, u32[]{:S(2)}) collective-permute-start(bf16[12,16,256]{2,1,0:T(8,128)(2,1)S(1)} %get-tuple-element.70), channel_id=1, source_target_pairs={{0,1},{1,2},{2,3},{3,0},{4,5},{5,6},{6,7},{7,4},{8,9},{9,10},{10,1... | collective-permute-start | bytes 294920 | tf_op jit(solution)/shard_map/ppermute | solution.py:354
  41.4 5.7 %collective-permute-start.9 = (bf16[12,16,256]{2,1,0:T(8,128)(2,1)S(1)}, bf16[12,16,256]{2,1,0:T(8,128)(2,1)S(1)}, u32[]{:S(2)}, u32[]{:S(2)}) collective-permute-start(bf16[12,16,256]{2,1,0:T(8,128)(2,1)S(1)} %get-tuple-element.71), channel_id=1, source_target_pairs={{0,2},{1,3},{2,0},{3,1},{4,6},{5,7},{6,4},{7,5},{8,10},{9,11},{10,... | collective-permute-start | bytes 294920 | tf_op jit(solution)/shard_map/ppermute | solution.py:354
  49.9 5.0 %collective-permute-start.11 = (bf16[13,16,256]{2,1,0:T(8,128)(2,1)S(1)}, bf16[13,16,256]{2,1,0:T(8,128)(2,1)S(1)}, u32[]{:S(2)}, u32[]{:S(2)}) collective-permute-start(bf16[13,16,256]{2,1,0:T(8,128)(2,1)S(1)} %get-tuple-element.76), channel_id=1, source_target_pairs={{0,1},{1,2},{2,3},{3,0},{4,5},{5,6},{6,7},{7,4},{8,9},{9,10},{10,1... | collective-permute-start | bytes 319496 | tf_op jit(solution)/shard_map/ppermute | solution.py:354
  50.1 6.3 %collective-permute-start.12 = (bf16[13,16,256]{2,1,0:T(8,128)(2,1)S(1)}, bf16[13,16,256]{2,1,0:T(8,128)(2,1)S(1)}, u32[]{:S(2)}, u32[]{:S(2)}) collective-permute-start(bf16[13,16,256]{2,1,0:T(8,128)(2,1)S(1)} %get-tuple-element.77), channel_id=1, source_target_pairs={{0,2},{1,3},{2,0},{3,1},{4,6},{5,7},{6,4},{7,5},{8,10},{9,11},{10,... | collective-permute-start | bytes 319496 | tf_op jit(solution)/shard_map/ppermute | solution.py:354
  53.2 3.6 %collective-permute-start.13 = (bf16[13,16,256]{2,1,0:T(8,128)(2,1)S(1)}, bf16[13,16,256]{2,1,0:T(8,128)(2,1)S(1)}, u32[]{:S(2)}, u32[]{:S(2)}) collective-permute-start(bf16[13,16,256]{2,1,0:T(8,128)(2,1)S(1)} %get-tuple-element.78), channel_id=1, source_target_pairs={{0,3},{1,0},{2,1},{3,2},{4,7},{5,4},{6,5},{7,6},{8,11},{9,8},{10,9... | collective-permute-start | bytes 319496 | tf_op jit(solution)/shard_map/ppermute | solution.py:354
  57.4 10.4 %collective-permute-start.14 = (bf16[9,12,16,128]{3,2,1,0:T(8,128)(2,1)S(1)}, bf16[9,12,16,128]{3,2,1,0:T(8,128)(2,1)S(1)}, u32[]{:S(2)}, u32[]{:S(2)}) collective-permute-start(bf16[9,12,16,128]{3,2,1,0:T(8,128)(2,1)S(1)} %get-tuple-element.80), channel_id=1, source_target_pairs={{0,4},{4,0},{8,12},{12,8},{16,20},{20,16},{24,28},{28,24},{32,36},... | collective-permute-start | bytes 1327112 | tf_op jit(solution)/shard_map/ppermute | solution.py:544
  66.4 13.9 %collective-permute-start.18 = (bf16[8,12,16,128]{3,2,1,0:T(8,128)(2,1)S(1)}, bf16[8,12,16,128]{3,2,1,0:T(8,128)(2,1)S(1)}, u32[]{:S(2)}, u32[]{:S(2)}) collective-permute-start(bf16[8,12,16,128]{3,2,1,0:T(8,128)(2,1)S(1)} %get-tuple-element.83.own), channel_id=1, source_target_pairs={{4,8},{8,4},{12,16},{16,12},{20,24},{24,20},{28,32},{32,28},{36,40... | collective-permute-start | bytes 1179656 | tf_op jit(solution)/shard_map/ppermute | solution.py:545
  67.9 4.6 %collective-permute-start.15 = (f32[16,128]{1,0:T(8,128)S(1)}, f32[16,128]{1,0:T(8,128)S(1)}, u32[]{:S(2)}, u32[]{:S(2)}) collective-permute-start(f32[16,128]{1,0:T(8,128)S(1)} %bitcast_add_fusion), channel_id=1, source_target_pairs={{0,28},{4,24},{8,20},{12,16},{16,12},{20,8},{24,4},{28,0},{32,60},... | collective-permute-start | bytes 24584 | tf_op jit(solution)/shard_map/ppermute | solution.py:548
  72.4 7.8 %collective-permute-start.16 = (f32[16,128]{1,0:T(8,128)S(1)}, f32[16,128]{1,0:T(8,128)S(1)}, u32[]{:S(2)}, u32[]{:S(2)}) collective-permute-start(f32[16,128]{1,0:T(8,128)S(1)} %add.29), channel_id=1, source_target_pairs={{0,100},{4,96},{8,108},{12,104},{16,116},{20,112},{24,124},{28,120... | collective-permute-start | bytes 24584 | tf_op jit(solution)/shard_map/ppermute | solution.py:548
  80.3 3.3 %collective-permute-start.17 = (f32[16,128]{1,0:T(8,128)S(1)}, f32[16,128]{1,0:T(8,128)S(1)}, u32[]{:S(2)}, u32[]{:S(2)}) collective-permute-start(f32[16,128]{1,0:T(8,128)S(1)} %add.30), channel_id=1, source_target_pairs={{0,36},{4,32},{8,44},{12,40},{16,52},{20,48},{24,60},{28,56},{32,4... | collective-permute-start | bytes 24584 | tf_op jit(solution)/shard_map/ppermute | solution.py:548
  83.6 3.1 %collective-permute-start.19 = (f32[16,128]{1,0:T(8,128)S(1)}, f32[16,128]{1,0:T(8,128)S(1)}, u32[]{:S(2)}, u32[]{:S(2)}) collective-permute-start(f32[16,128]{1,0:T(8,128)S(1)} %add.31), channel_id=1, source_target_pairs={{0,12},{4,8},{8,4},{12,0},{16,28},{20,24},{24,20},{28,16},{32,44},... | collective-permute-start | bytes 24584 | tf_op jit(solution)/shard_map/ppermute | solution.py:548

commit v3 on v2

--- a/solution.py
+++ b/solution.py
@@ -12,30 +12,32 @@
 SMEM = pl.BlockSpec(memory_space=pltpu.SMEM)
 HBM = pl.BlockSpec(memory_space=pltpu.HBM)
 MIB = 1024 * 1024
+AHEAD = 3
 GROUP = 4
 
 
 def split_kernel(place, state, sens, *refs):
-    one, two, three, own, own_sens, later, held, sem = refs
+    one, two, three, own, own_sens, later_one, later_two, kept, held, sem = refs
     levels, _, width = own.shape
     depth = state.shape[2] // width
     copies = [
-        pltpu.make_async_copy(whole, held.at[i], sem.at[i])
-        for i, whole in enumerate((state, sens))
+        pltpu.make_async_copy(state, kept, sem.at[0]),
+        pltpu.make_async_copy(sens, held, sem.at[1]),
     ]
     for copy in copies:
         copy.start()
     for i, targets in enumerate(
         (
             ((own, 0, 0), (one, 0, 1), (two, 0, 2), (three, 0, 3)),
-            ((own_sens, 0, 0), (one, 1, 1), (later, 0, 2), (three, 1, 3)),
+            ((own_sens, 0, 0), (later_one, 0, 1), (later_two, 0, 2), (three, 1, 3)),
         )
     ):
         copies[i].wait()
         for part, at, s in targets:
             start = lax.rem(place[0] + s, depth) * width
-            part[at * levels : (at + 1) * levels] = held[
-                i, :, :, pl.ds(pl.multiple_of(start, width), width)
+            whole = (kept, held)[i]
+            part[at * levels : (at + 1) * levels] = whole[
+                :, :, pl.ds(pl.multiple_of(start, width), width)
             ]
 
 
@@ -55,7 +57,7 @@
             inside = source - shift
             far = jnp.where((inside >= 0) & (inside < blocks), 1, 0)
             at = jnp.where(far == 1, half + counts[1], counts[0])
-            entries[0, at] = b * slots + k
+            entries[0, at] = k
             entries[1, at] = b
             entries[2, at] = jnp.where(far == 1, inside, source)
             counts = (counts[0] + 1 - far, counts[1] + far)
@@ -70,14 +72,23 @@
     entries[2, 2 * half - 1] = counts[1]
 
 
-def prepare_kernel(inverse, held, sem):
-    copy = pltpu.make_async_copy(inverse, held, sem.at[0])
-    copy.start()
-    copy.wait()
-
-
-def list_kernel(total_blocks, place, neighbours, pair, count, entries, pair_out, count_out):
-    pair_out[...] = pair[...]
+def prepare_kernel(inverse, rates, weights, held, held_rates, held_weights, sem):
+    copies = [
+        pltpu.make_async_copy(inverse, held, sem.at[0]),
+        pltpu.make_async_copy(rates, held_rates, sem.at[1]),
+    ]
+    for b in range(AHEAD):
+        copies.append(pltpu.make_async_copy(weights.at[:, b], held_weights.at[b], sem.at[2 + b]))
+    for copy in copies:
+        copy.start()
+    for copy in copies:
+        copy.wait()
+
+
+def list_kernel(total_blocks, place, neighbours, coupling, count, entries, pair, count_out):
+    high = coupling[...].astype(jnp.bfloat16)
+    low = (coupling[...] - high.astype(jnp.float32)).astype(jnp.bfloat16)
+    pair[...] = jnp.concatenate([high, low], axis=1)
     count_out[...] = count[...]
     list_entries(place, neighbours, entries, total_blocks)
 
@@ -149,8 +160,8 @@
                 mixed[at, q, :, lanes] = totals[q].astype(jnp.bfloat16)
     for s in range(depth):
         parts[s][:levels] = mixed[s]
-    if number:
-        parts[depth - 1][levels:] = refs[depth + 1][...]
+    for i in range(number):
+        parts[2 * i + 1][levels:] = refs[depth + 1 + i][...]
 
 
 def mix_last_kernel(place, *refs):
@@ -202,16 +213,20 @@
     zero = jnp.zeros(near.shape[2:], jnp.bfloat16)
     tracers = zero.shape[0]
 
-    def step(i, _):
+    def step(i, loaded):
         if ready is not None:
-            for g in range(GROUP):
-                ready(start + i * GROUP + g)
+            last = entries[1, start + i * GROUP]
+            for g in range(1, GROUP):
+                last = jnp.maximum(last, entries[1, start + i * GROUP + g])
+            loaded = ready(last + 1, loaded)
         found = []
         for g in range(GROUP):
             at = start + i * GROUP + g
-            entry, block, source = entries[0, at], entries[1, at], entries[2, at]
+            slot, block, source = entries[0, at], entries[1, at], entries[2, at]
             for l in range(0, levels, 2):
-                lhs = jnp.concatenate([weights[entry, l], weights[entry, l + 1]], axis=1)
+                lhs = jnp.concatenate(
+                    [weights[block, l, slot], weights[block, l + 1, slot]], axis=1
+                )
                 rhs = jnp.concatenate(
                     [
                         jnp.concatenate([near[source, l], zero], axis=1),
@@ -229,62 +244,48 @@
             moved = moved if g % 2 else moved.T
             total[block, l] += moved[:tracers]
             total[block, l + 1] += moved[tracers:]
-        return 0
-
-    lax.fori_loop(0, steps, step, 0)
+        return loaded
+
+    return lax.fori_loop(0, steps, step, jnp.int32(AHEAD))
 
 
 def near_kernel(load, place, entries, weights, own, mate, state, rates, coupling, *refs):
     if load:
-        held, total, near, rates_in, state_in, extra, sem = refs
+        _, held, total, near, sem = refs
+        state_in = state
     else:
-        total, near, rates_in, state_in, extra = refs
+        total, near, state_in, extra = refs
         held = weights
     blocks, levels, tracers, _ = own.shape
     odd = place[1]
     half = entries.shape[1] // 2
-    more = [
-        pltpu.make_async_copy(rates, rates_in, extra.at[0]),
-        pltpu.make_async_copy(state, state_in, extra.at[1]),
-    ]
-    for copy in more:
+    if not load:
+        copy = pltpu.make_async_copy(state, state_in, extra.at[0])
         copy.start()
 
     ready = None
     if load:
-        slots = weights.shape[2]
-
-        def fetch(at):
-            entry, block = entries[0, at], entries[1, at]
-            return pltpu.make_async_copy(
-                weights.at[:, block, entry - block * slots],
-                held.at[entry],
-                sem.at[entry],
-            )
-
-        def begin(at, _):
-            fetch(at).start()
-            return 0
-
-        def finish(at, _):
-            fetch(at).wait()
-            return 0
-
-        lax.fori_loop(0, entries[2, half - 1], begin, 0)
-        lax.fori_loop(half, half + entries[2, 2 * half - 1], begin, 0)
-
-        def ready(at):
-            @pl.when(at < entries[2, half - 1])
-            def _():
-                fetch(at).wait()
+
+        def fetch(b):
+            return pltpu.make_async_copy(weights.at[:, b], held.at[b], sem.at[b])
+
+        def ready(needed, loaded):
+            def finish(b, _):
+                fetch(b).wait()
+                return 0
+
+            needed = jnp.maximum(needed, loaded)
+            lax.fori_loop(loaded, needed, finish, 0)
+            return needed
+
+        for b in range(AHEAD, blocks):
+            fetch(b).start()
 
     near[pl.ds(blocks, blocks)] = own[...]
     near[pl.ds((1 - odd) * 2 * blocks, blocks)] = mate[:blocks]
     near[3 * blocks] = jnp.zeros(near.shape[1:], near.dtype)
 
     def add_source():
-        for copy in more:
-            copy.wait()
         for b in range(blocks):
             lanes = slice(b * 128, (b + 1) * 128)
             values = jnp.concatenate([own[b, l] for l in range(levels)], axis=1)
@@ -293,7 +294,7 @@
             )
             both = both[:tracers] + both[tracers:]
             for l in range(levels):
-                source = rates_in[l : l + 1, lanes] * both[:, l * 128 : (l + 1) * 128]
+                source = rates[l : l + 1, lanes] * both[:, l * 128 : (l + 1) * 128]
                 total[b, l] += source - state_in[l, :, lanes].astype(jnp.float32)
 
     total[...] = jnp.zeros(total.shape, total.dtype)
@@ -301,15 +302,16 @@
         add_source()
     steps = entries[0, 2 * half - 1]
     if not load:
-        steps = lax.div(steps, 2)
-    add_entries(entries, 0, steps, held, near, total, ready)
+        steps = lax.div(steps, 3)
+    loaded = add_entries(entries, 0, steps, held, near, total, ready)
     if not load:
+        copy.wait()
         add_source()
     if load:
-        lax.fori_loop(half, half + entries[2, 2 * half - 1], finish, 0)
-
-
-def rest_kernel(place, entries, weights, own, mate, before, total, near):
+        ready(blocks, loaded)
+
+
+def rest_kernel(third, place, entries, weights, own, mate, before, total, near):
     blocks = own.shape[0]
     half = entries.shape[1] // 2
     near[pl.ds(blocks, blocks)] = own[...]
@@ -317,24 +319,29 @@
     near[3 * blocks] = jnp.zeros(near.shape[1:], near.dtype)
     total[...] = before[...]
     steps = entries[0, 2 * half - 1]
-    done = lax.div(steps, 2)
-    add_entries(entries, done * GROUP, steps - done, weights, near, total)
+    start, stop = lax.div(third * steps, 3), lax.div((third + 1) * steps, 3)
+    add_entries(entries, start * GROUP, stop - start, weights, near, total)
 
 
 def far_kernel(more, place, entries, weights, far, before, count, *refs):
-    behind, new, parts, (near, total) = refs[:more], refs[more], refs[more + 1 : -2], refs[-2:]
+    behind, out, parts = refs[:more], refs[more], refs[more + 1 : -4]
+    near, total, new, sem = refs[-4:]
     blocks, levels, tracers, _ = far.shape
     half = entries.shape[1] // 2
     near[pl.ds(0, blocks)] = far[...]
     near[blocks] = jnp.zeros(near.shape[1:], near.dtype)
     total[...] = before[...]
     add_entries(entries, half, entries[1, 2 * half - 1], weights, near, total)
+    copies = []
     for b in range(blocks):
         lanes = slice(b * 128, (b + 1) * 128)
         wet_levels = count[:, lanes] - place[0] * levels
         for l in range(levels):
             value = jnp.where(wet_levels > l, total[b, l], 0.0)
             new[l, :, lanes] = value.astype(jnp.bfloat16)
+        here = pl.ds(b * 128, 128)
+        copies.append(pltpu.make_async_copy(new.at[:, :, here], out.at[:, :, here], sem.at[b]))
+        copies[-1].start()
     depth = len(parts)
     for s in range(depth):
         width = parts[s].shape[2]
@@ -342,6 +349,8 @@
         parts[s][:levels] = new[:, :, pl.ds(pl.multiple_of(start, width), width)]
     for passed_on in behind:
         parts[depth - 1][levels:] = passed_on[levels:]
+    for copy in copies:
+        copy.wait()
 
 
 def ring(count, shift):
@@ -375,8 +384,6 @@
     state = jnp.transpose(adjoint_seed, (1, 0, 2))
     sens = jnp.transpose(sensitivity, (1, 0, 2))
     count = depth_count.reshape(1, cols)
-    high = lax.reduce_precision(coupling, 8, 7)
-    pair = jnp.concatenate([high, coupling - high], axis=1).astype(jnp.bfloat16)
     scale = 1.0 / math.sqrt(levels * depth * total_blocks * 128)
 
     width = cols // depth
@@ -403,28 +410,33 @@
     def several(number):
         return jax.ShapeDtypeStruct((number * levels, tracers, width), jnp.bfloat16)
 
-    *messages, own_state, own_sens, later_sens = pl.pallas_call(
+    *messages, own_state, own_sens, one_later, two_later, kept_state = pl.pallas_call(
         split_kernel,
-        out_shape=[several(number) for number in (2, 1, 2, 1, 1, 1)],
+        out_shape=[several(number) for number in (1, 1, 2, 1, 1, 1, 1)]
+        + [pltpu.VMEM(whole.shape, jnp.bfloat16)],
         in_specs=[SMEM, HBM, HBM],
-        out_specs=[VMEM] * 6,
+        out_specs=[VMEM] * 8,
         scratch_shapes=[
-            pltpu.VMEM((2,) + whole.shape, jnp.bfloat16),
+            pltpu.VMEM(whole.shape, jnp.bfloat16),
             pltpu.SemaphoreType.DMA((2,)),
         ],
         compiler_params=params(8),
         name="split",
     )(place, leave(state), leave(sens))
     slabs = exchange([own_state] + messages, "depth")
-    inverse = pl.pallas_call(
+    inverse, rates, held = pl.pallas_call(
         prepare_kernel,
-        out_shape=pltpu.VMEM(inv_mix.shape, jnp.float32),
-        in_specs=[HBM],
-        out_specs=VMEM,
-        scratch_shapes=[pltpu.SemaphoreType.DMA((1,))],
+        out_shape=[
+            pltpu.VMEM(inv_mix.shape, jnp.float32),
+            pltpu.VMEM(rates.shape, jnp.float32),
+            pltpu.VMEM((blocks, levels, slots, 128, 128), jnp.bfloat16),
+        ],
+        in_specs=[HBM] * 3,
+        out_specs=[VMEM] * 3,
+        scratch_shapes=[pltpu.SemaphoreType.DMA((2 + AHEAD,))],
         compiler_params=params(4),
         name="prepare",
-    )(leave(inv_mix))
+    )(leave(inv_mix), leave(rates), leave(transport))
 
     def early(slab):
         return pl.pallas_call(
@@ -452,10 +464,12 @@
             functools.partial(far_kernel, len(behind)),
             out_shape=shapes,
             in_specs=[SMEM] * 2 + [VMEM] * (4 + len(behind)),
-            out_specs=[VMEM] * len(shapes),
+            out_specs=[HBM] + [VMEM] * (len(shapes) - 1),
             scratch_shapes=[
                 pltpu.VMEM((blocks + 1,) + block_shape[1:], jnp.bfloat16),
                 pltpu.VMEM(block_shape, jnp.float32),
+                pltpu.VMEM(whole.shape, jnp.bfloat16),
+                pltpu.SemaphoreType.DMA((blocks,)),
             ],
             compiler_params=params(4),
             cost_estimate=cost(0, 8 * MIB),
@@ -463,39 +477,34 @@
         )(place, entries, keep(held), keep(far), keep(total), keep(count), *behind)
 
     near_scratch = pltpu.VMEM((3 * blocks + 1,) + block_shape[1:], jnp.bfloat16)
-    scratch = [
-        near_scratch,
-        pltpu.VMEM((levels, cols), jnp.float32),
-        pltpu.VMEM((levels, tracers, cols), jnp.bfloat16),
-        pltpu.SemaphoreType.DMA((2,)),
-    ]
     block_array = jax.ShapeDtypeStruct(block_shape, jnp.bfloat16)
 
     partial = early(slabs[0])
-    one_sens, three_sens = slabs[1], slabs[3]
+    three_sens = slabs[3]
     mixed = pl.pallas_call(
-        functools.partial(mix_kernel, 1),
-        out_shape=[slab] * (depth - 1) + [several(2)],
-        in_specs=[SMEM] + [VMEM] * (depth + 2),
+        functools.partial(mix_kernel, 2),
+        out_shape=[several(number) for number in (1, 2, 1, 2)],
+        in_specs=[SMEM] + [VMEM] * (depth + 3),
         out_specs=[VMEM] * depth,
         scratch_shapes=[mixed_scratch],
         compiler_params=params(4),
         name="mix",
-    )(place, *slabs[1:], keep(inverse), keep(partial), later_sens)
+    )(place, *slabs[1:], keep(inverse), keep(partial), one_later, two_later)
     slabs = exchange(mixed, "depth")
-    pair, neighbours, _ = lax.optimization_barrier((pair, neighbours, mixed))
+    one_sens = slabs[1]
+    coupling, neighbours, _ = lax.optimization_barrier((coupling, neighbours, mixed))
     entries, pair, count = pl.pallas_call(
         functools.partial(list_kernel, total_blocks),
         out_shape=[
             jax.ShapeDtypeStruct((3, 128), jnp.int32),
-            jax.ShapeDtypeStruct(pair.shape, pair.dtype),
+            jax.ShapeDtypeStruct((tracers, 2 * tracers), jnp.bfloat16),
             jax.ShapeDtypeStruct(count.shape, count.dtype),
         ],
         in_specs=[SMEM, SMEM, VMEM, VMEM],
         out_specs=[SMEM, VMEM, VMEM],
         compiler_params=params(4),
         name="list",
-    )(place, neighbours, pair, count)
+    )(place, neighbours, coupling, count)
     slabs, entries, pair = lax.optimization_barrier((slabs, entries, pair))
     (own,) = gather(slabs, [block_array])
     mate = lax.ppermute(own, "horiz", swap)
@@ -503,16 +512,20 @@
     held, total = pl.pallas_call(
         functools.partial(near_kernel, True),
         out_shape=[
-            pltpu.VMEM((blocks * slots, levels, 128, 128), jnp.bfloat16),
+            pltpu.VMEM((blocks, levels, slots, 128, 128), jnp.bfloat16),
             total_shape,
         ],
-        in_specs=[SMEM, SMEM, HBM, VMEM, VMEM, HBM, HBM, VMEM],
+        in_specs=[SMEM, SMEM, HBM] + [VMEM] * 6,
         out_specs=[VMEM, VMEM],
-        scratch_shapes=scratch + [pltpu.SemaphoreType.DMA((blocks * slots,))],
+        input_output_aliases={8: 0},
+        scratch_shapes=[near_scratch, pltpu.SemaphoreType.DMA((blocks,))],
         compiler_params=params(4),
         cost_estimate=cost(0, 16 * MIB),
         name="near_load",
-    )(place, entries, leave(transport), keep(own), keep(mate), leave(state), leave(rates), pair)
+    )(
+        place, entries, leave(transport), keep(own), keep(mate),
+        keep(kept_state), keep(rates), pair, keep(held),
+    )
     shapes = [whole] + [slab] * (depth - 1) + [several(2)]
     first, *parts = move_far(far, total, shapes, slabs[3])
 
@@ -552,30 +565,33 @@
     total = pl.pallas_call(
         functools.partial(near_kernel, False),
         out_shape=total_shape,
-        in_specs=[SMEM, SMEM, VMEM, VMEM, VMEM, HBM, HBM, VMEM],
+        in_specs=[SMEM, SMEM, VMEM, VMEM, VMEM, HBM, VMEM, VMEM],
         out_specs=VMEM,
-        scratch_shapes=scratch,
+        scratch_shapes=[
+            near_scratch,
+            pltpu.VMEM(whole.shape, jnp.bfloat16),
+            pltpu.SemaphoreType.DMA((1,)),
+        ],
         compiler_params=params(4),
         cost_estimate=cost(0, 10 * MIB),
         name="near",
-    )(place, entries, keep(held), keep(own), keep(mate), leave(first), leave(rates), pair)
+    )(place, entries, keep(held), keep(own), keep(mate), leave(first), keep(rates), pair)
     terms = add_pairs(terms, 7)
     terms, total = lax.optimization_barrier((terms, total))
-    total = pl.pallas_call(
-        rest_kernel,
-        out_shape=total_shape,
-        in_specs=[SMEM, SMEM] + [VMEM] * 4,
-        out_specs=VMEM,
-        scratch_shapes=[near_scratch],
-        compiler_params=params(4),
-        cost_estimate=cost(0, 10 * MIB),
-        name="rest",
-    )(place, entries, keep(held), keep(own), keep(mate), keep(total))
-    terms = add_pairs(terms, 25)
-    terms, total = lax.optimization_barrier((terms, total))
+    for third, flip in ((1, 25), (2, 9)):
+        total = pl.pallas_call(
+            functools.partial(rest_kernel, third),
+            out_shape=total_shape,
+            in_specs=[SMEM, SMEM] + [VMEM] * 4,
+            out_specs=VMEM,
+            scratch_shapes=[near_scratch],
+            compiler_params=params(4),
+            cost_estimate=cost(0, 10 * MIB),
+            name="rest",
+        )(place, entries, keep(held), keep(own), keep(mate), keep(total))
+        terms = add_pairs(terms, flip)
+        terms, total = lax.optimization_barrier((terms, total))
     (second,) = move_far(far, total, [whole])
-    terms = add_pairs(terms, 9)
-    terms, second = lax.optimization_barrier((terms, second))
     terms = add_pairs(terms, 3)
     gradient = terms[:, 0]
     return (jnp.transpose(first, (1, 0, 2)), jnp.transpose(second, (1, 0, 2)), gradient)

time: 87.6 us -> 84.5 us (0.965)
  waiting for transfers between devices: 16.9 us -> 13.3 us
  Pallas kernels: 33.4 us -> 35.1 us
  local copies, waits for them, and re-layouts: 1.37 us -> 0.01 us
  starting transfers between devices: 33.4 us -> 34.4 us
    pallas_call x4 -> x5, Pallas kernels: 8.79 us -> 12.3 us  [the longest x2 4.6 us: per_device(): pl.pallas_call(functools.partial(rest_kernel, third), out_shape=total_sha...]
    ppermute x4, waiting for transfers between devices: 4.84 us -> 2.28 us  [add_pairs(): lax.ppermute(terms, 'horiz', [(i, i ^ flip) for i in range(horiz)])]
    unnamed x4 -> x6, local copies, waits for them, and re-layouts: 1.37 us -> 0.01 us
    ppermute x12, starting transfers between devices: 14.4 us -> 15.6 us  [exchange(): lax.ppermute(parts[s], axis, ring(count, s))]
    pallas_call x2, Pallas kernels: 6.41 us -> 5.17 us  [move_far(): pl.pallas_call(functools.partial(far_kernel, len(behind)), out_shape=shap...]
    ppermute x12, waiting for transfers between devices: 10.5 us -> 9.44 us  [exchange(): lax.ppermute(parts[s], axis, ring(count, s))]
  transfers between devices with their start and end apart: 20 -> 20, of which waited for: 11 -> 11; matrix products, arithmetic and copies ran while one was open for 1% -> 0% of each run, Pallas kernels for 25% -> 29%
where the time goes in v3:
time: 84.5 us; the launch traced here: 84.3 us
  Pallas kernels  35.1 us (42%)
  starting transfers between devices  34.4 us (41%)
  waiting for transfers between devices  13.3 us (16%)
    ppermute x12, starting transfers between devices, exchange(): lax.ppermute(parts[s], axis, ring(count, s))  15.6 us
    ppermute x12, waiting for transfers between devices, exchange(): lax.ppermute(parts[s], axis, ring(count, s))  9.44 us
    ppermute x1, starting transfers between devices, per_device(): mate = lax.ppermute(message, 'horiz', swap)  8.57 us
    pallas_call x1, Pallas kernels, per_device(): pl.pallas_call(functools.partial(near_kernel, True), out_shape=[pltpu.VME...  6.09 us
    ppermute x4, starting transfers between devices, add_pairs(): lax.ppermute(terms, 'horiz', [(i, i ^ flip) for i in range(horiz)])  5.78 us
    pallas_call x2, Pallas kernels, move_far(): pl.pallas_call(functools.partial(far_kernel, len(behind)), out_shape=shap...  5.17 us
    pallas_call x2, Pallas kernels, per_device(): pl.pallas_call(functools.partial(rest_kernel, third), out_shape=total_sha...  4.6 us
    pallas_call x1, Pallas kernels, per_device(): pl.pallas_call(prepare_kernel, out_shape=[pltpu.VMEM(inv_mix.shape, jnp.f...  3.48 us
  transfers between devices with their start and end apart: 20, of which 11 were waited for; matrix products, arithmetic and copies ran while one was open for 0% of the time, Pallas kernels for 29%

profile of v3, /device:TPU:1, one launch (start us, length us, event | category | flops | bytes accessed | tf_op | source)
XLA Modules:
  0.0 84.3 jit_solution(8503129872707739552)
XLA Ops:
  0.7 1.7 %split.1 = (bf16[12,16,256]{2,1,0:T(8,128)(2,1)S(1)}, bf16[12,16,256]{2,1,0:T(8,128)(2,1)S(1)}, bf16[24,16,256]{2,1,0:T(8,128)(2,1)S(1)}, bf16[12,16,256]{2,1,0:...) custom-call(s32[3]{0:T(128)S(1)} %pad_add_fusion.place, ...), custom_call_target="tpu_custom_call" | custom-call | tf_op jit(solution)/shard_map/split/pallas_call | solution.py:413
  2.5 3.6 %collective-permute-start.2 = (bf16[24,16,256]{2,1,0:T(8,128)(2,1)S(1)}, bf16[24,16,256]{2,1,0:T(8,128)(2,1)S(1)}, u32[]{:S(2)}, u32[]{:S(2)}) collective-permute-start(bf16[24,16,256]{2,1,0:T(8,128)(2,1)S(1)} %get-tuple-element.54), channel_id=1, source_target_pairs={{0,3},{1,0},{2,1},{3,2},{4,7},{5,4},{6,5},{7,6},{8,11},{9,8},{10,9... | collective-permute-start | bytes 589832 | tf_op jit(solution)/shard_map/ppermute | solution.py:363
  6.1 1.6 %collective-permute-start.1 = (bf16[12,16,256]{2,1,0:T(8,128)(2,1)S(1)}, bf16[12,16,256]{2,1,0:T(8,128)(2,1)S(1)}, u32[]{:S(2)}, u32[]{:S(2)}) collective-permute-start(bf16[12,16,256]{2,1,0:T(8,128)(2,1)S(1)} %get-tuple-element.53), channel_id=1, source_target_pairs={{0,2},{1,3},{2,0},{3,1},{4,6},{5,7},{6,4},{7,5},{8,10},{9,11},{10,... | collective-permute-start | bytes 294920 | tf_op jit(solution)/shard_map/ppermute | solution.py:363
  7.8 3.5 %prepare.1 = (f32[48,48,256]{2,1,0:T(8,128)S(1)}, f32[12,1024]{1,0:T(8,128)S(1)}, bf16[8,12,5,128,128]{4,3,2,1,0:T(8,128)(2,1)S(1)}) custom-call(f32[48,48,256]{2,1,0:T(8,128)} %inverse.1, f32[12,1024]{1,0:T(8,128)} %rates.1, bf16[12,8,5,128,128]{4,3,2,1,0:T(8,128)(2,1)} %weights.3), custom_call_target="tpu_custom_call" | custom-call | tf_op jit(solution)/shard_map/prepare/pallas_call | solution.py:427
  11.2 1.2 %early.2.refs_4_ = f32[4,12,16,256]{3,2,1,0:T(8,128)S(1)} custom-call(s32[3]{0:T(128)S(1)} %pad_add_fusion.place, bf16[12,16,256]{2,1,0:T(8,128)(2,1)S(1)} %get-tuple-element.56.slab, f32[48,48,256]{2,1,0:T(8,128)S(1)} %get-tuple-element.55.inverse.refs_3_), custom_call_target="tpu_custom_call" | custom-call | bytes 3145728 | tf_op jit(solution)/shard_map/early/pallas_call | solution.py:442
  12.5 2.5 %mix.1 = (bf16[12,16,256]{2,1,0:T(8,128)(2,1)S(1)}, bf16[24,16,256]{2,1,0:T(8,128)(2,1)S(1)}, bf16[12,16,256]{2,1,0:T(8,128)(2,1)S(1)}, bf16[24,16,256]{2,1,0:T(8,128)(2,1)S(1)}) custom-call(s32[3]{0:T(128)S(1)} %pad_add_fusion.place, bf16[12,16,256]{2,1,0:T(8,128)(2,1)S(1)} %collective-permute-done.refs_0_, ...), custom_call_target="tpu_custom_call" | custom-call | tf_op jit(solution)/shard_map/mix/pallas_call | solution.py:484
  15.0 1.7 %collective-permute-start.3 = (bf16[24,16,256]{2,1,0:T(8,128)(2,1)S(1)}, bf16[24,16,256]{2,1,0:T(8,128)(2,1)S(1)}, u32[]{:S(2)}, u32[]{:S(2)}) collective-permute-start(bf16[24,16,256]{2,1,0:T(8,128)(2,1)S(1)} %get-tuple-element.60.refs_1_), channel_id=1, source_target_pairs={{0,1},{1,2},{2,3},{3,0},{4,5},{5,6},{6,7},{7,4},{8,9},{9,10},{10,1... | collective-permute-start | bytes 589832 | tf_op jit(solution)/shard_map/ppermute | solution.py:363
  16.7 1.1 %collective-permute-start.5 = (bf16[24,16,256]{2,1,0:T(8,128)(2,1)S(1)}, bf16[24,16,256]{2,1,0:T(8,128)(2,1)S(1)}, u32[]{:S(2)}, u32[]{:S(2)}) collective-permute-start(bf16[24,16,256]{2,1,0:T(8,128)(2,1)S(1)} %get-tuple-element.62.refs_2_), channel_id=1, source_target_pairs={{0,3},{1,0},{2,1},{3,2},{4,7},{5,4},{6,5},{7,6},{8,11},{9,8},{10,9... | collective-permute-start | bytes 589832 | tf_op jit(solution)/shard_map/ppermute | solution.py:363
  17.7 0.8 collective-permute-start.4
  18.5 1.6 %list.1 = (s32[3,128]{1,0:T(4,128)S(1)}, bf16[16,32]{1,0:T(8,128)(2,1)S(1)}, s32[1,1024]{1,0:T(1,128)S(1)}) custom-call(s32[3]{0:T(128)S(1)} %pad_add_fusion.place, s32[8,5]{1,0:T(8,128)S(1)} %copy-done.1, f32[16,16]{1,0:T(8,128)S(1)} %copy-done, s32[1,1024]{1,0:T(1,128)S(1)} %bitcast.10), custom_call_target="tpu_custom_call" | custom-call | tf_op jit(solution)/shard_map/list/pallas_call | solution.py:496
  20.2 3.3 %collective-permute-done.4.refs_2_ = bf16[12,16,256]{2,1,0:T(8,128)(2,1)S(1)} collective-permute-done((bf16[12,16,256]{2,1,0:T(8,128)(2,1)S(1)}, bf16[12,16,256]{2,1,0:T(8,128)(2,1)S(1)}, u32[]{:S(2)}, u32[]{:S(2)}) %collective-permute-start.4) | collective-permute-done | bytes 98336 | tf_op jit(solution)/shard_map/ppermute | solution.py:363
  24.1 3.2 %collective-permute-start.6 = (bf16[8,12,16,128]{3,2,1,0:T(8,128)(2,1)S(1)}, bf16[8,12,16,128]{3,2,1,0:T(8,128)(2,1)S(1)}, u32[]{:S(2)}, u32[]{:S(2)}) collective-permute-start(bf16[8,12,16,128]{3,2,1,0:T(8,128)(2,1)S(1)} %gather.2.own), channel_id=1, source_target_pairs={{0,4},{4,0},{8,12},{12,8},{16,20},{20,16},{24,28},{28,24},{32,36},... | collective-permute-start | bytes 1179656 | tf_op jit(solution)/shard_map/ppermute | solution.py:510
  27.3 1.2 %collective-permute-start.7 = (bf16[8,12,16,128]{3,2,1,0:T(8,128)(2,1)S(1)}, bf16[8,12,16,128]{3,2,1,0:T(8,128)(2,1)S(1)}, u32[]{:S(2)}, u32[]{:S(2)}) collective-permute-start(bf16[8,12,16,128]{3,2,1,0:T(8,128)(2,1)S(1)} %gather.2.own), channel_id=1, source_target_pairs={{4,8},{8,4},{12,16},{16,12},{20,24},{24,20},{28,32},{32,28},{36,40... | collective-permute-start | bytes 1179656 | tf_op jit(solution)/shard_map/ppermute | solution.py:511
  28.7 6.1 %near_load.1 = (bf16[8,12,5,128,128]{4,3,2,1,0:T(8,128)(2,1)S(1)}, f32[8,12,16,128]{3,2,1,0:T(8,128)S(1)}) custom-call(s32[3]{0:T(128)S(1)} %pad_add_fusion.place, s32[3,128]{1,0:T(4,128)S(1)} %get-tuple-element.67.entries, bf16[12,8,5,128,128]{4,3,2,1,0:T(8,128)(2,1)} %weights.3, ...), custom_call_target="tpu_custom_call", output_to_operand_aliasing={{0}: (8, {})} | custom-call | bytes 16777216 | tf_op jit(solution)/shard_map/near_load/pallas_call | solution.py:512
  34.8 2.6 %far.2 = (bf16[12,16,1024]{2,1,0:T(8,128)(2,1)}, bf16[12,16,256]{2,1,0:T(8,128)(2,1)S(1)}, bf16[12,16,256]{2,1,0:T(8,128)(2,1)S(1)}, bf16[12,16,256]{2,1,0:T(8,128)(2,1)S(1)}, bf16[24,16,256]{2,1,0:T(8,128)(2,1)S(1)}) custom-call(s32[3]{0:T(128)S(1)} %pad_add_fusion.place, s32[3,128]{1,0:T(4,128)S(1)} %get-tuple-element.67.entries, ...), custom_call_target="tpu_custom_call" | custom-call | bytes 8388608 | tf_op jit(solution)/shard_map/far/pallas_call | solution.py:463
  37.4 2.2 %collective-permute-start.10 = (bf16[24,16,256]{2,1,0:T(8,128)(2,1)S(1)}, bf16[24,16,256]{2,1,0:T(8,128)(2,1)S(1)}, u32[]{:S(2)}, u32[]{:S(2)}) collective-permute-start(bf16[24,16,256]{2,1,0:T(8,128)(2,1)S(1)} %get-tuple-element.82), channel_id=1, source_target_pairs={{0,3},{1,0},{2,1},{3,2},{4,7},{5,4},{6,5},{7,6},{8,11},{9,8},{10,9... | collective-permute-start | bytes 589832 | tf_op jit(solution)/shard_map/ppermute | solution.py:363
  39.6 1.3 %collective-permute-start.9 = (bf16[12,16,256]{2,1,0:T(8,128)(2,1)S(1)}, bf16[12,16,256]{2,1,0:T(8,128)(2,1)S(1)}, u32[]{:S(2)}, u32[]{:S(2)}) collective-permute-start(bf16[12,16,256]{2,1,0:T(8,128)(2,1)S(1)} %get-tuple-element.81), channel_id=1, source_target_pairs={{0,2},{1,3},{2,0},{3,1},{4,6},{5,7},{6,4},{7,5},{8,10},{9,11},{10,... | collective-permute-start | bytes 294920 | tf_op jit(solution)/shard_map/ppermute | solution.py:363
  41.6 1.2 %early.3.refs_4_ = f32[4,12,16,256]{3,2,1,0:T(8,128)S(1)} custom-call(s32[3]{0:T(128)S(1)} %pad_add_fusion.place, bf16[12,16,256]{2,1,0:T(8,128)(2,1)S(1)} %get-tuple-element.83.slab, f32[48,48,256]{2,1,0:T(8,128)S(1)} %get-tuple-element.55.inverse.refs_3_), custom_call_target="tpu_custom_call" | custom-call | bytes 3145728 | tf_op jit(solution)/shard_map/early/pallas_call | solution.py:442
  42.8 2.6 %collective-permute-done.8.refs_0_ = bf16[12,16,256]{2,1,0:T(8,128)(2,1)S(1)} collective-permute-done((bf16[12,16,256]{2,1,0:T(8,128)(2,1)S(1)}, bf16[12,16,256]{2,1,0:T(8,128)(2,1)S(1)}, u32[]{:S(2)}, u32[]{:S(2)}) %collective-permute-start.8) | collective-permute-done | bytes 98336 | tf_op jit(solution)/shard_map/ppermute | solution.py:363
  45.3 2.7 %mix_last.1 = (bf16[13,16,256]{2,1,0:T(8,128)(2,1)S(1)}, bf16[13,16,256]{2,1,0:T(8,128)(2,1)S(1)}, bf16[13,16,256]{2,1,0:T(8,128)(2,1)S(1)}, bf16[13,16,256]{2,1,0:T(8,128)(2,1)S(1)}) custom-call(s32[3]{0:T(128)S(1)} %pad_add_fusion.place, bf16[12,16,256]{2,1,0:T(8,128)(2,1)S(1)} %collective-permute-done.8.refs_0_, ...), custom_call_target="tpu_custom_call" | custom-call | tf_op jit(solution)/shard_map/mix_last/pallas_call | solution.py:542
  48.3 3.1 %collective-permute-start.12 = (bf16[13,16,256]{2,1,0:T(8,128)(2,1)S(1)}, bf16[13,16,256]{2,1,0:T(8,128)(2,1)S(1)}, u32[]{:S(2)}, u32[]{:S(2)}) collective-permute-start(bf16[13,16,256]{2,1,0:T(8,128)(2,1)S(1)} %get-tuple-element.87), channel_id=1, source_target_pairs={{0,2},{1,3},{2,0},{3,1},{4,6},{5,7},{6,4},{7,5},{8,10},{9,11},{10,... | collective-permute-start | bytes 319496 | tf_op jit(solution)/shard_map/ppermute | solution.py:363
  51.4 1.7 %collective-permute-done.11.refs_1_ = bf16[13,16,256]{2,1,0:T(8,128)(2,1)S(1)} collective-permute-done((bf16[13,16,256]{2,1,0:T(8,128)(2,1)S(1)}, bf16[13,16,256]{2,1,0:T(8,128)(2,1)S(1)}, u32[]{:S(2)}, u32[]{:S(2)}) %collective-permute-start.11) | collective-permute-done | bytes 106528 | tf_op jit(solution)/shard_map/ppermute | solution.py:363
  53.1 1.6 %collective-permute-done.12.refs_2_ = bf16[13,16,256]{2,1,0:T(8,128)(2,1)S(1)} collective-permute-done((bf16[13,16,256]{2,1,0:T(8,128)(2,1)S(1)}, bf16[13,16,256]{2,1,0:T(8,128)(2,1)S(1)}, u32[]{:S(2)}, u32[]{:S(2)}) %collective-permute-start.12) | collective-permute-done | bytes 106528 | tf_op jit(solution)/shard_map/ppermute | solution.py:363
  55.6 8.6 %collective-permute-start.15 = (bf16[9,12,16,128]{3,2,1,0:T(8,128)(2,1)S(1)}, bf16[9,12,16,128]{3,2,1,0:T(8,128)(2,1)S(1)}, u32[]{:S(2)}, u32[]{:S(2)}) collective-permute-start(bf16[9,12,16,128]{3,2,1,0:T(8,128)(2,1)S(1)} %get-tuple-element.91), channel_id=1, source_target_pairs={{0,4},{4,0},{8,12},{12,8},{16,20},{20,16},{24,28},{28,24},{32,36},... | collective-permute-start | bytes 1327112 | tf_op jit(solution)/shard_map/ppermute | solution.py:557
  64.2 1.4 %collective-permute-done.15.mate = bf16[9,12,16,128]{3,2,1,0:T(8,128)(2,1)S(1)} collective-permute-done((bf16[9,12,16,128]{3,2,1,0:T(8,128)(2,1)S(1)}, bf16[9,12,16,128]{3,2,1,0:T(8,128)(2,1)S(1)}, u32[]{:S(2)}, u32[]{:S(2)}) %collective-permute-start.15) | collective-permute-done | bytes 442400 | tf_op jit(solution)/shard_map/ppermute | solution.py:557
  65.6 0.9 %collective-permute-start.16 = (f32[16,128]{1,0:T(8,128)S(1)}, f32[16,128]{1,0:T(8,128)S(1)}, u32[]{:S(2)}, u32[]{:S(2)}) collective-permute-start(f32[16,128]{1,0:T(8,128)S(1)} %bitcast_add_fusion), channel_id=1, source_target_pairs={{0,28},{4,24},{8,20},{12,16},{16,12},{20,8},{24,4},{28,0},{32,60},... | collective-permute-start | bytes 24584 | tf_op jit(solution)/shard_map/ppermute | solution.py:561
  66.5 2.8 %near.1.before = f32[8,12,16,128]{3,2,1,0:T(8,128)S(1)} custom-call(s32[3]{0:T(128)S(1)} %pad_add_fusion.place, s32[3,128]{1,0:T(4,128)S(1)} %get-tuple-element.67.entries, bf16[8,12,5,128,128]{4,3,2,1,0:T(8,128)(2,1)S(1)} %get-tuple-element.76.weights, bf16[8,12,16,128]{3,2,1,0:T(8,128)(2,1)S(1)} %get-tuple-element.93.own, ...), custom_call_target="tpu_custom_call" | custom-call | bytes 10485760 | tf_op jit(solution)/shard_map/near/pallas_call | solution.py:565
  69.3 1.0 %collective-permute-done.16 = f32[16,128]{1,0:T(8,128)S(1)} collective-permute-done((f32[16,128]{1,0:T(8,128)S(1)}, f32[16,128]{1,0:T(8,128)S(1)}, u32[]{:S(2)}, u32[]{:S(2)}) %collective-permute-start.16) | collective-permute-done | bytes 8224 | tf_op jit(solution)/shard_map/ppermute | solution.py:561
  70.4 4.8 %collective-permute-start.17 = (f32[16,128]{1,0:T(8,128)S(1)}, f32[16,128]{1,0:T(8,128)S(1)}, u32[]{:S(2)}, u32[]{:S(2)}) collective-permute-start(f32[16,128]{1,0:T(8,128)S(1)} %add.29), channel_id=1, source_target_pairs={{0,100},{4,96},{8,108},{12,104},{16,116},{20,112},{24,124},{28,120... | collective-permute-start | bytes 24584 | tf_op jit(solution)/shard_map/ppermute | solution.py:561
  75.2 2.3 %rest.2.before = f32[8,12,16,128]{3,2,1,0:T(8,128)S(1)} custom-call(s32[3]{0:T(128)S(1)} %pad_add_fusion.place, s32[3,128]{1,0:T(4,128)S(1)} %get-tuple-element.67.entries, bf16[8,12,5,128,128]{4,3,2,1,0:T(8,128)(2,1)S(1)} %get-tuple-element.76.weights, bf16[8,12,16,128]{3,2,1,0:T(8,128)(2,1)S(1)} %get-tuple-element.93.own, ...), custom_call_target="tpu_custom_call" | custom-call | bytes 10485760 | tf_op jit(solution)/shard_map/rest/pallas_call | solution.py:582
  77.6 2.3 %rest.3.before = f32[8,12,16,128]{3,2,1,0:T(8,128)S(1)} custom-call(s32[3]{0:T(128)S(1)} %pad_add_fusion.place, s32[3,128]{1,0:T(4,128)S(1)} %get-tuple-element.67.entries, bf16[8,12,5,128,128]{4,3,2,1,0:T(8,128)(2,1)S(1)} %get-tuple-element.76.weights, bf16[8,12,16,128]{3,2,1,0:T(8,128)(2,1)S(1)} %get-tuple-element.93.own, ...), custom_call_target="tpu_custom_call" | custom-call | bytes 10485760 | tf_op jit(solution)/shard_map/rest/pallas_call | solution.py:582
  80.6 2.6 %far.3 = bf16[12,16,1024]{2,1,0:T(8,128)(2,1)} custom-call(s32[3]{0:T(128)S(1)} %pad_add_fusion.place, s32[3,128]{1,0:T(4,128)S(1)} %get-tuple-element.67.entries, bf16[8,12,5,128,128]{4,3,2,1,0:T(8,128)(2,1)S(1)} %get-tuple-element.76.weights, bf16[8,12,16,128]{3,2,1,0:T(8,128)(2,1)S(1)} %collective-permute-done.14.far, f32[8,12,16,128]{3,2,1,0:T(8,128)S(1)} %rest.3.before, ...), custom_call_target="tpu_custom_call" | custom-call | bytes 8388608 | tf_op jit(solution)/shard_map/far/pallas_call | solution.py:463
  (36 shorter events, 4.9 us)
Async XLA Ops:
  0.6 17.9 %copy-start.1 = (s32[8,5]{1,0:T(8,128)S(1)}, s32[8,5]{1,0:T(8,128)}, u32[]{:S(2)}) copy-start(s32[8,5]{1,0:T(8,128)} %neighbours) | copy-start | bytes 484
  0.6 17.9 %copy-start = (f32[16,16]{1,0:T(8,128)S(1)}, f32[16,16]{1,0:T(8,128)}, u32[]{:S(2)}) copy-start(f32[16,16]{1,0:T(8,128)} %coupling) | copy-start | bytes 3076
  0.7 17.9 %copy-start.2 = (s32[1024]{0:T(1024)S(1)}, s32[1024]{0:T(1024)}, u32[]{:S(2)}) copy-start(s32[1024]{0:T(1024)} %param.15) | copy-start | bytes 12292
  2.5 10.0 %collective-permute-start.2 = (bf16[24,16,256]{2,1,0:T(8,128)(2,1)S(1)}, bf16[24,16,256]{2,1,0:T(8,128)(2,1)S(1)}, u32[]{:S(2)}, u32[]{:S(2)}) collective-permute-start(bf16[24,16,256]{2,1,0:T(8,128)(2,1)S(1)} %get-tuple-element.54), channel_id=1, source_target_pairs={{0,3},{1,0},{2,1},{3,2},{4,7},{5,4},{6,5},{7,6},{8,11},{9,8},{10,9... | collective-permute-start | bytes 589832 | tf_op jit(solution)/shard_map/ppermute | solution.py:363
  6.1 6.3 %collective-permute-start = (bf16[12,16,256]{2,1,0:T(8,128)(2,1)S(1)}, bf16[12,16,256]{2,1,0:T(8,128)(2,1)S(1)}, u32[]{:S(2)}, u32[]{:S(2)}) collective-permute-start(bf16[12,16,256]{2,1,0:T(8,128)(2,1)S(1)} %get-tuple-element.52), channel_id=1, source_target_pairs={{0,1},{1,2},{2,3},{3,0},{4,5},{5,6},{6,7},{7,4},{8,9},{9,10},{10,1... | collective-permute-start | bytes 294920 | tf_op jit(solution)/shard_map/ppermute | solution.py:363
  6.1 6.3 %collective-permute-start.1 = (bf16[12,16,256]{2,1,0:T(8,128)(2,1)S(1)}, bf16[12,16,256]{2,1,0:T(8,128)(2,1)S(1)}, u32[]{:S(2)}, u32[]{:S(2)}) collective-permute-start(bf16[12,16,256]{2,1,0:T(8,128)(2,1)S(1)} %get-tuple-element.53), channel_id=1, source_target_pairs={{0,2},{1,3},{2,0},{3,1},{4,6},{5,7},{6,4},{7,5},{8,10},{9,11},{10,... | collective-permute-start | bytes 294920 | tf_op jit(solution)/shard_map/ppermute | solution.py:363
  15.0 8.5 %collective-permute-start.3 = (bf16[24,16,256]{2,1,0:T(8,128)(2,1)S(1)}, bf16[24,16,256]{2,1,0:T(8,128)(2,1)S(1)}, u32[]{:S(2)}, u32[]{:S(2)}) collective-permute-start(bf16[24,16,256]{2,1,0:T(8,128)(2,1)S(1)} %get-tuple-element.60.refs_1_), channel_id=1, source_target_pairs={{0,1},{1,2},{2,3},{3,0},{4,5},{5,6},{6,7},{7,4},{8,9},{9,10},{10,1... | collective-permute-start | bytes 589832 | tf_op jit(solution)/shard_map/ppermute | solution.py:363
  16.7 6.8 %collective-permute-start.5 = (bf16[24,16,256]{2,1,0:T(8,128)(2,1)S(1)}, bf16[24,16,256]{2,1,0:T(8,128)(2,1)S(1)}, u32[]{:S(2)}, u32[]{:S(2)}) collective-permute-start(bf16[24,16,256]{2,1,0:T(8,128)(2,1)S(1)} %get-tuple-element.62.refs_2_), channel_id=1, source_target_pairs={{0,3},{1,0},{2,1},{3,2},{4,7},{5,4},{6,5},{7,6},{8,11},{9,8},{10,9... | collective-permute-start | bytes 589832 | tf_op jit(solution)/shard_map/ppermute | solution.py:363
  17.7 5.8 %collective-permute-start.4 = (bf16[12,16,256]{2,1,0:T(8,128)(2,1)S(1)}, bf16[12,16,256]{2,1,0:T(8,128)(2,1)S(1)}, u32[]{:S(2)}, u32[]{:S(2)}) collective-permute-start(bf16[12,16,256]{2,1,0:T(8,128)(2,1)S(1)} %get-tuple-element.61.refs_8_), channel_id=1, source_target_pairs={{0,2},{1,3},{2,0},{3,1},{4,6},{5,7},{6,4},{7,5},{8,10},{9,11},{10,... | collective-permute-start | bytes 294920 | tf_op jit(solution)/shard_map/ppermute | solution.py:363
  24.1 4.5 %collective-permute-start.6 = (bf16[8,12,16,128]{3,2,1,0:T(8,128)(2,1)S(1)}, bf16[8,12,16,128]{3,2,1,0:T(8,128)(2,1)S(1)}, u32[]{:S(2)}, u32[]{:S(2)}) collective-permute-start(bf16[8,12,16,128]{3,2,1,0:T(8,128)(2,1)S(1)} %gather.2.own), channel_id=1, source_target_pairs={{0,4},{4,0},{8,12},{12,8},{16,20},{20,16},{24,28},{28,24},{32,36},... | collective-permute-start | bytes 1179656 | tf_op jit(solution)/shard_map/ppermute | solution.py:510
  27.3 7.5 %collective-permute-start.7 = (bf16[8,12,16,128]{3,2,1,0:T(8,128)(2,1)S(1)}, bf16[8,12,16,128]{3,2,1,0:T(8,128)(2,1)S(1)}, u32[]{:S(2)}, u32[]{:S(2)}) collective-permute-start(bf16[8,12,16,128]{3,2,1,0:T(8,128)(2,1)S(1)} %gather.2.own), channel_id=1, source_target_pairs={{4,8},{8,4},{12,16},{16,12},{20,24},{24,20},{28,32},{32,28},{36,40... | collective-permute-start | bytes 1179656 | tf_op jit(solution)/shard_map/ppermute | solution.py:511
  37.4 7.9 %collective-permute-start.10 = (bf16[24,16,256]{2,1,0:T(8,128)(2,1)S(1)}, bf16[24,16,256]{2,1,0:T(8,128)(2,1)S(1)}, u32[]{:S(2)}, u32[]{:S(2)}) collective-permute-start(bf16[24,16,256]{2,1,0:T(8,128)(2,1)S(1)} %get-tuple-element.82), channel_id=1, source_target_pairs={{0,3},{1,0},{2,1},{3,2},{4,7},{5,4},{6,5},{7,6},{8,11},{9,8},{10,9... | collective-permute-start | bytes 589832 | tf_op jit(solution)/shard_map/ppermute | solution.py:363
  39.6 5.7 %collective-permute-start.8 = (bf16[12,16,256]{2,1,0:T(8,128)(2,1)S(1)}, bf16[12,16,256]{2,1,0:T(8,128)(2,1)S(1)}, u32[]{:S(2)}, u32[]{:S(2)}) collective-permute-start(bf16[12,16,256]{2,1,0:T(8,128)(2,1)S(1)} %get-tuple-element.80), channel_id=1, source_target_pairs={{0,1},{1,2},{2,3},{3,0},{4,5},{5,6},{6,7},{7,4},{8,9},{9,10},{10,1... | collective-permute-start | bytes 294920 | tf_op jit(solution)/shard_map/ppermute | solution.py:363
  39.6 5.7 %collective-permute-start.9 = (bf16[12,16,256]{2,1,0:T(8,128)(2,1)S(1)}, bf16[12,16,256]{2,1,0:T(8,128)(2,1)S(1)}, u32[]{:S(2)}, u32[]{:S(2)}) collective-permute-start(bf16[12,16,256]{2,1,0:T(8,128)(2,1)S(1)} %get-tuple-element.81), channel_id=1, source_target_pairs={{0,2},{1,3},{2,0},{3,1},{4,6},{5,7},{6,4},{7,5},{8,10},{9,11},{10,... | collective-permute-start | bytes 294920 | tf_op jit(solution)/shard_map/ppermute | solution.py:363
  48.1 5.0 %collective-permute-start.11 = (bf16[13,16,256]{2,1,0:T(8,128)(2,1)S(1)}, bf16[13,16,256]{2,1,0:T(8,128)(2,1)S(1)}, u32[]{:S(2)}, u32[]{:S(2)}) collective-permute-start(bf16[13,16,256]{2,1,0:T(8,128)(2,1)S(1)} %get-tuple-element.86), channel_id=1, source_target_pairs={{0,1},{1,2},{2,3},{3,0},{4,5},{5,6},{6,7},{7,4},{8,9},{9,10},{10,1... | collective-permute-start | bytes 319496 | tf_op jit(solution)/shard_map/ppermute | solution.py:363
  48.3 6.3 %collective-permute-start.12 = (bf16[13,16,256]{2,1,0:T(8,128)(2,1)S(1)}, bf16[13,16,256]{2,1,0:T(8,128)(2,1)S(1)}, u32[]{:S(2)}, u32[]{:S(2)}) collective-permute-start(bf16[13,16,256]{2,1,0:T(8,128)(2,1)S(1)} %get-tuple-element.87), channel_id=1, source_target_pairs={{0,2},{1,3},{2,0},{3,1},{4,6},{5,7},{6,4},{7,5},{8,10},{9,11},{10,... | collective-permute-start | bytes 319496 | tf_op jit(solution)/shard_map/ppermute | solution.py:363
  51.4 3.6 %collective-permute-start.13 = (bf16[13,16,256]{2,1,0:T(8,128)(2,1)S(1)}, bf16[13,16,256]{2,1,0:T(8,128)(2,1)S(1)}, u32[]{:S(2)}, u32[]{:S(2)}) collective-permute-start(bf16[13,16,256]{2,1,0:T(8,128)(2,1)S(1)} %get-tuple-element.88), channel_id=1, source_target_pairs={{0,3},{1,0},{2,1},{3,2},{4,7},{5,4},{6,5},{7,6},{8,11},{9,8},{10,9... | collective-permute-start | bytes 319496 | tf_op jit(solution)/shard_map/ppermute | solution.py:363
  55.6 10.0 %collective-permute-start.15 = (bf16[9,12,16,128]{3,2,1,0:T(8,128)(2,1)S(1)}, bf16[9,12,16,128]{3,2,1,0:T(8,128)(2,1)S(1)}, u32[]{:S(2)}, u32[]{:S(2)}) collective-permute-start(bf16[9,12,16,128]{3,2,1,0:T(8,128)(2,1)S(1)} %get-tuple-element.91), channel_id=1, source_target_pairs={{0,4},{4,0},{8,12},{12,8},{16,20},{20,16},{24,28},{28,24},{32,36},... | collective-permute-start | bytes 1327112 | tf_op jit(solution)/shard_map/ppermute | solution.py:557
  64.2 16.5 %collective-permute-start.14 = (bf16[8,12,16,128]{3,2,1,0:T(8,128)(2,1)S(1)}, bf16[8,12,16,128]{3,2,1,0:T(8,128)(2,1)S(1)}, u32[]{:S(2)}, u32[]{:S(2)}) collective-permute-start(bf16[8,12,16,128]{3,2,1,0:T(8,128)(2,1)S(1)} %get-tuple-element.93.own), channel_id=1, source_target_pairs={{4,8},{8,4},{12,16},{16,12},{20,24},{24,20},{28,32},{32,28},{36,40... | collective-permute-start | bytes 1179656 | tf_op jit(solution)/shard_map/ppermute | solution.py:558
  65.6 4.7 %collective-permute-start.16 = (f32[16,128]{1,0:T(8,128)S(1)}, f32[16,128]{1,0:T(8,128)S(1)}, u32[]{:S(2)}, u32[]{:S(2)}) collective-permute-start(f32[16,128]{1,0:T(8,128)S(1)} %bitcast_add_fusion), channel_id=1, source_target_pairs={{0,28},{4,24},{8,20},{12,16},{16,12},{20,8},{24,4},{28,0},{32,60},... | collective-permute-start | bytes 24584 | tf_op jit(solution)/shard_map/ppermute | solution.py:561
  70.4 7.1 %collective-permute-start.17 = (f32[16,128]{1,0:T(8,128)S(1)}, f32[16,128]{1,0:T(8,128)S(1)}, u32[]{:S(2)}, u32[]{:S(2)}) collective-permute-start(f32[16,128]{1,0:T(8,128)S(1)} %add.29), channel_id=1, source_target_pairs={{0,100},{4,96},{8,108},{12,104},{16,116},{20,112},{24,124},{28,120... | collective-permute-start | bytes 24584 | tf_op jit(solution)/shard_map/ppermute | solution.py:561
  77.5 3.2 %collective-permute-start.18 = (f32[16,128]{1,0:T(8,128)S(1)}, f32[16,128]{1,0:T(8,128)S(1)}, u32[]{:S(2)}, u32[]{:S(2)}) collective-permute-start(f32[16,128]{1,0:T(8,128)S(1)} %add.30), channel_id=1, source_target_pairs={{0,36},{4,32},{8,44},{12,40},{16,52},{20,48},{24,60},{28,56},{32,4... | collective-permute-start | bytes 24584 | tf_op jit(solution)/shard_map/ppermute | solution.py:561
  80.6 3.1 %collective-permute-start.19 = (f32[16,128]{1,0:T(8,128)S(1)}, f32[16,128]{1,0:T(8,128)S(1)}, u32[]{:S(2)}, u32[]{:S(2)}) collective-permute-start(f32[16,128]{1,0:T(8,128)S(1)} %add.31), channel_id=1, source_target_pairs={{0,12},{4,8},{8,4},{12,0},{16,28},{20,24},{24,20},{28,16},{32,44},... | collective-permute-start | bytes 24584 | tf_op jit(solution)/shard_map/ppermute | solution.py:561

commit v4 on v3

--- a/solution.py
+++ b/solution.py
@@ -181,6 +181,8 @@
     low = (terms - high.astype(jnp.float32)).astype(jnp.bfloat16)
     for s in range(depth):
         parts[s][levels] = jnp.concatenate([high, low], axis=1)
+        for l in range(levels + 1, parts[s].shape[0]):
+            parts[s][l] = jnp.zeros(parts[s].shape[1:], parts[s].dtype)
 
 
 def gather_kernel(depth, scale, place, *refs):
@@ -402,6 +404,7 @@
 
     whole = jax.ShapeDtypeStruct((levels, tracers, cols), jnp.bfloat16)
     slab = jax.ShapeDtypeStruct((levels, tracers, width), jnp.bfloat16)
+    longest = jax.ShapeDtypeStruct((levels + 2, tracers, width), jnp.bfloat16)
     longer = jax.ShapeDtypeStruct((levels + 1, tracers, width), jnp.bfloat16)
     total_shape = jax.ShapeDtypeStruct(block_shape, jnp.float32)
     partial_shape = jax.ShapeDtypeStruct((depth, levels, tracers, width), jnp.float32)
@@ -541,7 +544,7 @@
     )(place, mixed[0], mixed[1], mixed[3], own_sens, one_sens, three_sens, count)
     parts = pl.pallas_call(
         mix_last_kernel,
-        out_shape=[longer] * depth,
+        out_shape=[longer, longer, longest, longer],
         in_specs=[SMEM] + [VMEM] * (depth + 7),
         out_specs=[VMEM] * depth,
         scratch_shapes=[mixed_scratch],

time: 84.5 us -> 84.5 us (level); the launches traced: 84.3 us -> 83.2 us
  waiting for transfers between devices: 13.3 us -> 12.4 us
  transfers between devices with their start and end apart: 20 -> 20, of which waited for: 11 -> 8; matrix products, arithmetic and copies ran while one was open for 0% -> 0% of each run, Pallas kernels for 29% -> 29%
where the time goes in v4:
time: 84.5 us; the launch traced here: 83.2 us
  Pallas kernels  35.1 us (42%)
  starting transfers between devices  34.2 us (40%)
  waiting for transfers between devices  12.4 us (15%)
    ppermute x12, starting transfers between devices, exchange(): lax.ppermute(parts[s], axis, ring(count, s))  15.7 us
    ppermute x12, waiting for transfers between devices, exchange(): lax.ppermute(parts[s], axis, ring(count, s))  8.99 us
    ppermute x1, starting transfers between devices, per_device(): mate = lax.ppermute(message, 'horiz', swap)  7.77 us
    ppermute x4, starting transfers between devices, add_pairs(): lax.ppermute(terms, 'horiz', [(i, i ^ flip) for i in range(horiz)])  6.29 us
    pallas_call x1, Pallas kernels, per_device(): pl.pallas_call(functools.partial(near_kernel, True), out_shape=[pltpu.VME...  6.12 us
    pallas_call x2, Pallas kernels, move_far(): pl.pallas_call(functools.partial(far_kernel, len(behind)), out_shape=shap...  5.15 us
    pallas_call x2, Pallas kernels, per_device(): pl.pallas_call(functools.partial(rest_kernel, third), out_shape=total_sha...  4.61 us
    pallas_call x1, Pallas kernels, per_device(): pl.pallas_call(prepare_kernel, out_shape=[pltpu.VMEM(inv_mix.shape, jnp.f...  3.48 us
  transfers between devices with their start and end apart: 20, of which 8 were waited for; matrix products, arithmetic and copies ran while one was open for 0% of the time, Pallas kernels for 29%

profile of v4, /device:TPU:1, one launch (start us, length us, event | category | flops | bytes accessed | tf_op | source)
XLA Modules:
  0.0 83.2 jit_solution(15626110171215362749)
XLA Ops:
  0.7 1.7 %split.1 = (bf16[12,16,256]{2,1,0:T(8,128)(2,1)S(1)}, bf16[12,16,256]{2,1,0:T(8,128)(2,1)S(1)}, bf16[24,16,256]{2,1,0:T(8,128)(2,1)S(1)}, bf16[12,16,256]{2,1,0:...) custom-call(s32[3]{0:T(128)S(1)} %pad_add_fusion.place, ...), custom_call_target="tpu_custom_call" | custom-call | tf_op jit(solution)/shard_map/split/pallas_call | solution.py:416
  2.5 3.6 %collective-permute-start.2 = (bf16[24,16,256]{2,1,0:T(8,128)(2,1)S(1)}, bf16[24,16,256]{2,1,0:T(8,128)(2,1)S(1)}, u32[]{:S(2)}, u32[]{:S(2)}) collective-permute-start(bf16[24,16,256]{2,1,0:T(8,128)(2,1)S(1)} %get-tuple-element.54), channel_id=1, source_target_pairs={{0,3},{1,0},{2,1},{3,2},{4,7},{5,4},{6,5},{7,6},{8,11},{9,8},{10,9... | collective-permute-start | bytes 589832 | tf_op jit(solution)/shard_map/ppermute | solution.py:365
  6.1 1.6 %collective-permute-start.1 = (bf16[12,16,256]{2,1,0:T(8,128)(2,1)S(1)}, bf16[12,16,256]{2,1,0:T(8,128)(2,1)S(1)}, u32[]{:S(2)}, u32[]{:S(2)}) collective-permute-start(bf16[12,16,256]{2,1,0:T(8,128)(2,1)S(1)} %get-tuple-element.53), channel_id=1, source_target_pairs={{0,2},{1,3},{2,0},{3,1},{4,6},{5,7},{6,4},{7,5},{8,10},{9,11},{10,... | collective-permute-start | bytes 294920 | tf_op jit(solution)/shard_map/ppermute | solution.py:365
  7.8 3.5 %prepare.1 = (f32[48,48,256]{2,1,0:T(8,128)S(1)}, f32[12,1024]{1,0:T(8,128)S(1)}, bf16[8,12,5,128,128]{4,3,2,1,0:T(8,128)(2,1)S(1)}) custom-call(f32[48,48,256]{2,1,0:T(8,128)} %inverse.1, f32[12,1024]{1,0:T(8,128)} %rates.1, bf16[12,8,5,128,128]{4,3,2,1,0:T(8,128)(2,1)} %weights.3), custom_call_target="tpu_custom_call" | custom-call | tf_op jit(solution)/shard_map/prepare/pallas_call | solution.py:430
  11.2 1.2 %early.2.refs_4_ = f32[4,12,16,256]{3,2,1,0:T(8,128)S(1)} custom-call(s32[3]{0:T(128)S(1)} %pad_add_fusion.place, bf16[12,16,256]{2,1,0:T(8,128)(2,1)S(1)} %get-tuple-element.56.slab, f32[48,48,256]{2,1,0:T(8,128)S(1)} %get-tuple-element.55.inverse.refs_3_), custom_call_target="tpu_custom_call" | custom-call | bytes 3145728 | tf_op jit(solution)/shard_map/early/pallas_call | solution.py:445
  12.5 2.5 %mix.1 = (bf16[12,16,256]{2,1,0:T(8,128)(2,1)S(1)}, bf16[24,16,256]{2,1,0:T(8,128)(2,1)S(1)}, bf16[12,16,256]{2,1,0:T(8,128)(2,1)S(1)}, bf16[24,16,256]{2,1,0:T(8,128)(2,1)S(1)}) custom-call(s32[3]{0:T(128)S(1)} %pad_add_fusion.place, bf16[12,16,256]{2,1,0:T(8,128)(2,1)S(1)} %collective-permute-done.refs_0_, ...), custom_call_target="tpu_custom_call" | custom-call | tf_op jit(solution)/shard_map/mix/pallas_call | solution.py:487
  15.0 1.7 %collective-permute-start.3 = (bf16[24,16,256]{2,1,0:T(8,128)(2,1)S(1)}, bf16[24,16,256]{2,1,0:T(8,128)(2,1)S(1)}, u32[]{:S(2)}, u32[]{:S(2)}) collective-permute-start(bf16[24,16,256]{2,1,0:T(8,128)(2,1)S(1)} %get-tuple-element.60.refs_1_), channel_id=1, source_target_pairs={{0,1},{1,2},{2,3},{3,0},{4,5},{5,6},{6,7},{7,4},{8,9},{9,10},{10,1... | collective-permute-start | bytes 589832 | tf_op jit(solution)/shard_map/ppermute | solution.py:365
  16.7 1.1 %collective-permute-start.5 = (bf16[24,16,256]{2,1,0:T(8,128)(2,1)S(1)}, bf16[24,16,256]{2,1,0:T(8,128)(2,1)S(1)}, u32[]{:S(2)}, u32[]{:S(2)}) collective-permute-start(bf16[24,16,256]{2,1,0:T(8,128)(2,1)S(1)} %get-tuple-element.62.refs_2_), channel_id=1, source_target_pairs={{0,3},{1,0},{2,1},{3,2},{4,7},{5,4},{6,5},{7,6},{8,11},{9,8},{10,9... | collective-permute-start | bytes 589832 | tf_op jit(solution)/shard_map/ppermute | solution.py:365
  17.8 0.8 collective-permute-start.4
  18.6 1.6 %list.1 = (s32[3,128]{1,0:T(4,128)S(1)}, bf16[16,32]{1,0:T(8,128)(2,1)S(1)}, s32[1,1024]{1,0:T(1,128)S(1)}) custom-call(s32[3]{0:T(128)S(1)} %pad_add_fusion.place, s32[8,5]{1,0:T(8,128)S(1)} %copy-done.1, f32[16,16]{1,0:T(8,128)S(1)} %copy-done, s32[1,1024]{1,0:T(1,128)S(1)} %bitcast.10), custom_call_target="tpu_custom_call" | custom-call | tf_op jit(solution)/shard_map/list/pallas_call | solution.py:499
  20.2 3.3 %collective-permute-done.4.refs_2_ = bf16[12,16,256]{2,1,0:T(8,128)(2,1)S(1)} collective-permute-done((bf16[12,16,256]{2,1,0:T(8,128)(2,1)S(1)}, bf16[12,16,256]{2,1,0:T(8,128)(2,1)S(1)}, u32[]{:S(2)}, u32[]{:S(2)}) %collective-permute-start.4) | collective-permute-done | bytes 98336 | tf_op jit(solution)/shard_map/ppermute | solution.py:365
  24.1 3.2 %collective-permute-start.6 = (bf16[8,12,16,128]{3,2,1,0:T(8,128)(2,1)S(1)}, bf16[8,12,16,128]{3,2,1,0:T(8,128)(2,1)S(1)}, u32[]{:S(2)}, u32[]{:S(2)}) collective-permute-start(bf16[8,12,16,128]{3,2,1,0:T(8,128)(2,1)S(1)} %gather.2.own), channel_id=1, source_target_pairs={{0,4},{4,0},{8,12},{12,8},{16,20},{20,16},{24,28},{28,24},{32,36},... | collective-permute-start | bytes 1179656 | tf_op jit(solution)/shard_map/ppermute | solution.py:513
  27.3 1.2 %collective-permute-start.7 = (bf16[8,12,16,128]{3,2,1,0:T(8,128)(2,1)S(1)}, bf16[8,12,16,128]{3,2,1,0:T(8,128)(2,1)S(1)}, u32[]{:S(2)}, u32[]{:S(2)}) collective-permute-start(bf16[8,12,16,128]{3,2,1,0:T(8,128)(2,1)S(1)} %gather.2.own), channel_id=1, source_target_pairs={{4,8},{8,4},{12,16},{16,12},{20,24},{24,20},{28,32},{32,28},{36,40... | collective-permute-start | bytes 1179656 | tf_op jit(solution)/shard_map/ppermute | solution.py:514
  28.7 6.1 %near_load.1 = (bf16[8,12,5,128,128]{4,3,2,1,0:T(8,128)(2,1)S(1)}, f32[8,12,16,128]{3,2,1,0:T(8,128)S(1)}) custom-call(s32[3]{0:T(128)S(1)} %pad_add_fusion.place, s32[3,128]{1,0:T(4,128)S(1)} %get-tuple-element.67.entries, bf16[12,8,5,128,128]{4,3,2,1,0:T(8,128)(2,1)} %weights.3, ...), custom_call_target="tpu_custom_call", output_to_operand_aliasing={{0}: (8, {})} | custom-call | bytes 16777216 | tf_op jit(solution)/shard_map/near_load/pallas_call | solution.py:515
  34.8 2.6 %far.2 = (bf16[12,16,1024]{2,1,0:T(8,128)(2,1)}, bf16[12,16,256]{2,1,0:T(8,128)(2,1)S(1)}, bf16[12,16,256]{2,1,0:T(8,128)(2,1)S(1)}, bf16[12,16,256]{2,1,0:T(8,128)(2,1)S(1)}, bf16[24,16,256]{2,1,0:T(8,128)(2,1)S(1)}) custom-call(s32[3]{0:T(128)S(1)} %pad_add_fusion.place, s32[3,128]{1,0:T(4,128)S(1)} %get-tuple-element.67.entries, ...), custom_call_target="tpu_custom_call" | custom-call | bytes 8388608 | tf_op jit(solution)/shard_map/far/pallas_call | solution.py:466
  37.4 2.2 %collective-permute-start.10 = (bf16[24,16,256]{2,1,0:T(8,128)(2,1)S(1)}, bf16[24,16,256]{2,1,0:T(8,128)(2,1)S(1)}, u32[]{:S(2)}, u32[]{:S(2)}) collective-permute-start(bf16[24,16,256]{2,1,0:T(8,128)(2,1)S(1)} %get-tuple-element.82), channel_id=1, source_target_pairs={{0,3},{1,0},{2,1},{3,2},{4,7},{5,4},{6,5},{7,6},{8,11},{9,8},{10,9... | collective-permute-start | bytes 589832 | tf_op jit(solution)/shard_map/ppermute | solution.py:365
  39.6 1.3 %collective-permute-start.9 = (bf16[12,16,256]{2,1,0:T(8,128)(2,1)S(1)}, bf16[12,16,256]{2,1,0:T(8,128)(2,1)S(1)}, u32[]{:S(2)}, u32[]{:S(2)}) collective-permute-start(bf16[12,16,256]{2,1,0:T(8,128)(2,1)S(1)} %get-tuple-element.81), channel_id=1, source_target_pairs={{0,2},{1,3},{2,0},{3,1},{4,6},{5,7},{6,4},{7,5},{8,10},{9,11},{10,... | collective-permute-start | bytes 294920 | tf_op jit(solution)/shard_map/ppermute | solution.py:365
  41.6 1.2 %early.3.refs_4_ = f32[4,12,16,256]{3,2,1,0:T(8,128)S(1)} custom-call(s32[3]{0:T(128)S(1)} %pad_add_fusion.place, bf16[12,16,256]{2,1,0:T(8,128)(2,1)S(1)} %get-tuple-element.83.slab, f32[48,48,256]{2,1,0:T(8,128)S(1)} %get-tuple-element.55.inverse.refs_3_), custom_call_target="tpu_custom_call" | custom-call | bytes 3145728 | tf_op jit(solution)/shard_map/early/pallas_call | solution.py:445
  42.8 2.5 %collective-permute-done.8.refs_0_ = bf16[12,16,256]{2,1,0:T(8,128)(2,1)S(1)} collective-permute-done((bf16[12,16,256]{2,1,0:T(8,128)(2,1)S(1)}, bf16[12,16,256]{2,1,0:T(8,128)(2,1)S(1)}, u32[]{:S(2)}, u32[]{:S(2)}) %collective-permute-start.8) | collective-permute-done | bytes 98336 | tf_op jit(solution)/shard_map/ppermute | solution.py:365
  45.3 2.7 %mix_last.1 = (bf16[13,16,256]{2,1,0:T(8,128)(2,1)S(1)}, bf16[13,16,256]{2,1,0:T(8,128)(2,1)S(1)}, bf16[14,16,256]{2,1,0:T(8,128)(2,1)S(1)}, bf16[13,16,256]{2,1,0:T(8,128)(2,1)S(1)}) custom-call(s32[3]{0:T(128)S(1)} %pad_add_fusion.place, bf16[12,16,256]{2,1,0:T(8,128)(2,1)S(1)} %collective-permute-done.8.refs_0_, ...), custom_call_target="tpu_custom_call" | custom-call | tf_op jit(solution)/shard_map/mix_last/pallas_call | solution.py:545
  48.1 0.8 collective-permute-start.12
  48.8 2.0 %collective-permute-start.11 = (bf16[13,16,256]{2,1,0:T(8,128)(2,1)S(1)}, bf16[13,16,256]{2,1,0:T(8,128)(2,1)S(1)}, u32[]{:S(2)}, u32[]{:S(2)}) collective-permute-start(bf16[13,16,256]{2,1,0:T(8,128)(2,1)S(1)} %get-tuple-element.86), channel_id=1, source_target_pairs={{0,1},{1,2},{2,3},{3,0},{4,5},{5,6},{6,7},{7,4},{8,9},{9,10},{10,1... | collective-permute-start | bytes 319496 | tf_op jit(solution)/shard_map/ppermute | solution.py:365
  51.5 3.1 %collective-permute-done.11.refs_1_ = bf16[13,16,256]{2,1,0:T(8,128)(2,1)S(1)} collective-permute-done((bf16[13,16,256]{2,1,0:T(8,128)(2,1)S(1)}, bf16[13,16,256]{2,1,0:T(8,128)(2,1)S(1)}, u32[]{:S(2)}, u32[]{:S(2)}) %collective-permute-start.11) | collective-permute-done | bytes 106528 | tf_op jit(solution)/shard_map/ppermute | solution.py:365
  55.3 7.8 %collective-permute-start.15 = (bf16[9,12,16,128]{3,2,1,0:T(8,128)(2,1)S(1)}, bf16[9,12,16,128]{3,2,1,0:T(8,128)(2,1)S(1)}, u32[]{:S(2)}, u32[]{:S(2)}) collective-permute-start(bf16[9,12,16,128]{3,2,1,0:T(8,128)(2,1)S(1)} %get-tuple-element.91), channel_id=1, source_target_pairs={{0,4},{4,0},{8,12},{12,8},{16,20},{20,16},{24,28},{28,24},{32,36},... | collective-permute-start | bytes 1327112 | tf_op jit(solution)/shard_map/ppermute | solution.py:560
  63.1 1.4 %collective-permute-done.15.mate = bf16[9,12,16,128]{3,2,1,0:T(8,128)(2,1)S(1)} collective-permute-done((bf16[9,12,16,128]{3,2,1,0:T(8,128)(2,1)S(1)}, bf16[9,12,16,128]{3,2,1,0:T(8,128)(2,1)S(1)}, u32[]{:S(2)}, u32[]{:S(2)}) %collective-permute-start.15) | collective-permute-done | bytes 442400 | tf_op jit(solution)/shard_map/ppermute | solution.py:560
  64.5 1.4 %collective-permute-start.16 = (f32[16,128]{1,0:T(8,128)S(1)}, f32[16,128]{1,0:T(8,128)S(1)}, u32[]{:S(2)}, u32[]{:S(2)}) collective-permute-start(f32[16,128]{1,0:T(8,128)S(1)} %bitcast_add_fusion), channel_id=1, source_target_pairs={{0,28},{4,24},{8,20},{12,16},{16,12},{20,8},{24,4},{28,0},{32,60},... | collective-permute-start | bytes 24584 | tf_op jit(solution)/shard_map/ppermute | solution.py:564
  65.9 2.8 %near.1.before = f32[8,12,16,128]{3,2,1,0:T(8,128)S(1)} custom-call(s32[3]{0:T(128)S(1)} %pad_add_fusion.place, s32[3,128]{1,0:T(4,128)S(1)} %get-tuple-element.67.entries, bf16[8,12,5,128,128]{4,3,2,1,0:T(8,128)(2,1)S(1)} %get-tuple-element.76.weights, bf16[8,12,16,128]{3,2,1,0:T(8,128)(2,1)S(1)} %get-tuple-element.93.own, ...), custom_call_target="tpu_custom_call" | custom-call | bytes 10485760 | tf_op jit(solution)/shard_map/near/pallas_call | solution.py:568
  69.2 4.8 %collective-permute-start.17 = (f32[16,128]{1,0:T(8,128)S(1)}, f32[16,128]{1,0:T(8,128)S(1)}, u32[]{:S(2)}, u32[]{:S(2)}) collective-permute-start(f32[16,128]{1,0:T(8,128)S(1)} %add.29), channel_id=1, source_target_pairs={{0,100},{4,96},{8,108},{12,104},{16,116},{20,112},{24,124},{28,120... | collective-permute-start | bytes 24584 | tf_op jit(solution)/shard_map/ppermute | solution.py:564
  74.0 2.3 %rest.2.before = f32[8,12,16,128]{3,2,1,0:T(8,128)S(1)} custom-call(s32[3]{0:T(128)S(1)} %pad_add_fusion.place, s32[3,128]{1,0:T(4,128)S(1)} %get-tuple-element.67.entries, bf16[8,12,5,128,128]{4,3,2,1,0:T(8,128)(2,1)S(1)} %get-tuple-element.76.weights, bf16[8,12,16,128]{3,2,1,0:T(8,128)(2,1)S(1)} %get-tuple-element.93.own, ...), custom_call_target="tpu_custom_call" | custom-call | bytes 10485760 | tf_op jit(solution)/shard_map/rest/pallas_call | solution.py:585
  76.4 2.3 %rest.3.before = f32[8,12,16,128]{3,2,1,0:T(8,128)S(1)} custom-call(s32[3]{0:T(128)S(1)} %pad_add_fusion.place, s32[3,128]{1,0:T(4,128)S(1)} %get-tuple-element.67.entries, bf16[8,12,5,128,128]{4,3,2,1,0:T(8,128)(2,1)S(1)} %get-tuple-element.76.weights, bf16[8,12,16,128]{3,2,1,0:T(8,128)(2,1)S(1)} %get-tuple-element.93.own, ...), custom_call_target="tpu_custom_call" | custom-call | bytes 10485760 | tf_op jit(solution)/shard_map/rest/pallas_call | solution.py:585
  78.7 0.8 collective-permute-done.18
  79.5 2.6 %far.3 = bf16[12,16,1024]{2,1,0:T(8,128)(2,1)} custom-call(s32[3]{0:T(128)S(1)} %pad_add_fusion.place, s32[3,128]{1,0:T(4,128)S(1)} %get-tuple-element.67.entries, bf16[8,12,5,128,128]{4,3,2,1,0:T(8,128)(2,1)S(1)} %get-tuple-element.76.weights, bf16[8,12,16,128]{3,2,1,0:T(8,128)(2,1)S(1)} %collective-permute-done.14.far, f32[8,12,16,128]{3,2,1,0:T(8,128)S(1)} %rest.3.before, ...), custom_call_target="tpu_custom_call" | custom-call | bytes 8388608 | tf_op jit(solution)/shard_map/far/pallas_call | solution.py:466
  (36 shorter events, 4.8 us)
Async XLA Ops:
  0.6 17.9 %copy-start.1 = (s32[8,5]{1,0:T(8,128)S(1)}, s32[8,5]{1,0:T(8,128)}, u32[]{:S(2)}) copy-start(s32[8,5]{1,0:T(8,128)} %neighbours) | copy-start | bytes 484
  0.6 17.9 %copy-start = (f32[16,16]{1,0:T(8,128)S(1)}, f32[16,16]{1,0:T(8,128)}, u32[]{:S(2)}) copy-start(f32[16,16]{1,0:T(8,128)} %coupling) | copy-start | bytes 3076
  0.7 17.9 %copy-start.2 = (s32[1024]{0:T(1024)S(1)}, s32[1024]{0:T(1024)}, u32[]{:S(2)}) copy-start(s32[1024]{0:T(1024)} %param.15) | copy-start | bytes 12292
  2.5 10.0 %collective-permute-start.2 = (bf16[24,16,256]{2,1,0:T(8,128)(2,1)S(1)}, bf16[24,16,256]{2,1,0:T(8,128)(2,1)S(1)}, u32[]{:S(2)}, u32[]{:S(2)}) collective-permute-start(bf16[24,16,256]{2,1,0:T(8,128)(2,1)S(1)} %get-tuple-element.54), channel_id=1, source_target_pairs={{0,3},{1,0},{2,1},{3,2},{4,7},{5,4},{6,5},{7,6},{8,11},{9,8},{10,9... | collective-permute-start | bytes 589832 | tf_op jit(solution)/shard_map/ppermute | solution.py:365
  6.1 6.3 %collective-permute-start = (bf16[12,16,256]{2,1,0:T(8,128)(2,1)S(1)}, bf16[12,16,256]{2,1,0:T(8,128)(2,1)S(1)}, u32[]{:S(2)}, u32[]{:S(2)}) collective-permute-start(bf16[12,16,256]{2,1,0:T(8,128)(2,1)S(1)} %get-tuple-element.52), channel_id=1, source_target_pairs={{0,1},{1,2},{2,3},{3,0},{4,5},{5,6},{6,7},{7,4},{8,9},{9,10},{10,1... | collective-permute-start | bytes 294920 | tf_op jit(solution)/shard_map/ppermute | solution.py:365
  6.1 6.3 %collective-permute-start.1 = (bf16[12,16,256]{2,1,0:T(8,128)(2,1)S(1)}, bf16[12,16,256]{2,1,0:T(8,128)(2,1)S(1)}, u32[]{:S(2)}, u32[]{:S(2)}) collective-permute-start(bf16[12,16,256]{2,1,0:T(8,128)(2,1)S(1)} %get-tuple-element.53), channel_id=1, source_target_pairs={{0,2},{1,3},{2,0},{3,1},{4,6},{5,7},{6,4},{7,5},{8,10},{9,11},{10,... | collective-permute-start | bytes 294920 | tf_op jit(solution)/shard_map/ppermute | solution.py:365
  15.0 8.5 %collective-permute-start.3 = (bf16[24,16,256]{2,1,0:T(8,128)(2,1)S(1)}, bf16[24,16,256]{2,1,0:T(8,128)(2,1)S(1)}, u32[]{:S(2)}, u32[]{:S(2)}) collective-permute-start(bf16[24,16,256]{2,1,0:T(8,128)(2,1)S(1)} %get-tuple-element.60.refs_1_), channel_id=1, source_target_pairs={{0,1},{1,2},{2,3},{3,0},{4,5},{5,6},{6,7},{7,4},{8,9},{9,10},{10,1... | collective-permute-start | bytes 589832 | tf_op jit(solution)/shard_map/ppermute | solution.py:365
  16.7 6.8 %collective-permute-start.5 = (bf16[24,16,256]{2,1,0:T(8,128)(2,1)S(1)}, bf16[24,16,256]{2,1,0:T(8,128)(2,1)S(1)}, u32[]{:S(2)}, u32[]{:S(2)}) collective-permute-start(bf16[24,16,256]{2,1,0:T(8,128)(2,1)S(1)} %get-tuple-element.62.refs_2_), channel_id=1, source_target_pairs={{0,3},{1,0},{2,1},{3,2},{4,7},{5,4},{6,5},{7,6},{8,11},{9,8},{10,9... | collective-permute-start | bytes 589832 | tf_op jit(solution)/shard_map/ppermute | solution.py:365
  17.8 5.8 %collective-permute-start.4 = (bf16[12,16,256]{2,1,0:T(8,128)(2,1)S(1)}, bf16[12,16,256]{2,1,0:T(8,128)(2,1)S(1)}, u32[]{:S(2)}, u32[]{:S(2)}) collective-permute-start(bf16[12,16,256]{2,1,0:T(8,128)(2,1)S(1)} %get-tuple-element.61.refs_8_), channel_id=1, source_target_pairs={{0,2},{1,3},{2,0},{3,1},{4,6},{5,7},{6,4},{7,5},{8,10},{9,11},{10,... | collective-permute-start | bytes 294920 | tf_op jit(solution)/shard_map/ppermute | solution.py:365
  24.1 4.5 %collective-permute-start.6 = (bf16[8,12,16,128]{3,2,1,0:T(8,128)(2,1)S(1)}, bf16[8,12,16,128]{3,2,1,0:T(8,128)(2,1)S(1)}, u32[]{:S(2)}, u32[]{:S(2)}) collective-permute-start(bf16[8,12,16,128]{3,2,1,0:T(8,128)(2,1)S(1)} %gather.2.own), channel_id=1, source_target_pairs={{0,4},{4,0},{8,12},{12,8},{16,20},{20,16},{24,28},{28,24},{32,36},... | collective-permute-start | bytes 1179656 | tf_op jit(solution)/shard_map/ppermute | solution.py:513
  27.3 7.5 %collective-permute-start.7 = (bf16[8,12,16,128]{3,2,1,0:T(8,128)(2,1)S(1)}, bf16[8,12,16,128]{3,2,1,0:T(8,128)(2,1)S(1)}, u32[]{:S(2)}, u32[]{:S(2)}) collective-permute-start(bf16[8,12,16,128]{3,2,1,0:T(8,128)(2,1)S(1)} %gather.2.own), channel_id=1, source_target_pairs={{4,8},{8,4},{12,16},{16,12},{20,24},{24,20},{28,32},{32,28},{36,40... | collective-permute-start | bytes 1179656 | tf_op jit(solution)/shard_map/ppermute | solution.py:514
  37.4 8.0 %collective-permute-start.10 = (bf16[24,16,256]{2,1,0:T(8,128)(2,1)S(1)}, bf16[24,16,256]{2,1,0:T(8,128)(2,1)S(1)}, u32[]{:S(2)}, u32[]{:S(2)}) collective-permute-start(bf16[24,16,256]{2,1,0:T(8,128)(2,1)S(1)} %get-tuple-element.82), channel_id=1, source_target_pairs={{0,3},{1,0},{2,1},{3,2},{4,7},{5,4},{6,5},{7,6},{8,11},{9,8},{10,9... | collective-permute-start | bytes 589832 | tf_op jit(solution)/shard_map/ppermute | solution.py:365
  39.6 5.7 %collective-permute-start.8 = (bf16[12,16,256]{2,1,0:T(8,128)(2,1)S(1)}, bf16[12,16,256]{2,1,0:T(8,128)(2,1)S(1)}, u32[]{:S(2)}, u32[]{:S(2)}) collective-permute-start(bf16[12,16,256]{2,1,0:T(8,128)(2,1)S(1)} %get-tuple-element.80), channel_id=1, source_target_pairs={{0,1},{1,2},{2,3},{3,0},{4,5},{5,6},{6,7},{7,4},{8,9},{9,10},{10,1... | collective-permute-start | bytes 294920 | tf_op jit(solution)/shard_map/ppermute | solution.py:365
  39.6 5.7 %collective-permute-start.9 = (bf16[12,16,256]{2,1,0:T(8,128)(2,1)S(1)}, bf16[12,16,256]{2,1,0:T(8,128)(2,1)S(1)}, u32[]{:S(2)}, u32[]{:S(2)}) collective-permute-start(bf16[12,16,256]{2,1,0:T(8,128)(2,1)S(1)} %get-tuple-element.81), channel_id=1, source_target_pairs={{0,2},{1,3},{2,0},{3,1},{4,6},{5,7},{6,4},{7,5},{8,10},{9,11},{10,... | collective-permute-start | bytes 294920 | tf_op jit(solution)/shard_map/ppermute | solution.py:365
  48.1 6.6 %collective-permute-start.12 = (bf16[14,16,256]{2,1,0:T(8,128)(2,1)S(1)}, bf16[14,16,256]{2,1,0:T(8,128)(2,1)S(1)}, u32[]{:S(2)}, u32[]{:S(2)}) collective-permute-start(bf16[14,16,256]{2,1,0:T(8,128)(2,1)S(1)} %get-tuple-element.87), channel_id=1, source_target_pairs={{0,2},{1,3},{2,0},{3,1},{4,6},{5,7},{6,4},{7,5},{8,10},{9,11},{10,... | collective-permute-start | bytes 344072 | tf_op jit(solution)/shard_map/ppermute | solution.py:365
  48.8 5.8 %collective-permute-start.11 = (bf16[13,16,256]{2,1,0:T(8,128)(2,1)S(1)}, bf16[13,16,256]{2,1,0:T(8,128)(2,1)S(1)}, u32[]{:S(2)}, u32[]{:S(2)}) collective-permute-start(bf16[13,16,256]{2,1,0:T(8,128)(2,1)S(1)} %get-tuple-element.86), channel_id=1, source_target_pairs={{0,1},{1,2},{2,3},{3,0},{4,5},{5,6},{6,7},{7,4},{8,9},{9,10},{10,1... | collective-permute-start | bytes 319496 | tf_op jit(solution)/shard_map/ppermute | solution.py:365
  50.8 3.8 %collective-permute-start.13 = (bf16[13,16,256]{2,1,0:T(8,128)(2,1)S(1)}, bf16[13,16,256]{2,1,0:T(8,128)(2,1)S(1)}, u32[]{:S(2)}, u32[]{:S(2)}) collective-permute-start(bf16[13,16,256]{2,1,0:T(8,128)(2,1)S(1)} %get-tuple-element.88), channel_id=1, source_target_pairs={{0,3},{1,0},{2,1},{3,2},{4,7},{5,4},{6,5},{7,6},{8,11},{9,8},{10,9... | collective-permute-start | bytes 319496 | tf_op jit(solution)/shard_map/ppermute | solution.py:365
  55.3 9.2 %collective-permute-start.15 = (bf16[9,12,16,128]{3,2,1,0:T(8,128)(2,1)S(1)}, bf16[9,12,16,128]{3,2,1,0:T(8,128)(2,1)S(1)}, u32[]{:S(2)}, u32[]{:S(2)}) collective-permute-start(bf16[9,12,16,128]{3,2,1,0:T(8,128)(2,1)S(1)} %get-tuple-element.91), channel_id=1, source_target_pairs={{0,4},{4,0},{8,12},{12,8},{16,20},{20,16},{24,28},{28,24},{32,36},... | collective-permute-start | bytes 1327112 | tf_op jit(solution)/shard_map/ppermute | solution.py:560
  63.0 16.5 %collective-permute-start.14 = (bf16[8,12,16,128]{3,2,1,0:T(8,128)(2,1)S(1)}, bf16[8,12,16,128]{3,2,1,0:T(8,128)(2,1)S(1)}, u32[]{:S(2)}, u32[]{:S(2)}) collective-permute-start(bf16[8,12,16,128]{3,2,1,0:T(8,128)(2,1)S(1)} %get-tuple-element.93.own), channel_id=1, source_target_pairs={{4,8},{8,4},{12,16},{16,12},{20,24},{24,20},{28,32},{32,28},{36,40... | collective-permute-start | bytes 1179656 | tf_op jit(solution)/shard_map/ppermute | solution.py:561
  64.5 4.7 %collective-permute-start.16 = (f32[16,128]{1,0:T(8,128)S(1)}, f32[16,128]{1,0:T(8,128)S(1)}, u32[]{:S(2)}, u32[]{:S(2)}) collective-permute-start(f32[16,128]{1,0:T(8,128)S(1)} %bitcast_add_fusion), channel_id=1, source_target_pairs={{0,28},{4,24},{8,20},{12,16},{16,12},{20,8},{24,4},{28,0},{32,60},... | collective-permute-start | bytes 24584 | tf_op jit(solution)/shard_map/ppermute | solution.py:564
  69.2 7.1 %collective-permute-start.17 = (f32[16,128]{1,0:T(8,128)S(1)}, f32[16,128]{1,0:T(8,128)S(1)}, u32[]{:S(2)}, u32[]{:S(2)}) collective-permute-start(f32[16,128]{1,0:T(8,128)S(1)} %add.29), channel_id=1, source_target_pairs={{0,100},{4,96},{8,108},{12,104},{16,116},{20,112},{24,124},{28,120... | collective-permute-start | bytes 24584 | tf_op jit(solution)/shard_map/ppermute | solution.py:564
  76.4 3.2 %collective-permute-start.18 = (f32[16,128]{1,0:T(8,128)S(1)}, f32[16,128]{1,0:T(8,128)S(1)}, u32[]{:S(2)}, u32[]{:S(2)}) collective-permute-start(f32[16,128]{1,0:T(8,128)S(1)} %add.30), channel_id=1, source_target_pairs={{0,36},{4,32},{8,44},{12,40},{16,52},{20,48},{24,60},{28,56},{32,4... | collective-permute-start | bytes 24584 | tf_op jit(solution)/shard_map/ppermute | solution.py:564
  79.5 3.1 %collective-permute-start.19 = (f32[16,128]{1,0:T(8,128)S(1)}, f32[16,128]{1,0:T(8,128)S(1)}, u32[]{:S(2)}, u32[]{:S(2)}) collective-permute-start(f32[16,128]{1,0:T(8,128)S(1)} %add.31), channel_id=1, source_target_pairs={{0,12},{4,8},{8,4},{12,0},{16,28},{20,24},{24,20},{28,16},{32,44},... | collective-permute-start | bytes 24584 | tf_op jit(solution)/shard_map/ppermute | solution.py:564
